TPU v7x, 256 devices: a whole 4x4x8 slice. The times are simulated.
256 devices in a mesh: ax: 4 (over z_lo), rad: 8 (over y, core), az: 8 (over x, z_hi).
Axes of the slice: x: 4, y: 4, z: 8 (z_hi: 2, z_lo: 4; z = z_hi * 4 + z_lo), core: 2. Of those that a mesh axis runs over, the one named last changes fastest.
Arguments:
- positions: float32 [3, 4, 8, 131072], P(None, 'ax', 'rad', 'az'), may hold values from 0 to 0.1
- velocity: float32 [3, 4, 8, 131072], P(None, 'ax', 'rad', 'az'), may hold values from -6 to 6
- diameter: float32 [4, 8, 131072], P('ax', 'rad', 'az'), may hold values from 0.02 to 0.1
- cell_index: int32 [4, 8, 131072], P('ax', 'rad', 'az'), may hold values from 0 to 32767
- pair_list: int32 [2, 4, 8, 262144], P(None, 'ax', 'rad', 'az'), may hold values from 0 to 34815, as said below
- live_pairs: int32 [4, 8, 8], P('ax', 'rad', 'az'), may hold values from 8192 to 32768, as said below
- gas_velocity: float32 [3, 32, 128, 2048], P(None, 'ax', 'rad', 'az'), may hold values from -6 to 6
Outputs:
- disturbance: float32 [3, 4, 8, 131072], P(None, 'ax', 'rad', 'az')
- drag_source: float32 [3, 32, 128, 2048], P(None, 'ax', 'rad', 'az')
Inputs may be any that keep to these rules, and one draw needn't show every extreme that they name: pair_list[0] is an own droplet, under 16384; a partner on a neighbouring device lies among that device's last 2048 droplets (q from 14336) or first 2048 droplets (q under 2 * 16384 + 2048); an own partner differs from the first droplet. `live_pairs`: slots at and beyond the count are padding and are ignored.
All inputs are finite; a program needn't handle non-finite values.
Results may differ from a plain program's by a relative error of at most 0.0003.
Values sent between devices are 32-bit elements; how exact they have to be, the bound alone decides.
No kernel may reach another device: no remote copies, remote signals or barrier semaphores. Data moves between devices by JAX's collectives and lax.ppermute only.
A program may use at most 128 MiB of HBM per device.

v0:
```python
import functools
import math

import jax
import jax.numpy as jnp
from jax import lax
from jax.experimental import pallas as pl
from jax.experimental.pallas import tpu as pltpu
from jax.sharding import PartitionSpec as P

piep_coef = 1.0
drag_coef = 20.0

LANES = 128
ROWS = 8
BLOCK = 2048
GAS_WINDOW = 10
BUCKET = 1024
BUCKETS = 20
NEAR_BUCKETS = 4
NEAR_HEADS = 6
OWN_HEADS = 10
DEAD = 1 << 29

NT = (((1,), (1,)), ((), ()))
VMEM = pltpu.VMEM
SMEM = pltpu.SMEM


def params(megabytes=40):
    return pltpu.CompilerParams(vmem_limit_bytes=megabytes << 20)


def lane_gather(table, index):
    numbers = lax.GatherDimensionNumbers(
        offset_dims=(),
        collapsed_slice_dims=(1,),
        start_index_map=(1,),
        operand_batching_dims=(0,),
        start_indices_batching_dims=(0,),
    )
    return lax.gather(
        table,
        index[..., None],
        numbers,
        slice_sizes=(1, 1),
        mode=lax.GatherScatterMode.PROMISE_IN_BOUNDS,
    )


def sort_network(regs, place, levels):
    sub = lax.broadcasted_iota(jnp.int32, (ROWS, LANES), 0)
    lane = lax.broadcasted_iota(jnp.int32, (ROWS, LANES), 1)
    count = len(regs)

    def bit_fill(bit, v):
        if bit >= levels:
            return 0
        kind, k = place[bit]
        if kind == "v":
            return -((v >> k) & 1)
        return -(((sub if kind == "s" else lane) >> k) & 1)

    flip = [0] * count
    for level in range(1, levels + 1):
        fills = {}
        for v in range(count):
            kind, k = place[level] if level < levels else ("v", 99)
            key = (v >> k) & 1 if kind == "v" else 0
            if key not in fills:
                fills[key] = bit_fill(level, v)
            new = fills[key]
            if isinstance(new, int) and isinstance(flip[v], int):
                if new != flip[v]:
                    regs[v] = ~regs[v]
            else:
                regs[v] = regs[v] ^ (new ^ flip[v])
            flip[v] = new
        for bit in reversed(range(level)):
            kind, k = place[bit]
            step = 1 << k
            if kind == "v":
                for v in range(count):
                    if not v & step:
                        a, b = regs[v], regs[v | step]
                        regs[v], regs[v | step] = jnp.minimum(a, b), jnp.maximum(a, b)
            else:
                axis, size, where = (0, ROWS, sub) if kind == "s" else (1, LANES, lane)
                lower = (where & step) == 0
                for v in range(count):
                    x = regs[v]
                    ahead = pltpu.roll(x, size - step, axis)
                    behind = ahead if 2 * step == size else pltpu.roll(x, step, axis)
                    regs[v] = jnp.where(lower, jnp.minimum(x, ahead), jnp.maximum(x, behind))
    return regs


def split_two(x):
    high = x.astype(jnp.bfloat16).astype(jnp.float32)
    return high, x - high


def split_three(x):
    high, rest = split_two(x)
    mid, low = split_two(rest)
    return high, mid, low


def packed_row(ref, row):
    return jnp.broadcast_to(ref[row : row + 1, :], (16, LANES)).astype(jnp.bfloat16)


def one_hot_rows(low, iota):
    one = jnp.ones((16, LANES), jnp.bfloat16)
    zero = jnp.zeros((16, LANES), jnp.bfloat16)
    return jnp.concatenate(
        [jnp.where(low == iota[k : k + 16, :], one, zero) for k in range(0, iota.shape[0], 16)],
        axis=0,
    )


def spread_rows(rel, parts, iota):
    hit = rel == iota[0:16, :]
    zero = jnp.zeros((16, LANES), jnp.bfloat16)
    return jnp.concatenate([jnp.where(hit, p, zero) for part in parts for p in part], axis=0)


def spread_add(rows, hots):
    out = lax.dot_general(
        jnp.concatenate(rows, axis=1) if len(rows) > 1 else rows[0],
        jnp.concatenate(hots, axis=1) if len(hots) > 1 else hots[0],
        NT,
        preferred_element_type=jnp.float32,
    )
    total = out[0:48]
    for s in range(48, out.shape[0], 48):
        total = total + out[s : s + 48]
    return total


def fill_iota(iota):
    rows = lax.broadcasted_iota(jnp.int32, iota.shape, 0)
    iota[...] = rows.astype(jnp.float32).astype(jnp.bfloat16)


def rows_of(block):
    start = block * 16
    return pl.ds(start if isinstance(block, int) else pl.multiple_of(start, 16), 16)


def wide(ref, *at):
    return jnp.broadcast_to(ref[at[:-1] + (slice(at[-1], at[-1] + 1),)], (ROWS, LANES))


def window(table, first, count, row, low, found):
    rel = row - first
    for u in range(count):
        found = jnp.where(rel == u, lane_gather(table[first + u], low), found)
    return found


def running_max(x, count):
    x = jnp.broadcast_to(x, (ROWS, LANES))
    step = 1
    while step < count:
        x = jnp.maximum(x, pltpu.roll(x, LANES - step, 1))
        step *= 2
    return x


def by_partner(axis, first, last):
    even = (lax.axis_index(axis) & 1) == 0
    return jnp.where(even, last, first), jnp.where(even, first, last)


def from_partners(axis, one, other, wrap=False):
    at, count = lax.axis_index(axis), lax.axis_size(axis)
    even = (at & 1) == 0
    before, after = jnp.where(even, other, one), jnp.where(even, one, other)
    if wrap:
        return before, after
    return jnp.where(at > 0, before, 0.0), jnp.where(at < count - 1, after, 0.0)


def fill_gas_rows(gas_ref, gas_rows):
    for r in range(16):
        rows = slice(r * ROWS, (r + 1) * ROWS)
        for c in range(3):
            for half in range(2):
                gas_rows[rows, half * 4 + c, :] = gas_ref[c, rows, half * LANES : (half + 1) * LANES]


def gas_index(block, keys_ref, slot):
    idx = slot[0]
    keys = keys_ref[rows_of(block), :]
    idx[0] = lax.shift_right_logical(keys, 19)
    idx[1] = lax.shift_right_logical(keys, 11) & (LANES - 1)


def gas_gather(block, g, ends, gas_rows, slot):
    idx, found = slot[0], slot[1]
    zero = jnp.zeros((ROWS, LANES), jnp.float32)
    first = ends[0, block * 16 + g]
    found[g] = window(gas_rows, first, GAS_WINDOW, wide(idx, 0, g), wide(idx, 1, g), zero)


def gas_rest(block, ends, gas_rows, slot):
    idx, found = slot[0], slot[1]

    @pl.when(ends[2, block * 16] >= GAS_WINDOW)
    def _():
        def one(g, carry):
            first = ends[0, block * 16 + g]
            row = jnp.broadcast_to(idx[0, pl.ds(g, 1), :], (ROWS, LANES))
            low = jnp.broadcast_to(idx[1, pl.ds(g, 1), :], (ROWS, LANES))

            def trip(t, total):
                base = jnp.minimum(first + GAS_WINDOW * t, LANES)
                return window(gas_rows, base, GAS_WINDOW, row, low, total)

            trips = (ends[1, block * 16 + g] - first) // GAS_WINDOW + 1
            found[g] = lax.fori_loop(1, trips, trip, found[g])
            return carry

        lax.fori_loop(0, 16, one, 0)


def seen_values(block, keys_ref, slot):
    idx, found, val = slot
    keys = keys_ref[rows_of(block), :]
    upper = (keys & (1 << 18)) != 0
    place_in = keys & (BLOCK - 1)
    val[0] = lax.shift_right_logical(place_in, 7).astype(jnp.float32)
    val[1] = (place_in & (LANES - 1)).astype(jnp.float32)
    for c in range(3):
        seen = jnp.where(upper, found[:, 4 + c, :], found[:, c, :])
        for n, part in enumerate(split_three(seen)):
            val[2 + 3 * c + n] = part


def seen_in_order(groups, slot, iota):
    val = slot[2]
    rows, hots = [], []
    for g in groups:
        parts = [[packed_row(val.at[2 + 3 * c + n], g) for c in range(3)] for n in range(3)]
        rows.append(spread_rows(packed_row(val.at[0], g), parts, iota))
        hots.append(one_hot_rows(packed_row(val.at[1], g), iota))
    return spread_add(rows, hots)


def write_states(block, total, pos_ref, vel_ref, diam_ref, out_ref, out_rows):
    rows = rows_of(block)
    for c in range(3):
        out_ref[out_rows, c, :] = pos_ref[c, rows, :]
        out_ref[out_rows, 3 + c, :] = total[16 * c : 16 * c + 16] - vel_ref[c, rows, :]
    out_ref[out_rows, 6, :] = 0.5 * diam_ref[rows, :]
    out_ref[out_rows, 7, :] = jnp.zeros((16, LANES), jnp.float32)


def states_step(gather, scatter, keys_ref, ends, gas_rows, iota, arrays):
    total = jnp.zeros((48, LANES), jnp.float32)
    if gather:
        gas_index(gather[0], keys_ref, gather[1])
    if scatter:
        seen_values(scatter[0], keys_ref, scatter[1])
    for g in range(16):
        if gather:
            gas_gather(gather[0], g, ends, gas_rows, gather[1])
        if scatter and g % 2:
            total = total + seen_in_order((g - 1, g), scatter[1], iota)
    if scatter:
        write_states(scatter[0], total, *arrays, *scatter[2:])
    if gather:
        gas_rest(gather[0], ends, gas_rows, gather[1])


def states_kernel(
    cell_hbm, gas_hbm, pos_hbm, vel_hbm, diam_hbm,
    keys_ref, ends_ref, table_ref, one_ref, other_ref,
    cell_ref, gas_ref, pos_ref, vel_ref, diam_ref,
    gas_rows, iota, ends, idx_a, found_a, val_a, idx_b, found_b, val_b, sems,
):
    sources = (cell_hbm, gas_hbm, pos_hbm, vel_hbm, diam_hbm)
    places = (cell_ref, gas_ref, pos_ref, vel_ref, diam_ref)
    copies = [
        pltpu.make_async_copy(x, y, sems.at[n]) for n, (x, y) in enumerate(zip(sources, places))
    ]
    for copy in copies:
        copy.start()
    copies[0].wait()
    sub = lax.broadcasted_iota(jnp.int32, (ROWS, LANES), 0)
    lane = lax.broadcasted_iota(jnp.int32, (ROWS, LANES), 1)
    cells = cell_ref[...].T
    regs = []
    for v in range(16):
        own = (lane & 15) * LANES + v * ROWS + sub
        regs.append(cells[v * ROWS : (v + 1) * ROWS] * BLOCK + own)
    place = [("v", k) for k in range(4)] + [("s", k) for k in range(3)] + [("l", k) for k in range(4)]
    regs = sort_network(regs, place, 11)
    keys_ref[...] = jnp.concatenate(regs, axis=0).T
    least = functools.reduce(jnp.minimum, regs)
    most = functools.reduce(jnp.maximum, regs)
    least = lax.shift_right_logical(jnp.min(least, axis=0, keepdims=True), 19)
    most = lax.shift_right_logical(jnp.max(most, axis=0, keepdims=True), 19)
    ends_ref[0:1, :] = least
    ends_ref[1:2, :] = most
    ends_ref[2:8, :] = running_max(most - least, 16)[0:6]
    copy = pltpu.make_async_copy(ends_ref, ends, sems.at[5])
    copy.start()
    copies[1].wait()
    fill_gas_rows(gas_ref, gas_rows)
    for other in copies[2:]:
        other.wait()
    copy.wait()
    fill_iota(iota)
    a, b = (idx_a, found_a, val_a), (idx_b, found_b, val_b)
    step = functools.partial(
        states_step, keys_ref=keys_ref, ends=ends, gas_rows=gas_rows, iota=iota,
        arrays=(pos_ref, vel_ref, diam_ref),
    )
    step((0, a), None)

    def two(k, carry):
        block = 2 * k
        step((block + 1, b), (block, a, table_ref, rows_of(block)))
        step((block + 2, a), (block + 1, b, table_ref, rows_of(block + 1)))
        return carry

    lax.fori_loop(0, 3, two, 0)
    step((7, b), (6, a, table_ref, rows_of(6)))
    step(None, (7, b, table_ref, rows_of(7)))
    table_ref[128:144] = jnp.zeros((16, ROWS, LANES), jnp.float32)
    one_ref[...], other_ref[...] = by_partner("az", table_ref[0:16], table_ref[112:128])


def slots(rows, parts, dtype=jnp.float32):
    one = [VMEM((2, 16, LANES), jnp.int32), VMEM((16, ROWS, LANES), dtype), VMEM((parts, rows, LANES), dtype)]
    return one + one


def droplet_states(cells, gas, pos, vel, diam):
    f32, i32 = jnp.float32, jnp.int32
    arrays = (cells, gas, pos, vel, diam)
    return pl.pallas_call(
        states_kernel,
        name="droplet_states",
        out_shape=(
            jax.ShapeDtypeStruct((128, LANES), i32),
            jax.ShapeDtypeStruct((ROWS, LANES), i32),
            jax.ShapeDtypeStruct((144, ROWS, LANES), f32),
            jax.ShapeDtypeStruct((16, ROWS, LANES), f32),
            jax.ShapeDtypeStruct((16, ROWS, LANES), f32),
        ),
        in_specs=[pl.BlockSpec(memory_space=pltpu.HBM)] * 5,
        scratch_shapes=[VMEM(x.shape, x.dtype) for x in arrays]
        + [VMEM((144, ROWS, LANES), f32), VMEM((LANES, LANES), jnp.bfloat16), SMEM((ROWS, LANES), i32)]
        + slots(16, 11)
        + [pltpu.SemaphoreType.DMA((6,))],
        compiler_params=params(60),
    )(*arrays)


def pair_sort_kernel(live_ref, pairs_ref, keys_ref, ends_ref):
    live = live_ref[0, 0]
    sub = lax.broadcasted_iota(jnp.int32, (ROWS, LANES), 0)
    lane = lax.broadcasted_iota(jnp.int32, (ROWS, LANES), 1)
    regs = []
    for v in range(32):
        rows = slice(v * ROWS, (v + 1) * ROWS)
        slot = v * 1024 + sub * LANES + lane
        head = pairs_ref[0, rows, :]
        tail = pairs_ref[1, rows, :] - 7 * BLOCK
        own = tail - BLOCK
        inside = (own >= 0) & (own < 8 * BLOCK)
        tail = jnp.where(inside, jnp.maximum(own, head) + BLOCK, tail)
        head = jnp.where(inside, jnp.minimum(own, head), head)
        bucket = lax.shift_right_logical(tail, 10)
        bucket = jnp.where(inside, bucket + 2, jnp.where(bucket >= 18, bucket - 16, bucket))
        turn = -(bucket & 1) & (8 * BLOCK - 1)
        key = (bucket << 24) | ((head ^ turn) << 10) | (tail & (BUCKET - 1))
        regs.append(jnp.where(slot < live, key, DEAD))
    place = (
        [("v", k) for k in range(4)]
        + [("s", k) for k in range(3)]
        + [("v", 4)]
        + [("l", k) for k in range(7)]
    )
    regs = sort_network(regs, place, 15)
    beyond = jnp.zeros((ROWS, LANES), jnp.float32)
    for key in regs:
        beyond = beyond + jnp.where(key < NEAR_BUCKETS << 24, 1.0, 0.0)
    beyond = jnp.sum(jnp.sum(beyond, axis=0, keepdims=True), axis=1, keepdims=True)
    ends_ref[8:16, :] = jnp.broadcast_to(beyond, (ROWS, LANES)).astype(jnp.int32)
    for half in range(2):
        rows = regs[16 * half : 16 * half + 16]
        keys_ref[half] = jnp.concatenate(rows, axis=0).T
        least_head = least_tail = jnp.full((ROWS, LANES), 1 << 20, jnp.int32)
        most_head = most_tail = jnp.full((ROWS, LANES), -1, jnp.int32)
        for key in rows:
            used = key < DEAD
            bucket = lax.shift_right_logical(key, 24)
            head = lax.shift_right_logical(key, 17) & (LANES - 1)
            head = head ^ (-(bucket & 1) & (LANES - 1))
            least_head = jnp.minimum(least_head, jnp.where(used, head, 1 << 20))
            most_head = jnp.maximum(most_head, jnp.where(used, head, -1))
            least_tail = jnp.minimum(least_tail, jnp.where(used, bucket, 1 << 20))
            most_tail = jnp.maximum(most_tail, jnp.where(used, bucket, -1))
        for n, x in enumerate((least_head, most_head, least_tail, most_tail)):
            reduce = jnp.max if n % 2 else jnp.min
            row = 4 * half + n
            bound = (LANES, LANES, BUCKETS, BUCKETS)[n]
            ends_ref[row : row + 1, :] = jnp.minimum(reduce(x, axis=0, keepdims=True), bound)


def pair_sort(live, pairs):
    return pl.pallas_call(
        pair_sort_kernel,
        name="pair_sort",
        out_shape=(
            jax.ShapeDtypeStruct((2, LANES, LANES), jnp.int32),
            jax.ShapeDtypeStruct((16, LANES), jnp.int32),
        ),
        in_specs=[pl.BlockSpec(memory_space=SMEM), pl.BlockSpec(memory_space=VMEM)],
        compiler_params=params(),
    )(live, pairs)


def take_items(state, groups, ends, part):
    low, high, heads = part
    items = []
    for _ in range(ROWS):
        g, bucket, head = state
        valid = g < groups
        seen = jnp.minimum(g, 2 * LANES - 1)
        at, lane = 4 * (seen & 1), seen >> 1
        items.append((seen, jnp.where(valid, bucket, -1), head, jnp.minimum(bucket, high) - low))
        more_heads = head + heads <= ends[at + 1, lane]
        more_tails = bucket < jnp.minimum(ends[at + 3, lane], high - 1)
        step = jnp.where(more_heads | more_tails, 0, 1)
        g = jnp.minimum(g + step, 2 * LANES)
        seen = jnp.minimum(g, 2 * LANES - 1)
        at, lane = 4 * (seen & 1), seen >> 1
        head = jnp.where(more_heads, head + heads, ends[at, lane])
        same = jnp.where(more_heads, bucket, bucket + 1)
        bucket = jnp.where(step == 1, jnp.maximum(ends[at + 2, lane], low), same)
        state = (g, bucket, head)
    return items, state


def pair_gather(k, item, keys_ref, near_table, far_parts, heads, slot, iota, pick):
    key_rows, rel_rows, near, far, _, hots = slot
    g, bucket, first, part = item
    keys = jnp.broadcast_to(keys_ref[g & 1, pl.ds(g >> 1, 1), :], (ROWS, LANES))
    of_bucket = lax.shift_right_logical(keys, 24)
    turn = -(of_bucket & 1) & (8 * BLOCK - 1)
    head = (lax.shift_right_logical(keys, 10) & (8 * BLOCK - 1)) ^ turn
    rel = lax.shift_right_logical(head, 7) - first
    tail_row = lax.shift_right_logical(keys, 7) & 7
    used = (of_bucket == bucket) & (rel >= 0) & (rel < heads)
    key_rows[k : k + 1, :] = jnp.where(used, keys, DEAD)[0:1]
    rel_rows[k : k + 1, :] = rel[0:1]
    zero = jnp.zeros((ROWS, LANES), jnp.float32)
    low = head & (LANES - 1)
    found = zero
    for u in range(heads):
        found = jnp.where(rel == u, lane_gather(near_table[first + u], low), found)
    near[k] = found
    low = (keys & (LANES - 1)).astype(jnp.float32)
    low = jnp.concatenate([low, low], axis=0).astype(jnp.bfloat16)
    hot = one_hot_rows(low, iota)
    hots[k] = hot
    found = jnp.dot(far_parts[part], hot, preferred_element_type=jnp.float32)
    hit = tail_row == lax.broadcasted_iota(jnp.int32, (ROWS, LANES), 0)
    masked = [jnp.where(hit, found[8 * q : 8 * q + 8], 0.0) for q in range(14)]
    masked = jnp.concatenate(masked, axis=0).astype(jnp.bfloat16)
    far[k] = jnp.dot(pick[...], masked, preferred_element_type=jnp.float32)[0:8]


def pair_values(slot):
    key_rows, rel_rows, near, far, val = slot[0:5]
    keys = key_rows[...]
    used = keys < DEAD
    turn = -(lax.shift_right_logical(keys, 24) & 1) & (LANES - 1)
    val[0] = rel_rows[...].astype(jnp.float32)
    val[1] = ((lax.shift_right_logical(keys, 10) & (LANES - 1)) ^ turn).astype(jnp.float32)
    val[2] = (lax.shift_right_logical(keys, 7) & 7).astype(jnp.float32)
    gap = jnp.zeros((ROWS, LANES), jnp.float32)
    for c in range(3):
        apart = far[:, c, :] - near[:, c, :]
        gap = gap + apart * apart
    far_radius, near_radius = far[:, 6, :], near[:, 6, :]
    far_ratio = far_radius * lax.rsqrt(gap + far_radius * far_radius)
    near_ratio = near_radius * lax.rsqrt(gap + near_radius * near_radius)
    weight_far = jnp.where(used, piep_coef * far_ratio * far_ratio * far_ratio, 0.0)
    weight_near = jnp.where(used, piep_coef * near_ratio * near_ratio * near_ratio, 0.0)
    for c in range(3):
        for n, part in enumerate(split_two(weight_far * far[:, 3 + c, :])):
            val[4 + 3 * n + c] = part
        for n, part in enumerate(split_two(weight_near * near[:, 3 + c, :])):
            val[10 + 3 * n + c] = part


def pair_scatter(k, item, slot, head_sum, tail_sum, iota, iota8):
    val, hots = slot[4:6]
    first, tail_first = item
    parts = [[packed_row(val.at[4 + 3 * n + c], k) for c in range(3)] for n in range(2)]
    rows = spread_rows(packed_row(val.at[0], k), parts, iota)
    out = spread_add([rows], [one_hot_rows(packed_row(val.at[1], k), iota)])
    for c in range(3):
        head_sum[c, pl.ds(first, 16), :] += out[16 * c : 16 * c + 16]

    hit = packed_row(val.at[2], k) == iota8[...]
    zero = jnp.zeros((16, LANES), jnp.bfloat16)
    tiles = []
    for n in range(10, 16, 2):
        both = jnp.concatenate([wide(val, n, k), wide(val, n + 1, k)], axis=0)
        tiles.append(jnp.where(hit, both.astype(jnp.bfloat16), zero))
    out = lax.dot_general(
        jnp.concatenate(tiles, axis=0),
        hots[k],
        NT,
        preferred_element_type=jnp.float32,
    )
    at = pl.ds(pl.multiple_of(tail_first, 8), 8)
    for c in range(3):
        tail_sum[c, at, :] += out[8 * c : 8 * c + 8] + out[24 + 8 * c : 32 + 8 * c]


def run_pairs(
    groups, start, part, ends, keys_ref, near_table, far_table, far_parts, sums, iota, iota8, pick, slots_
):
    fill_iota(iota)
    rows = lax.broadcasted_iota(jnp.int32, iota8.shape, 0) & 7
    iota8[...] = rows.astype(jnp.float32).astype(jnp.bfloat16)
    rows = lax.broadcasted_iota(jnp.int32, pick.shape, 0)
    columns = lax.broadcasted_iota(jnp.int32, pick.shape, 1)
    channel = lax.shift_right_logical(columns, 3)
    channel = jnp.where(channel >= 7, channel - 7, channel)
    pick[...] = jnp.where(rows == channel, 1.0, 0.0).astype(jnp.bfloat16)

    def one_bucket(n, carry):
        block = pl.ds(pl.multiple_of(n * 8, 8), 8)
        pieces = [split_two(far_table[block, c, :]) for c in range(7)]
        pieces = [p[0] for p in pieces] + [p[1] for p in pieces]
        for t in range(7):
            both = jnp.concatenate(pieces[2 * t : 2 * t + 2], axis=0)
            far_parts[n, 16 * t : 16 * t + 16, :] = both.astype(jnp.bfloat16)
        return carry

    lax.fori_loop(0, far_parts.shape[0], one_bucket, 0)
    a, b = slots_[0:6], slots_[6:12]

    def step(state, slot, pending, other):
        items, state = take_items(state, groups, ends, part)
        if other:
            pair_values(other)
        for k in range(ROWS):
            pair_gather(k, items[k], keys_ref, near_table, far_parts, part[2], slot, iota, pick)
            if other:
                pair_scatter(k, pending[k], other, *sums, iota, iota8)
        return tuple((item[2], item[3] * 8) for item in items), state, items[0][1] >= 0

    at, lane = 4 * (start & 1), start >> 1
    state = (start, jnp.maximum(ends[at + 2, lane], part[0]), ends[at, lane])
    carry = step(state, a, None, None)

    def two(carry):
        pending, state, _ = carry
        pending, state, _ = step(state, b, pending, a)
        return step(state, a, pending, b)

    lax.while_loop(lambda carry: carry[2], two, carry)


def near_pairs_kernel(
    ends, keys_ref, table_ref, one_in, other_in,
    heads_ref, one_ref, other_ref,
    shell, far_parts, head_sum, tail_sum, iota, iota8, pick, *slots_,
):
    shell[0:16], shell[16:32] = from_partners("az", one_in[...], other_in[...], True)
    shell[32:40] = jnp.zeros((8, ROWS, LANES), jnp.float32)
    head_sum[...] = jnp.zeros_like(head_sum)
    tail_sum[...] = jnp.zeros_like(tail_sum)
    groups = (ends[8, 0] + LANES - 1) // LANES
    run_pairs(
        groups, jnp.int32(0), (0, NEAR_BUCKETS, NEAR_HEADS), ends, keys_ref, table_ref, shell,
        far_parts, (head_sum, tail_sum), iota, iota8, pick, slots_,
    )
    heads_ref[...] = head_sum[:, 0:128, :]
    one_ref[...], other_ref[...] = by_partner("az", tail_sum[:, 0:16, :], tail_sum[:, 16:32, :])


def own_pairs_kernel(
    live_ref, ends, keys_ref, table_ref, heads_ref,
    corr_ref,
    far_parts, head_sum, tail_sum, iota, iota8, pick, *slots_,
):
    head_sum[:, 0:128, :] = heads_ref[...]
    head_sum[:, 128:144, :] = jnp.zeros((3, 16, LANES), jnp.float32)
    tail_sum[...] = jnp.zeros_like(tail_sum)
    groups = (live_ref[0, 0] + LANES - 1) // LANES
    start = jnp.minimum(ends[8, 0] // LANES, 2 * LANES - 1)
    run_pairs(
        groups, start, (NEAR_BUCKETS, BUCKETS, OWN_HEADS), ends, keys_ref, table_ref, table_ref,
        far_parts, (head_sum, tail_sum), iota, iota8, pick, slots_,
    )
    corr_ref[...] = head_sum[:, 0:128, :] + tail_sum[:, 0:128, :]


def pair_scratch(tail_rows):
    f32, i32 = jnp.float32, jnp.int32
    slot = [
        VMEM((ROWS, LANES), i32),
        VMEM((ROWS, LANES), i32),
        VMEM((ROWS, ROWS, LANES), f32),
        VMEM((ROWS, ROWS, LANES), f32),
        VMEM((16, ROWS, LANES), f32),
        VMEM((ROWS, LANES, LANES), jnp.bfloat16),
    ]
    return [
        VMEM((tail_rows // 8, 112, LANES), jnp.bfloat16),
        VMEM((3, 144, LANES), f32),
        VMEM((3, tail_rows, LANES), f32),
        VMEM((LANES, LANES), jnp.bfloat16),
        VMEM((16, LANES), jnp.bfloat16),
        VMEM((16, 112), jnp.bfloat16),
        *slot,
        *slot,
    ]


def near_pairs(ends, keys, table, one, other):
    f32 = jnp.float32
    smem, vmem = pl.BlockSpec(memory_space=SMEM), pl.BlockSpec(memory_space=VMEM)
    return pl.pallas_call(
        near_pairs_kernel,
        name="near_pairs",
        out_shape=(
            jax.ShapeDtypeStruct((3, 128, LANES), f32),
            jax.ShapeDtypeStruct((3, 16, LANES), f32),
            jax.ShapeDtypeStruct((3, 16, LANES), f32),
        ),
        in_specs=[smem, vmem, vmem, vmem, vmem],
        scratch_shapes=[VMEM((40, ROWS, LANES), f32)] + pair_scratch(40),
        compiler_params=params(),
    )(ends, keys, table, one, other)


def own_pairs(live, ends, keys, table, heads):
    smem, vmem = pl.BlockSpec(memory_space=SMEM), pl.BlockSpec(memory_space=VMEM)
    return pl.pallas_call(
        own_pairs_kernel,
        name="own_pairs",
        out_shape=jax.ShapeDtypeStruct((3, 128, LANES), jnp.float32),
        in_specs=[smem, smem, vmem, vmem, vmem],
        scratch_shapes=pair_scratch(136),
        compiler_params=params(),
    )(live, ends, keys, table, heads)


def force_gather(block, keys_ref, table_ref, total_ref, slot):
    force, got, val = slot
    rows = rows_of(block)
    scale = (-2.0 * drag_coef) * table_ref[rows, 6, :]
    for c in range(3):
        push = scale * (table_ref[rows, 3 + c, :] + total_ref[c, rows, :])
        force[:, c, :] = push[0:8]
        force[:, 4 + c, :] = push[8:16]
    keys = keys_ref[rows, :]
    val[0] = lax.shift_right_logical(keys, 19).astype(jnp.float32)
    val[1] = (lax.shift_right_logical(keys, 11) & (2 * LANES - 1)).astype(jnp.float32)
    inner = lax.shift_right_logical(keys, 7) & 7
    low = keys & (LANES - 1)
    tables = [force[k] for k in range(ROWS)]
    for g in range(16):
        pick = jnp.broadcast_to(inner[g : g + 1, :], (ROWS, LANES))
        at = jnp.broadcast_to(low[g : g + 1, :], (ROWS, LANES))
        found = jnp.zeros((ROWS, LANES), jnp.float32)
        for k in range(ROWS):
            found = jnp.where(pick == k, lane_gather(tables[k], at), found)
        got[g] = found
    upper = (keys & 1024) != 0
    for c in range(3):
        pushed = jnp.where(upper, got[:, 4 + c, :], got[:, c, :])
        for n, part in enumerate(split_two(pushed)):
            val[2 + 2 * c + n] = part


def force_add(g, base, slot, cells, iota):
    val = slot[2]

    def row(n):
        if isinstance(g, int):
            return packed_row(val.at[n], g)
        return jnp.broadcast_to(val[n, pl.ds(g, 1), :], (16, LANES)).astype(jnp.bfloat16)

    rel = row(0) - base.astype(jnp.float32).astype(jnp.bfloat16)
    parts = [[row(2 + 2 * c + n) for c in range(3)] for n in range(2)]
    out = spread_add([spread_rows(rel, parts, iota)], [one_hot_rows(row(1), iota)])
    for c in range(3):
        for half in range(2):
            part = out[16 * c : 16 * c + 16, half * LANES : (half + 1) * LANES]
            cells[2 * c + half, pl.ds(base, 16), :] += part


def force_rest(block, ends, slot, cells, iota):
    @pl.when(ends[2, block * 16] >= 16)
    def _():
        def one(g, carry):
            first, most = ends[0, block * 16 + g], ends[1, block * 16 + g]

            def trip(t, carry):
                force_add(g, jnp.minimum(first + 16 * t, LANES), slot, cells, iota)
                return carry

            lax.fori_loop(1, (most - first) // 16 + 1, trip, 0)
            return carry

        lax.fori_loop(0, 16, one, 0)


def deposit_step(gather, scatter, ends, keys_ref, table_ref, total_ref, cells, iota):
    if gather:
        force_gather(gather[0], keys_ref, table_ref, total_ref, gather[1])
    if scatter:
        for g in range(16):
            force_add(g, ends[0, scatter[0] * 16 + g], scatter[1], cells, iota)
        force_rest(scatter[0], ends, scatter[1], cells, iota)


def deposit_kernel(
    ends, keys_ref, table_ref, corr_ref, one_in, other_in,
    out_ref, total_ref, one_ref, other_ref,
    cells, iota, force_a, got_a, val_a, force_b, got_b, val_b,
):
    fill_iota(iota)
    cells[...] = jnp.zeros_like(cells)
    total_ref[...] = corr_ref[...]
    before, after = from_partners("az", one_in[...], other_in[...], True)
    total_ref[:, 0:16, :] += before
    total_ref[:, 112:128, :] += after
    a, b = (force_a, got_a, val_a), (force_b, got_b, val_b)
    step = functools.partial(
        deposit_step, ends=ends, keys_ref=keys_ref, table_ref=table_ref, total_ref=total_ref,
        cells=cells, iota=iota,
    )
    step((0, a), None)

    def two(k, carry):
        block = 2 * k
        step((block + 1, b), (block, a))
        step((block + 2, a), (block + 1, b))
        return carry

    lax.fori_loop(0, 3, two, 0)
    step((7, b), (6, a))
    step(None, (7, b))
    for c in range(3):
        for half in range(2):
            columns = slice(half * LANES, (half + 1) * LANES)
            out_ref[c, :, columns] = cells[2 * c + half, 0:128, :]
            one, other = by_partner(
                "ax", cells[2 * c + half, 0:32, :], cells[2 * c + half, 96:128, :]
            )
            one_ref[c, :, columns] = one
            other_ref[c, :, columns] = other


def deposits(ends, keys, table, corr, one, other):
    f32 = jnp.float32
    smem, vmem = pl.BlockSpec(memory_space=SMEM), pl.BlockSpec(memory_space=VMEM)
    slot = [VMEM((ROWS, ROWS, LANES), f32), VMEM((16, ROWS, LANES), f32), VMEM((8, 16, LANES), f32)]
    return pl.pallas_call(
        deposit_kernel,
        name="deposits",
        out_shape=(
            jax.ShapeDtypeStruct((3, 128, 2 * LANES), f32),
            jax.ShapeDtypeStruct((3, 128, LANES), f32),
            jax.ShapeDtypeStruct((3, 32, 2 * LANES), f32),
            jax.ShapeDtypeStruct((3, 32, 2 * LANES), f32),
        ),
        in_specs=[smem] + [vmem] * 5,
        scratch_shapes=[VMEM((6, 144, LANES), f32), VMEM((2 * LANES, LANES), jnp.bfloat16)]
        + slot
        + slot,
        compiler_params=params(),
    )(ends, keys, table, corr, one, other)


def axial_kernel(taps, cells_ref, one_in, other_in, out_ref, one_ref, other_ref, first_ref, last_ref):
    for c in range(3):
        before, after = from_partners("ax", one_in[c], other_in[c])
        padded = jnp.concatenate([before, cells_ref[c], after], axis=0)
        total = taps[0] * padded[0:128]
        for k in range(1, 5):
            total = total + taps[k] * padded[16 * k : 16 * k + 128]
        out_ref[c] = total
        for a in range(8):
            first_ref[2 * a : 2 * a + 2, :] = total[16 * a : 16 * a + 2]
            last_ref[2 * a : 2 * a + 2, :] = total[16 * a + 14 : 16 * a + 16]
        one_ref[c], other_ref[c] = by_partner("rad", first_ref[...], last_ref[...])


def radial_kernel(
    taps, cells_ref, one_in, other_in, out_ref, one_ref, other_ref, padded, before_ref, after_ref
):
    lane = lax.broadcasted_iota(jnp.int32, (LANES, LANES), 1)
    edges = jnp.zeros((LANES, LANES), jnp.float32)
    for c in range(3):
        before_ref[...], after_ref[...] = from_partners("rad", one_in[c], other_in[c])
        for a in range(8):
            padded[0:2, :] = before_ref[2 * a : 2 * a + 2, :]
            padded[2:18, :] = cells_ref[c, 16 * a : 16 * a + 16, :]
            padded[18:20, :] = after_ref[2 * a : 2 * a + 2, :]
            total = taps[0] * padded[0:16, :]
            for k in range(1, 5):
                total = total + taps[k] * padded[k : k + 16, :]
            out_ref[c, 16 * a : 16 * a + 16, :] = total
        left, right = out_ref[c, :, 0:LANES], out_ref[c, :, LANES:]
        if c:
            left = pltpu.roll(left, 2 * c, 1)
        right = pltpu.roll(right, 10 + 2 * c, 1)
        edges = jnp.where((lane >> 1) == c, left, edges)
        edges = jnp.where((lane >> 1) == 4 + c, right, edges)
    turned = edges.T
    one_ref[...], other_ref[...] = by_partner("az", turned[0:8], turned[8:16])


def azimuthal_kernel(taps, cells_ref, one_in, other_in, out_ref):
    lane = lax.broadcasted_iota(jnp.int32, (LANES, LANES), 1)
    rest = jnp.zeros((LANES - 16, LANES), jnp.float32)
    before, after = from_partners("az", one_in[...], other_in[...], True)
    edges = jnp.concatenate([after, before, rest], axis=0).T
    for c in range(3):
        ahead = pltpu.roll(edges, LANES - 2 * c, 1) if c else edges
        halo = jnp.where(lane < 64, ahead, pltpu.roll(edges, 118 - 2 * c, 1))
        left, right = cells_ref[c, :, 0:LANES], cells_ref[c, :, LANES:]
        out_left, out_right = taps[2] * left, taps[2] * right
        for k in (1, 2):
            tap = taps[2 + k]
            inner = lane < LANES - k
            x, y, z = (pltpu.roll(v, LANES - k, 1) for v in (left, right, halo))
            out_left = out_left + tap * jnp.where(inner, x, y)
            out_right = out_right + tap * jnp.where(inner, y, z)
            inner = lane >= k
            x, y, z = (pltpu.roll(v, k, 1) for v in (left, right, halo))
            out_left = out_left + tap * jnp.where(inner, x, z)
            out_right = out_right + tap * jnp.where(inner, y, x)
        out_ref[c, :, 0:LANES] = out_left
        out_ref[c, :, LANES:] = out_right


def filtered(deposit, one, other):
    f32 = jnp.float32
    raw = [math.exp(-0.5 * k * k) for k in range(-2, 3)]
    taps = [x / sum(raw) for x in raw]
    whole = jax.ShapeDtypeStruct(deposit.shape, f32)
    radial_face = jax.ShapeDtypeStruct((3, 16, 2 * LANES), f32)
    edge = jax.ShapeDtypeStruct((8, LANES), f32)
    cells, one, other = pl.pallas_call(
        functools.partial(axial_kernel, taps),
        name="axial_filter",
        out_shape=(whole, radial_face, radial_face),
        scratch_shapes=[VMEM((16, 2 * LANES), f32)] * 2,
        compiler_params=params(),
    )(deposit, *swapped(one, other, "ax"))
    cells, one, other = pl.pallas_call(
        functools.partial(radial_kernel, taps),
        name="radial_filter",
        out_shape=(whole, edge, edge),
        scratch_shapes=[VMEM((24, 2 * LANES), f32)] + [VMEM((16, 2 * LANES), f32)] * 2,
        compiler_params=params(),
    )(cells, *swapped(one, other, "rad"))
    return pl.pallas_call(
        functools.partial(azimuthal_kernel, taps),
        name="azimuthal_filter",
        out_shape=whole,
        compiler_params=params(),
    )(cells, *swapped(one, other, "az", True))


def swapped(one, other, axis, wrap=False):
    count = lax.axis_size(axis)

    def partner(i, odd):
        j = i + 1 if i % 2 == odd else i - 1
        return j % count if wrap or 0 <= j < count else i

    return [
        lax.ppermute(x, axis, [(i, partner(i, odd)) for i in range(count)])
        for odd, x in enumerate((one, other))
    ]


def per_device(positions, velocity, diameter, cell_index, pair_list, live_pairs, gas_velocity):
    live = live_pairs.reshape(1, 1)
    cells = cell_index.reshape(128, LANES)
    gas = gas_velocity.reshape(3, 128, 2 * LANES)
    pos = positions.reshape(3, 128, LANES)
    vel = velocity.reshape(3, 128, LANES)
    diam = diameter.reshape(128, LANES)
    cell_keys, cell_ends, table, one, other = droplet_states(cells, gas, pos, vel, diam)
    one, other = swapped(one, other, "az", True)
    pair_keys, pair_ends = pair_sort(live, pair_list.reshape(2, 256, LANES))
    heads, one, other = near_pairs(pair_ends, pair_keys, table, one, other)
    one, other = swapped(one, other, "az", True)
    corr = own_pairs(live, pair_ends, pair_keys, table, heads)
    deposit, correction, one, other = deposits(cell_ends, cell_keys, table, corr, one, other)
    smoothed = filtered(deposit, one, other)
    return (correction.reshape(positions.shape), smoothed.reshape(gas_velocity.shape))


def solution(mesh):
    return jax.shard_map(
        per_device,
        mesh=mesh,
        in_specs=(
            P(None, "ax", "rad", "az"),
            P(None, "ax", "rad", "az"),
            P("ax", "rad", "az"),
            P("ax", "rad", "az"),
            P(None, "ax", "rad", "az"),
            P("ax", "rad", "az"),
            P(None, "ax", "rad", "az"),
        ),
        out_specs=(P(None, "ax", "rad", "az"), P(None, "ax", "rad", "az")),
        check_vma=False,
    )
```

profile of v0, /device:TPU:40, one launch (start us, length us, event | category | flops | bytes accessed | tf_op | source)
XLA Modules:
  0.0 144.7 jit_solution(12372147218839459523)
XLA Ops:
  0.6 0.0 copy-start.2
  0.6 9.1 %droplet_states.1 = (s32[128,128]{1,0:T(8,128)}, s32[8,128]{1,0:T(8,128)}, f32[144,8,128]{2,1,0:T(8,128)}, f32[16,8,128]{2,1,0:T(8,128)}, f32[16,8,128]{2,1,0:T(8,128)}) custom-call(s32[128,128]{1,0:T(8,128)} %bitcast.16, f32[3,128,256]{2,1,0:T(8,128)} %bitcast.12, f32[3,128,128]{2,1,0:T(8,128)} %bitcast.14, f32[3,128,128]{2,1,0:T(8,128)} %bitcast.15, ...), custom_call_target="tpu_custom_call" | custom-call | tf_op jit(solution)/shard_map/droplet_states/pallas_call | solution.py:344
  9.7 6.9 %collective-permute-start = (f32[16,8,128]{2,1,0:T(8,128)}, f32[16,8,128]{2,1,0:T(8,128)S(1)}, u32[]{:S(2)}, u32[]{:S(2)}) collective-permute-start(f32[16,8,128]{2,1,0:T(8,128)} %get-tuple-element.27), channel_id=1, source_target_pairs={{0,1},{1,0},{2,3},{3,2},{4,5},{5,4},{6,7},{7,6},{8,9},{9,8},{10,11... | collective-permute-start | bytes 196616 | tf_op jit(solution)/shard_map/ppermute | solution.py:890
  16.6 3.3 %collective-permute-start.1 = (f32[16,8,128]{2,1,0:T(8,128)}, f32[16,8,128]{2,1,0:T(8,128)S(1)}, u32[]{:S(2)}, u32[]{:S(2)}) collective-permute-start(f32[16,8,128]{2,1,0:T(8,128)} %get-tuple-element.28), channel_id=1, source_target_pairs={{0,7},{1,2},{2,1},{3,4},{4,3},{5,6},{6,5},{7,0},{8,15},{9,10},{10,... | collective-permute-start | bytes 196616 | tf_op jit(solution)/shard_map/ppermute | solution.py:890
  20.6 0.0 copy-done.2
  20.6 3.9 %pair_sort.1 = (s32[2,128,128]{2,1,0:T(8,128)S(1)}, s32[16,128]{1,0:T(8,128)S(1)}) custom-call(s32[1,1]{1,0:T(1,128)} %bitcast.9.live_ref, s32[2,256,128]{2,1,0:T(8,128)S(1)} %bitcast.11), custom_call_target="tpu_custom_call" | custom-call | tf_op jit(solution)/shard_map/pair_sort/pallas_call | solution.py:416
  24.5 0.0 collective-permute-done.one_in
  24.5 3.4 %collective-permute-done.1.other_in = f32[16,8,128]{2,1,0:T(8,128)S(1)} collective-permute-done((f32[16,8,128]{2,1,0:T(8,128)}, f32[16,8,128]{2,1,0:T(8,128)S(1)}, u32[]{:S(2)}, u32[]{:S(2)}) %collective-permute-start.1) | collective-permute-done | bytes 65568 | tf_op jit(solution)/shard_map/ppermute | solution.py:890
  27.9 1.1 copy-done
  29.0 31.5 %near_pairs.1 = (f32[3,128,128]{2,1,0:T(8,128)S(1)}, f32[3,16,128]{2,1,0:T(8,128)S(1)}, f32[3,16,128]{2,1,0:T(8,128)S(1)}) custom-call(s32[16,128]{1,0:T(8,128)S(1)} %get-tuple-element.25.ends, s32[2,128,128]{2,1,0:T(8,128)S(1)} %get-tuple-element.26.keys_ref, f32[144,8,128]{2,1,0:T(8,128)S(1)} %copy-done, f32[16,8,128]{2,1,0:T(8,128)S(1)} %collective-permute-done.one_in, ...), custom_call_target="tpu_custom_call" | custom-call | tf_op jit(solution)/shard_map/near_pairs/pallas_call | solution.py:635
  60.5 0.0 copy-start.1
  60.5 0.1 collective-permute-start.2
  60.6 7.2 %collective-permute-start.3 = (f32[3,16,128]{2,1,0:T(8,128)S(1)}, f32[3,16,128]{2,1,0:T(8,128)S(1)}, u32[]{:S(2)}, u32[]{:S(2)}) collective-permute-start(f32[3,16,128]{2,1,0:T(8,128)S(1)} %get-tuple-element.31), channel_id=1, source_target_pairs={{0,7},{1,2},{2,1},{3,4},{4,3},{5,6},{6,5},{7,0},{8,15},{9,10},{10,... | collective-permute-start | bytes 73736 | tf_op jit(solution)/shard_map/ppermute | solution.py:890
  67.8 45.3 %own_pairs.1.corr_ref = f32[3,128,128]{2,1,0:T(8,128)S(1)} custom-call(s32[1,1]{1,0:T(1,128)} %bitcast.10.live_ref, s32[16,128]{1,0:T(8,128)S(1)} %get-tuple-element.25.ends, s32[2,128,128]{2,1,0:T(8,128)S(1)} %get-tuple-element.26.keys_ref, f32[144,8,128]{2,1,0:T(8,128)S(1)} %copy-done, f32[3,128,128]{2,1,0:T(8,128)S(1)} %get-tuple-element.29.heads_ref), custom_call_target="tpu_custom_call" | custom-call | tf_op jit(solution)/shard_map/own_pairs/pallas_call | solution.py:651
  113.1 0.0 collective-permute-done.2.one_in
  113.1 0.0 collective-permute-done.3.other_in
  113.1 5.7 %deposits.1 = (f32[3,128,256]{2,1,0:T(8,128)S(1)}, f32[3,128,128]{2,1,0:T(8,128)}, f32[3,32,256]{2,1,0:T(8,128)S(1)}, f32[3,32,256]{2,1,0:T(8,128)S(1)}) custom-call(s32[8,128]{1,0:T(8,128)S(1)} %copy-done.4, s32[128,128]{1,0:T(8,128)S(1)} %copy-done.3, f32[144,8,128]{2,1,0:T(8,128)S(1)} %copy-done.1, f32[3,128,128]{2,1,0:T(8,128)S(1)} %own_pairs.1.corr_ref, ...), custom_call_target="tpu_custom_call" | custom-call | tf_op jit(solution)/shard_map/deposits/pallas_call | solution.py:773
  118.8 0.0 collective-permute-start.4
  118.8 3.3 %collective-permute-start.5 = (f32[3,32,256]{2,1,0:T(8,128)S(1)}, f32[3,32,256]{2,1,0:T(8,128)S(1)}, u32[]{:S(2)}, u32[]{:S(2)}) collective-permute-start(f32[3,32,256]{2,1,0:T(8,128)S(1)} %get-tuple-element.35), channel_id=1, source_target_pairs={{0,0},{64,128},{128,64},{192,192},{1,1},{65,129},{129,65},{193,193... | collective-permute-start | bytes 294920 | tf_op jit(solution)/shard_map/ppermute | solution.py:890
  122.1 1.3 collective-permute-done.4.one_in
  123.4 1.9 %collective-permute-done.5.other_in = f32[3,32,256]{2,1,0:T(8,128)S(1)} collective-permute-done((f32[3,32,256]{2,1,0:T(8,128)S(1)}, f32[3,32,256]{2,1,0:T(8,128)S(1)}, u32[]{:S(2)}, u32[]{:S(2)}) %collective-permute-start.5) | collective-permute-done | bytes 98336 | tf_op jit(solution)/shard_map/ppermute | solution.py:890
  125.3 0.2 axial_filter.1
  125.5 0.1 collective-permute-start.6
  125.6 1.9 %collective-permute-start.7 = (f32[3,16,256]{2,1,0:T(8,128)S(1)}, f32[3,16,256]{2,1,0:T(8,128)S(1)}, u32[]{:S(2)}, u32[]{:S(2)}) collective-permute-start(f32[3,16,256]{2,1,0:T(8,128)S(1)} %get-tuple-element.38), channel_id=1, source_target_pairs={{0,0},{8,16},{16,8},{24,32},{32,24},{40,48},{48,40},{56,56},{1,1},... | collective-permute-start | bytes 147464 | tf_op jit(solution)/shard_map/ppermute | solution.py:890
  127.5 0.0 collective-permute-done.6.one_in
  127.5 3.5 %collective-permute-done.7.other_in = f32[3,16,256]{2,1,0:T(8,128)S(1)} collective-permute-done((f32[3,16,256]{2,1,0:T(8,128)S(1)}, f32[3,16,256]{2,1,0:T(8,128)S(1)}, u32[]{:S(2)}, u32[]{:S(2)}) %collective-permute-start.7) | collective-permute-done | bytes 49184 | tf_op jit(solution)/shard_map/ppermute | solution.py:890
  131.0 0.5 radial_filter.1
  131.5 1.9 %collective-permute-start.8 = (f32[8,128]{1,0:T(8,128)S(1)}, f32[8,128]{1,0:T(8,128)S(1)}, u32[]{:S(2)}, u32[]{:S(2)}) collective-permute-start(f32[8,128]{1,0:T(8,128)S(1)} %get-tuple-element.40), channel_id=1, source_target_pairs={{0,1},{1,0},{2,3},{3,2},{4,5},{5,4},{6,7},{7,6},{8,9},{9,8},{10,11... | collective-permute-start | bytes 12296 | tf_op jit(solution)/shard_map/ppermute | solution.py:890
  133.5 3.3 %collective-permute-start.9 = (f32[8,128]{1,0:T(8,128)S(1)}, f32[8,128]{1,0:T(8,128)S(1)}, u32[]{:S(2)}, u32[]{:S(2)}) collective-permute-start(f32[8,128]{1,0:T(8,128)S(1)} %get-tuple-element.41), channel_id=1, source_target_pairs={{0,7},{1,2},{2,1},{3,4},{4,3},{5,6},{6,5},{7,0},{8,15},{9,10},{10,... | collective-permute-start | bytes 12296 | tf_op jit(solution)/shard_map/ppermute | solution.py:890
  136.8 2.3 %collective-permute-done.8.one_in = f32[8,128]{1,0:T(8,128)S(1)} collective-permute-done((f32[8,128]{1,0:T(8,128)S(1)}, f32[8,128]{1,0:T(8,128)S(1)}, u32[]{:S(2)}, u32[]{:S(2)}) %collective-permute-start.8) | collective-permute-done | bytes 4128 | tf_op jit(solution)/shard_map/ppermute | solution.py:890
  139.1 4.0 %collective-permute-done.9.other_in = f32[8,128]{1,0:T(8,128)S(1)} collective-permute-done((f32[8,128]{1,0:T(8,128)S(1)}, f32[8,128]{1,0:T(8,128)S(1)}, u32[]{:S(2)}, u32[]{:S(2)}) %collective-permute-start.9) | collective-permute-done | bytes 4128 | tf_op jit(solution)/shard_map/ppermute | solution.py:890
  143.1 1.6 %azimuthal_filter.1 = f32[3,128,256]{2,1,0:T(8,128)} custom-call(f32[3,128,256]{2,1,0:T(8,128)S(1)} %get-tuple-element.39.cells_ref, f32[8,128]{1,0:T(8,128)S(1)} %collective-permute-done.8.one_in, f32[8,128]{1,0:T(8,128)S(1)} %collective-permute-done.9.other_in), custom_call_target="tpu_custom_call" | custom-call | tf_op jit(solution)/shard_map/azimuthal_filter/pallas_call | solution.py:874
  (6 shorter events, 0.0 us)
Async XLA Ops:
  0.6 20.0 %copy-start.2 = (s32[2,1,1,32768]{3,2,1,0:T(1,128)S(1)}, s32[2,1,1,32768]{3,2,1,0:T(1,128)}, u32[]{:S(2)}) copy-start(s32[2,1,1,32768]{3,2,1,0:T(1,128)} %param.11) | copy-start | bytes 786436
  9.7 14.8 %collective-permute-start = (f32[16,8,128]{2,1,0:T(8,128)}, f32[16,8,128]{2,1,0:T(8,128)S(1)}, u32[]{:S(2)}, u32[]{:S(2)}) collective-permute-start(f32[16,8,128]{2,1,0:T(8,128)} %get-tuple-element.27), channel_id=1, source_target_pairs={{0,1},{1,0},{2,3},{3,2},{4,5},{5,4},{6,7},{7,6},{8,9},{9,8},{10,11... | collective-permute-start | bytes 196616 | tf_op jit(solution)/shard_map/ppermute | solution.py:890
  16.6 11.3 %collective-permute-start.1 = (f32[16,8,128]{2,1,0:T(8,128)}, f32[16,8,128]{2,1,0:T(8,128)S(1)}, u32[]{:S(2)}, u32[]{:S(2)}) collective-permute-start(f32[16,8,128]{2,1,0:T(8,128)} %get-tuple-element.28), channel_id=1, source_target_pairs={{0,7},{1,2},{2,1},{3,4},{4,3},{5,6},{6,5},{7,0},{8,15},{9,10},{10,... | collective-permute-start | bytes 196616 | tf_op jit(solution)/shard_map/ppermute | solution.py:890
  27.9 1.1 copy-start
  60.5 52.6 %copy-start.1 = (f32[144,8,128]{2,1,0:T(8,128)S(1)}, f32[144,8,128]{2,1,0:T(8,128)}, u32[]{:S(2)}) copy-start(f32[144,8,128]{2,1,0:T(8,128)} %get-tuple-element.24.table_ref) | copy-start | bytes 1769476
  60.5 52.6 %collective-permute-start.2 = (f32[3,16,128]{2,1,0:T(8,128)S(1)}, f32[3,16,128]{2,1,0:T(8,128)S(1)}, u32[]{:S(2)}, u32[]{:S(2)}) collective-permute-start(f32[3,16,128]{2,1,0:T(8,128)S(1)} %get-tuple-element.30), channel_id=1, source_target_pairs={{0,1},{1,0},{2,3},{3,2},{4,5},{5,4},{6,7},{7,6},{8,9},{9,8},{10,11... | collective-permute-start | bytes 73736 | tf_op jit(solution)/shard_map/ppermute | solution.py:890
  60.6 52.5 %collective-permute-start.3 = (f32[3,16,128]{2,1,0:T(8,128)S(1)}, f32[3,16,128]{2,1,0:T(8,128)S(1)}, u32[]{:S(2)}, u32[]{:S(2)}) collective-permute-start(f32[3,16,128]{2,1,0:T(8,128)S(1)} %get-tuple-element.31), channel_id=1, source_target_pairs={{0,7},{1,2},{2,1},{3,4},{4,3},{5,6},{6,5},{7,0},{8,15},{9,10},{10,... | collective-permute-start | bytes 73736 | tf_op jit(solution)/shard_map/ppermute | solution.py:890
  67.8 45.3 %copy-start.3 = (s32[128,128]{1,0:T(8,128)S(1)}, s32[128,128]{1,0:T(8,128)}, u32[]{:S(2)}) copy-start(s32[128,128]{1,0:T(8,128)} %get-tuple-element.23.keys_ref) | copy-start | bytes 196612
  67.8 45.3 %copy-start.4 = (s32[8,128]{1,0:T(8,128)S(1)}, s32[8,128]{1,0:T(8,128)}, u32[]{:S(2)}) copy-start(s32[8,128]{1,0:T(8,128)} %get-tuple-element.22.ends) | copy-start | bytes 12292
  118.8 4.6 %collective-permute-start.4 = (f32[3,32,256]{2,1,0:T(8,128)S(1)}, f32[3,32,256]{2,1,0:T(8,128)S(1)}, u32[]{:S(2)}, u32[]{:S(2)}) collective-permute-start(f32[3,32,256]{2,1,0:T(8,128)S(1)} %get-tuple-element.34), channel_id=1, source_target_pairs={{0,64},{64,0},{128,192},{192,128},{1,65},{65,1},{129,193},{193,129... | collective-permute-start | bytes 294920 | tf_op jit(solution)/shard_map/ppermute | solution.py:890
  118.8 6.5 %collective-permute-start.5 = (f32[3,32,256]{2,1,0:T(8,128)S(1)}, f32[3,32,256]{2,1,0:T(8,128)S(1)}, u32[]{:S(2)}, u32[]{:S(2)}) collective-permute-start(f32[3,32,256]{2,1,0:T(8,128)S(1)} %get-tuple-element.35), channel_id=1, source_target_pairs={{0,0},{64,128},{128,64},{192,192},{1,1},{65,129},{129,65},{193,193... | collective-permute-start | bytes 294920 | tf_op jit(solution)/shard_map/ppermute | solution.py:890
  125.5 2.0 %collective-permute-start.6 = (f32[3,16,256]{2,1,0:T(8,128)S(1)}, f32[3,16,256]{2,1,0:T(8,128)S(1)}, u32[]{:S(2)}, u32[]{:S(2)}) collective-permute-start(f32[3,16,256]{2,1,0:T(8,128)S(1)} %get-tuple-element.37), channel_id=1, source_target_pairs={{0,8},{8,0},{16,24},{24,16},{32,40},{40,32},{48,56},{56,48},{1,9},... | collective-permute-start | bytes 147464 | tf_op jit(solution)/shard_map/ppermute | solution.py:890
  125.6 5.4 %collective-permute-start.7 = (f32[3,16,256]{2,1,0:T(8,128)S(1)}, f32[3,16,256]{2,1,0:T(8,128)S(1)}, u32[]{:S(2)}, u32[]{:S(2)}) collective-permute-start(f32[3,16,256]{2,1,0:T(8,128)S(1)} %get-tuple-element.38), channel_id=1, source_target_pairs={{0,0},{8,16},{16,8},{24,32},{32,24},{40,48},{48,40},{56,56},{1,1},... | collective-permute-start | bytes 147464 | tf_op jit(solution)/shard_map/ppermute | solution.py:890
  131.5 7.6 %collective-permute-start.8 = (f32[8,128]{1,0:T(8,128)S(1)}, f32[8,128]{1,0:T(8,128)S(1)}, u32[]{:S(2)}, u32[]{:S(2)}) collective-permute-start(f32[8,128]{1,0:T(8,128)S(1)} %get-tuple-element.40), channel_id=1, source_target_pairs={{0,1},{1,0},{2,3},{3,2},{4,5},{5,4},{6,7},{7,6},{8,9},{9,8},{10,11... | collective-permute-start | bytes 12296 | tf_op jit(solution)/shard_map/ppermute | solution.py:890
  133.5 9.6 %collective-permute-start.9 = (f32[8,128]{1,0:T(8,128)S(1)}, f32[8,128]{1,0:T(8,128)S(1)}, u32[]{:S(2)}, u32[]{:S(2)}) collective-permute-start(f32[8,128]{1,0:T(8,128)S(1)} %get-tuple-element.41), channel_id=1, source_target_pairs={{0,7},{1,2},{2,1},{3,4},{4,3},{5,6},{6,5},{7,0},{8,15},{9,10},{10,... | collective-permute-start | bytes 12296 | tf_op jit(solution)/shard_map/ppermute | solution.py:890
where the time goes:
time: 146 us; the launch traced here: 145 us
  Pallas kernels  97.8 us (67%)
  starting transfers between devices  28 us (19%)
  waiting for transfers between devices  16.4 us (11%)
    pallas_call x1, Pallas kernels, own_pairs(): pl.pallas_call(own_pairs_kernel, name='own_pairs', out_shape=jax.ShapeDty...  45.3 us
    pallas_call x1, Pallas kernels, near_pairs(): pl.pallas_call(near_pairs_kernel, name='near_pairs', out_shape=(jax.Shape...  31.5 us
    ppermute x10, starting transfers between devices, swapped(): lax.ppermute(x, axis, [(i, partner(i, odd)) for i in range(count)])  28 us
    ppermute x10, waiting for transfers between devices, swapped(): lax.ppermute(x, axis, [(i, partner(i, odd)) for i in range(count)])  16.4 us
    pallas_call x1, Pallas kernels, droplet_states(): pl.pallas_call(states_kernel, name='droplet_states', out_shape=(jax.Shape...  9.09 us
    pallas_call x1, Pallas kernels, deposits(): pl.pallas_call(deposit_kernel, name='deposits', out_shape=(jax.ShapeDtype...  5.68 us
    pallas_call x1, Pallas kernels, pair_sort(): pl.pallas_call(pair_sort_kernel, name='pair_sort', out_shape=(jax.ShapeDt...  3.85 us
  transfers between devices with their start and end apart: 10, of which 6 were waited for; matrix products, arithmetic and copies ran while one was open for 0% of the time, Pallas kernels for 34%

commit v1 on v0

--- a/solution.py
+++ b/solution.py
@@ -18,8 +18,8 @@
 BUCKET = 1024
 BUCKETS = 20
 NEAR_BUCKETS = 4
-NEAR_HEADS = 6
-OWN_HEADS = 10
+NEAR_HEADS = 8
+OWN_HEADS = 12
 DEAD = 1 << 29
 
 NT = (((1,), (1,)), ((), ()))
@@ -182,6 +182,58 @@
     return jnp.where(at > 0, before, 0.0), jnp.where(at < count - 1, after, 0.0)
 
 
+PLACE_STEP = 0.1 / 65535.0
+RADIUS_LEAST = 0.01
+RADIUS_STEP = 0.04 / 65535.0
+SLIP_HALF = 1 << 20
+
+
+def largest_slip(table, rows):
+    most = jnp.zeros((ROWS, LANES), jnp.float32)
+    for n in range(0, rows, ROWS):
+        for c in range(3):
+            most = jnp.maximum(most, jnp.abs(table[n : n + ROWS, 3 + c, :]))
+    most = jnp.max(jnp.max(most, axis=0, keepdims=True), axis=1, keepdims=True)
+    return jnp.broadcast_to(jnp.maximum(most, 1e-30), (ROWS, LANES))
+
+
+def code_rows(table, n, largest, words):
+    rows = pl.ds(n * ROWS, ROWS)
+
+    def whole(c, least, step):
+        x = ((table[rows, c, :] - least) * (1.0 / step) + 0.5).astype(jnp.int32)
+        return jnp.clip(x, 0, 65535)
+
+    x, y, z = (whole(c, 0.0, PLACE_STEP) for c in range(3))
+    radius = whole(6, RADIUS_LEAST, RADIUS_STEP)
+    scale = (SLIP_HALF - 1.0) / largest
+    u, v, w = (
+        (table[rows, 3 + c, :] * scale + (SLIP_HALF + 0.5)).astype(jnp.int32) for c in range(3)
+    )
+    coded = (
+        x | (y << 16),
+        z | (radius << 16),
+        u | ((w & 2047) << 21),
+        v | (lax.shift_right_logical(w, 11) << 21),
+    )
+    for k, word in enumerate(coded):
+        words[pl.ds(n * 32 + k, ROWS, stride=4), :] = word
+
+
+def decoded(words, largest):
+    low = [x & 65535 for x in words[0:2]]
+    high = [lax.shift_right_logical(x, 16) for x in words[0:2]]
+    place = (low[0], high[0], low[1])
+    radius = high[1].astype(jnp.float32) * RADIUS_STEP + RADIUS_LEAST
+    mask = 2 * SLIP_HALF - 1
+    third = lax.shift_right_logical(words[2], 21) | (lax.shift_right_logical(words[3], 21) << 11)
+    scale = largest * (1.0 / (SLIP_HALF - 1.0))
+    slip = [
+        (x - SLIP_HALF).astype(jnp.float32) * scale for x in (words[2] & mask, words[3] & mask, third)
+    ]
+    return place, radius, slip
+
+
 def fill_gas_rows(gas_ref, gas_rows):
     for r in range(16):
         rows = slice(r * ROWS, (r + 1) * ROWS)
@@ -276,7 +328,7 @@
 
 def states_kernel(
     cell_hbm, gas_hbm, pos_hbm, vel_hbm, diam_hbm,
-    keys_ref, ends_ref, table_ref, one_ref, other_ref,
+    keys_ref, ends_ref, table_ref, words_ref, largest_ref, one_ref, other_ref,
     cell_ref, gas_ref, pos_ref, vel_ref, diam_ref,
     gas_rows, iota, ends, idx_a, found_a, val_a, idx_b, found_b, val_b, sems,
 ):
@@ -329,7 +381,11 @@
     lax.fori_loop(0, 3, two, 0)
     step((7, b), (6, a, table_ref, rows_of(6)))
     step(None, (7, b, table_ref, rows_of(7)))
-    table_ref[128:144] = jnp.zeros((16, ROWS, LANES), jnp.float32)
+    largest = largest_slip(table_ref, 128)
+    largest_ref[...] = largest
+    for n in range(16):
+        code_rows(table_ref, n, largest, words_ref)
+    words_ref[512:576, :] = jnp.zeros((64, LANES), jnp.int32)
     one_ref[...], other_ref[...] = by_partner("az", table_ref[0:16], table_ref[112:128])
 
 
@@ -347,7 +403,9 @@
         out_shape=(
             jax.ShapeDtypeStruct((128, LANES), i32),
             jax.ShapeDtypeStruct((ROWS, LANES), i32),
-            jax.ShapeDtypeStruct((144, ROWS, LANES), f32),
+            jax.ShapeDtypeStruct((128, ROWS, LANES), f32),
+            jax.ShapeDtypeStruct((576, LANES), i32),
+            jax.ShapeDtypeStruct((ROWS, LANES), f32),
             jax.ShapeDtypeStruct((16, ROWS, LANES), f32),
             jax.ShapeDtypeStruct((16, ROWS, LANES), f32),
         ),
@@ -440,68 +498,69 @@
         g = jnp.minimum(g + step, 2 * LANES)
         seen = jnp.minimum(g, 2 * LANES - 1)
         at, lane = 4 * (seen & 1), seen >> 1
-        head = jnp.where(more_heads, head + heads, ends[at, lane])
+        head = jnp.where(more_heads, head + heads, ends[at, lane] & -2)
         same = jnp.where(more_heads, bucket, bucket + 1)
         bucket = jnp.where(step == 1, jnp.maximum(ends[at + 2, lane], low), same)
         state = (g, bucket, head)
     return items, state
 
 
-def pair_gather(k, item, keys_ref, near_table, far_parts, heads, slot, iota, pick):
-    key_rows, rel_rows, near, far, _, hots = slot
+def word_window(words, first, count, pair, low):
+    found = jnp.zeros((ROWS, LANES), jnp.int32)
+    for u in range(count):
+        rows = words[pl.ds(pl.multiple_of((first + u) * ROWS, ROWS), ROWS), :]
+        found = jnp.where(pair == u, lane_gather(rows, low), found)
+    return found
+
+
+def pair_gather(k, item, keys_ref, near_words, far_words, heads, slot):
+    key_rows, rel_rows, near, far = slot
     g, bucket, first, part = item
     keys = jnp.broadcast_to(keys_ref[g & 1, pl.ds(g >> 1, 1), :], (ROWS, LANES))
     of_bucket = lax.shift_right_logical(keys, 24)
     turn = -(of_bucket & 1) & (8 * BLOCK - 1)
     head = (lax.shift_right_logical(keys, 10) & (8 * BLOCK - 1)) ^ turn
     rel = lax.shift_right_logical(head, 7) - first
-    tail_row = lax.shift_right_logical(keys, 7) & 7
     used = (of_bucket == bucket) & (rel >= 0) & (rel < heads)
     key_rows[k : k + 1, :] = jnp.where(used, keys, DEAD)[0:1]
     rel_rows[k : k + 1, :] = rel[0:1]
-    zero = jnp.zeros((ROWS, LANES), jnp.float32)
-    low = head & (LANES - 1)
-    found = zero
-    for u in range(heads):
-        found = jnp.where(rel == u, lane_gather(near_table[first + u], low), found)
-    near[k] = found
-    low = (keys & (LANES - 1)).astype(jnp.float32)
-    low = jnp.concatenate([low, low], axis=0).astype(jnp.bfloat16)
-    hot = one_hot_rows(low, iota)
-    hots[k] = hot
-    found = jnp.dot(far_parts[part], hot, preferred_element_type=jnp.float32)
-    hit = tail_row == lax.broadcasted_iota(jnp.int32, (ROWS, LANES), 0)
-    masked = [jnp.where(hit, found[8 * q : 8 * q + 8], 0.0) for q in range(14)]
-    masked = jnp.concatenate(masked, axis=0).astype(jnp.bfloat16)
-    far[k] = jnp.dot(pick[...], masked, preferred_element_type=jnp.float32)[0:8]
-
-
-def pair_values(slot):
-    key_rows, rel_rows, near, far, val = slot[0:5]
-    keys = key_rows[...]
+    near[k] = word_window(near_words, first >> 1, heads // 2, rel >> 1, head & (LANES - 1))
+    pair = lax.shift_right_logical(keys, 8) & 3
+    far[k] = word_window(far_words, part * 4, 4, pair, keys & (LANES - 1))
+
+
+def pair_values(slot, val, near_largest, far_largest):
+    key_rows, rel_rows, near, far = slot
+    keys, rel = key_rows[...], rel_rows[...]
     used = keys < DEAD
     turn = -(lax.shift_right_logical(keys, 24) & 1) & (LANES - 1)
-    val[0] = rel_rows[...].astype(jnp.float32)
+    val[0] = rel.astype(jnp.float32)
     val[1] = ((lax.shift_right_logical(keys, 10) & (LANES - 1)) ^ turn).astype(jnp.float32)
     val[2] = (lax.shift_right_logical(keys, 7) & 7).astype(jnp.float32)
+    val[3] = (keys & (LANES - 1)).astype(jnp.float32)
+
+    def words(ref, odd):
+        return [jnp.where(odd, ref[:, 4 + w, :], ref[:, w, :]) for w in range(4)]
+
+    near_place, near_radius, near_slip = decoded(words(near, (rel & 1) == 1), near_largest)
+    far_place, far_radius, far_slip = decoded(words(far, (keys & LANES) != 0), far_largest)
     gap = jnp.zeros((ROWS, LANES), jnp.float32)
-    for c in range(3):
-        apart = far[:, c, :] - near[:, c, :]
+    for x, y in zip(far_place, near_place):
+        apart = (x - y).astype(jnp.float32)
         gap = gap + apart * apart
-    far_radius, near_radius = far[:, 6, :], near[:, 6, :]
+    gap = gap * (PLACE_STEP * PLACE_STEP)
     far_ratio = far_radius * lax.rsqrt(gap + far_radius * far_radius)
     near_ratio = near_radius * lax.rsqrt(gap + near_radius * near_radius)
     weight_far = jnp.where(used, piep_coef * far_ratio * far_ratio * far_ratio, 0.0)
     weight_near = jnp.where(used, piep_coef * near_ratio * near_ratio * near_ratio, 0.0)
     for c in range(3):
-        for n, part in enumerate(split_two(weight_far * far[:, 3 + c, :])):
+        for n, part in enumerate(split_two(weight_far * far_slip[c])):
             val[4 + 3 * n + c] = part
-        for n, part in enumerate(split_two(weight_near * near[:, 3 + c, :])):
+        for n, part in enumerate(split_two(weight_near * near_slip[c])):
             val[10 + 3 * n + c] = part
 
 
-def pair_scatter(k, item, slot, head_sum, tail_sum, iota, iota8):
-    val, hots = slot[4:6]
+def pair_scatter(k, item, val, head_sum, tail_sum, iota, iota8):
     first, tail_first = item
     parts = [[packed_row(val.at[4 + 3 * n + c], k) for c in range(3)] for n in range(2)]
     rows = spread_rows(packed_row(val.at[0], k), parts, iota)
@@ -517,7 +576,7 @@
         tiles.append(jnp.where(hit, both.astype(jnp.bfloat16), zero))
     out = lax.dot_general(
         jnp.concatenate(tiles, axis=0),
-        hots[k],
+        one_hot_rows(packed_row(val.at[3], k), iota),
         NT,
         preferred_element_type=jnp.float32,
     )
@@ -526,83 +585,71 @@
         tail_sum[c, at, :] += out[8 * c : 8 * c + 8] + out[24 + 8 * c : 32 + 8 * c]
 
 
-def run_pairs(
-    groups, start, part, ends, keys_ref, near_table, far_table, far_parts, sums, iota, iota8, pick, slots_
-):
+def run_pairs(groups, start, part, ends, keys_ref, near, far, sums, iota, iota8, scratch):
     fill_iota(iota)
     rows = lax.broadcasted_iota(jnp.int32, iota8.shape, 0) & 7
     iota8[...] = rows.astype(jnp.float32).astype(jnp.bfloat16)
-    rows = lax.broadcasted_iota(jnp.int32, pick.shape, 0)
-    columns = lax.broadcasted_iota(jnp.int32, pick.shape, 1)
-    channel = lax.shift_right_logical(columns, 3)
-    channel = jnp.where(channel >= 7, channel - 7, channel)
-    pick[...] = jnp.where(rows == channel, 1.0, 0.0).astype(jnp.bfloat16)
-
-    def one_bucket(n, carry):
-        block = pl.ds(pl.multiple_of(n * 8, 8), 8)
-        pieces = [split_two(far_table[block, c, :]) for c in range(7)]
-        pieces = [p[0] for p in pieces] + [p[1] for p in pieces]
-        for t in range(7):
-            both = jnp.concatenate(pieces[2 * t : 2 * t + 2], axis=0)
-            far_parts[n, 16 * t : 16 * t + 16, :] = both.astype(jnp.bfloat16)
+    val, a, b = scratch[0], scratch[1:5], scratch[5:9]
+
+    def step(state, slot, pending):
+        items, state = take_items(state, groups, ends, part)
+        if pending:
+            pair_values(a, val, near[1], far[1])
+        for k in range(ROWS):
+            pair_gather(k, items[k], keys_ref, near[0], far[0], part[2], slot)
+            if pending:
+                pair_scatter(k, pending[k], val, *sums, iota, iota8)
+        return tuple((item[2], item[3] * 8) for item in items), state, items[0][1] >= 0
+
+    at, lane = 4 * (start & 1), start >> 1
+    state = (start, jnp.maximum(ends[at + 2, lane], part[0]), ends[at, lane] & -2)
+
+    def one(carry):
+        pending, state, _ = carry
+        carry = step(state, b, pending)
+        for x, y in zip(a, b):
+            x[...] = y[...]
         return carry
 
-    lax.fori_loop(0, far_parts.shape[0], one_bucket, 0)
-    a, b = slots_[0:6], slots_[6:12]
-
-    def step(state, slot, pending, other):
-        items, state = take_items(state, groups, ends, part)
-        if other:
-            pair_values(other)
-        for k in range(ROWS):
-            pair_gather(k, items[k], keys_ref, near_table, far_parts, part[2], slot, iota, pick)
-            if other:
-                pair_scatter(k, pending[k], other, *sums, iota, iota8)
-        return tuple((item[2], item[3] * 8) for item in items), state, items[0][1] >= 0
-
-    at, lane = 4 * (start & 1), start >> 1
-    state = (start, jnp.maximum(ends[at + 2, lane], part[0]), ends[at, lane])
-    carry = step(state, a, None, None)
-
-    def two(carry):
-        pending, state, _ = carry
-        pending, state, _ = step(state, b, pending, a)
-        return step(state, a, pending, b)
-
-    lax.while_loop(lambda carry: carry[2], two, carry)
+    lax.while_loop(lambda carry: carry[2], one, step(state, a, None))
 
 
 def near_pairs_kernel(
-    ends, keys_ref, table_ref, one_in, other_in,
+    ends, keys_ref, words_ref, largest_ref, one_in, other_in,
     heads_ref, one_ref, other_ref,
-    shell, far_parts, head_sum, tail_sum, iota, iota8, pick, *slots_,
+    shell, shell_words, head_sum, tail_sum, iota, iota8, *scratch,
 ):
     shell[0:16], shell[16:32] = from_partners("az", one_in[...], other_in[...], True)
-    shell[32:40] = jnp.zeros((8, ROWS, LANES), jnp.float32)
+    shell_largest = largest_slip(shell, 32)
+    for n in range(4):
+        code_rows(shell, n, shell_largest, shell_words)
+    shell_words[128:160, :] = jnp.zeros((32, LANES), jnp.int32)
     head_sum[...] = jnp.zeros_like(head_sum)
     tail_sum[...] = jnp.zeros_like(tail_sum)
     groups = (ends[8, 0] + LANES - 1) // LANES
     run_pairs(
-        groups, jnp.int32(0), (0, NEAR_BUCKETS, NEAR_HEADS), ends, keys_ref, table_ref, shell,
-        far_parts, (head_sum, tail_sum), iota, iota8, pick, slots_,
+        groups, jnp.int32(0), (0, NEAR_BUCKETS, NEAR_HEADS), ends, keys_ref,
+        (words_ref, largest_ref[...]), (shell_words, shell_largest),
+        (head_sum, tail_sum), iota, iota8, scratch,
     )
     heads_ref[...] = head_sum[:, 0:128, :]
     one_ref[...], other_ref[...] = by_partner("az", tail_sum[:, 0:16, :], tail_sum[:, 16:32, :])
 
 
 def own_pairs_kernel(
-    live_ref, ends, keys_ref, table_ref, heads_ref,
+    live_ref, ends, keys_ref, words_ref, largest_ref, heads_ref,
     corr_ref,
-    far_parts, head_sum, tail_sum, iota, iota8, pick, *slots_,
+    head_sum, tail_sum, iota, iota8, *scratch,
 ):
     head_sum[:, 0:128, :] = heads_ref[...]
     head_sum[:, 128:144, :] = jnp.zeros((3, 16, LANES), jnp.float32)
     tail_sum[...] = jnp.zeros_like(tail_sum)
     groups = (live_ref[0, 0] + LANES - 1) // LANES
     start = jnp.minimum(ends[8, 0] // LANES, 2 * LANES - 1)
+    coded = (words_ref, largest_ref[...])
     run_pairs(
-        groups, start, (NEAR_BUCKETS, BUCKETS, OWN_HEADS), ends, keys_ref, table_ref, table_ref,
-        far_parts, (head_sum, tail_sum), iota, iota8, pick, slots_,
+        groups, start, (NEAR_BUCKETS, BUCKETS, OWN_HEADS), ends, keys_ref, coded, coded,
+        (head_sum, tail_sum), iota, iota8, scratch,
     )
     corr_ref[...] = head_sum[:, 0:128, :] + tail_sum[:, 0:128, :]
 
@@ -612,24 +659,21 @@
     slot = [
         VMEM((ROWS, LANES), i32),
         VMEM((ROWS, LANES), i32),
-        VMEM((ROWS, ROWS, LANES), f32),
-        VMEM((ROWS, ROWS, LANES), f32),
-        VMEM((16, ROWS, LANES), f32),
-        VMEM((ROWS, LANES, LANES), jnp.bfloat16),
+        VMEM((ROWS, ROWS, LANES), i32),
+        VMEM((ROWS, ROWS, LANES), i32),
     ]
     return [
-        VMEM((tail_rows // 8, 112, LANES), jnp.bfloat16),
         VMEM((3, 144, LANES), f32),
         VMEM((3, tail_rows, LANES), f32),
         VMEM((LANES, LANES), jnp.bfloat16),
         VMEM((16, LANES), jnp.bfloat16),
-        VMEM((16, 112), jnp.bfloat16),
+        VMEM((16, ROWS, LANES), f32),
         *slot,
         *slot,
     ]
 
 
-def near_pairs(ends, keys, table, one, other):
+def near_pairs(ends, keys, words, largest, one, other):
     f32 = jnp.float32
     smem, vmem = pl.BlockSpec(memory_space=SMEM), pl.BlockSpec(memory_space=VMEM)
     return pl.pallas_call(
@@ -640,22 +684,23 @@
             jax.ShapeDtypeStruct((3, 16, LANES), f32),
             jax.ShapeDtypeStruct((3, 16, LANES), f32),
         ),
-        in_specs=[smem, vmem, vmem, vmem, vmem],
-        scratch_shapes=[VMEM((40, ROWS, LANES), f32)] + pair_scratch(40),
+        in_specs=[smem, vmem, vmem, vmem, vmem, vmem],
+        scratch_shapes=[VMEM((32, ROWS, LANES), f32), VMEM((160, LANES), jnp.int32)]
+        + pair_scratch(40),
         compiler_params=params(),
-    )(ends, keys, table, one, other)
-
-
-def own_pairs(live, ends, keys, table, heads):
+    )(ends, keys, words, largest, one, other)
+
+
+def own_pairs(live, ends, keys, words, largest, heads):
     smem, vmem = pl.BlockSpec(memory_space=SMEM), pl.BlockSpec(memory_space=VMEM)
     return pl.pallas_call(
         own_pairs_kernel,
         name="own_pairs",
         out_shape=jax.ShapeDtypeStruct((3, 128, LANES), jnp.float32),
-        in_specs=[smem, smem, vmem, vmem, vmem],
+        in_specs=[smem, smem, vmem, vmem, vmem, vmem],
         scratch_shapes=pair_scratch(136),
         compiler_params=params(),
-    )(live, ends, keys, table, heads)
+    )(live, ends, keys, words, largest, heads)
 
 
 def force_gather(block, keys_ref, table_ref, total_ref, slot):
@@ -899,12 +944,14 @@
     pos = positions.reshape(3, 128, LANES)
     vel = velocity.reshape(3, 128, LANES)
     diam = diameter.reshape(128, LANES)
-    cell_keys, cell_ends, table, one, other = droplet_states(cells, gas, pos, vel, diam)
+    cell_keys, cell_ends, table, words, largest, one, other = droplet_states(
+        cells, gas, pos, vel, diam
+    )
     one, other = swapped(one, other, "az", True)
     pair_keys, pair_ends = pair_sort(live, pair_list.reshape(2, 256, LANES))
-    heads, one, other = near_pairs(pair_ends, pair_keys, table, one, other)
+    heads, one, other = near_pairs(pair_ends, pair_keys, words, largest, one, other)
     one, other = swapped(one, other, "az", True)
-    corr = own_pairs(live, pair_ends, pair_keys, table, heads)
+    corr = own_pairs(live, pair_ends, pair_keys, words, largest, heads)
     deposit, correction, one, other = deposits(cell_ends, cell_keys, table, corr, one, other)
     smoothed = filtered(deposit, one, other)
     return (correction.reshape(positions.shape), smoothed.reshape(gas_velocity.shape))

time: 146 us -> 90 us (0.62)
  Pallas kernels: 97.8 us -> 40 us
  waiting for transfers between devices: 16.4 us -> 18.2 us
    pallas_call x1, Pallas kernels: 45.3 us -> 9.83 us  [own_pairs(): pl.pallas_call(own_pairs_kernel, name='own_pairs', out_shape=jax.ShapeDty...]
    pallas_call x1, Pallas kernels: 31.5 us -> 7.97 us  [near_pairs(): pl.pallas_call(near_pairs_kernel, name='near_pairs', out_shape=(jax.Shape...]
    ppermute x10, waiting for transfers between devices: 16.4 us -> 18.2 us  [swapped(): lax.ppermute(x, axis, [(i, partner(i, odd)) for i in range(count)])]
  transfers between devices with their start and end apart: 10 -> 10, of which waited for: 6 -> 6; matrix products, arithmetic and copies ran while one was open for 0% -> 0% of each run, Pallas kernels for 34% -> 15%
where the time goes in v1:
time: 90 us; the launch traced here: 88.8 us
  Pallas kernels  40 us (44%)
  starting transfers between devices  27.5 us (31%)
  waiting for transfers between devices  18.2 us (20%)
  local copies, waits for them, and re-layouts  1.62 us (2%)
  between operations  1.44 us (2%)
    ppermute x10, starting transfers between devices, swapped(): lax.ppermute(x, axis, [(i, partner(i, odd)) for i in range(count)])  27.5 us
    ppermute x10, waiting for transfers between devices, swapped(): lax.ppermute(x, axis, [(i, partner(i, odd)) for i in range(count)])  18.2 us
    pallas_call x1, Pallas kernels, droplet_states(): pl.pallas_call(states_kernel, name='droplet_states', out_shape=(jax.Shape...  10.3 us
    pallas_call x1, Pallas kernels, own_pairs(): pl.pallas_call(own_pairs_kernel, name='own_pairs', out_shape=jax.ShapeDty...  9.83 us
    pallas_call x1, Pallas kernels, near_pairs(): pl.pallas_call(near_pairs_kernel, name='near_pairs', out_shape=(jax.Shape...  7.97 us
    pallas_call x1, Pallas kernels, deposits(): pl.pallas_call(deposit_kernel, name='deposits', out_shape=(jax.ShapeDtype...  5.67 us
    pallas_call x1, Pallas kernels, pair_sort(): pl.pallas_call(pair_sort_kernel, name='pair_sort', out_shape=(jax.ShapeDt...  3.85 us
  transfers between devices with their start and end apart: 10, of which 6 were waited for; matrix products, arithmetic and copies ran while one was open for 0% of the time, Pallas kernels for 15%

profile of v1, /device:TPU:40, one launch (start us, length us, event | category | flops | bytes accessed | tf_op | source)
XLA Modules:
  0.0 88.8 jit_solution(5091387909206518968)
XLA Ops:
  0.6 0.0 copy-start.2
  0.6 10.3 %droplet_states.1 = (s32[128,128]{1,0:T(8,128)}, s32[8,128]{1,0:T(8,128)}, f32[128,8,128]{2,1,0:T(8,128)}, s32[576,128]{1,0:T(8,128)}, f32[8,128]{1,0:T(8,128)},...) custom-call(s32[128,128]{1,0:T(8,128)} %bitcast.16, f32[3,128,256]{2,1,0:T(8,128)} %bitcast.12, f32[3,128,128]{2,1,0:T(8,128)} %bitcast.14, ...), custom_call_target="tpu_custom_call" | custom-call | tf_op jit(solution)/shard_map/droplet_states/pallas_call | solution.py:400
  11.0 6.4 %collective-permute-start = (f32[16,8,128]{2,1,0:T(8,128)}, f32[16,8,128]{2,1,0:T(8,128)S(1)}, u32[]{:S(2)}, u32[]{:S(2)}) collective-permute-start(f32[16,8,128]{2,1,0:T(8,128)} %get-tuple-element.31), channel_id=1, source_target_pairs={{0,1},{1,0},{2,3},{3,2},{4,5},{5,4},{6,7},{7,6},{8,9},{9,8},{10,11... | collective-permute-start | bytes 196616 | tf_op jit(solution)/shard_map/ppermute | solution.py:935
  17.3 1.8 %collective-permute-start.1 = (f32[16,8,128]{2,1,0:T(8,128)}, f32[16,8,128]{2,1,0:T(8,128)S(1)}, u32[]{:S(2)}, u32[]{:S(2)}) collective-permute-start(f32[16,8,128]{2,1,0:T(8,128)} %get-tuple-element.32), channel_id=1, source_target_pairs={{0,7},{1,2},{2,1},{3,4},{4,3},{5,6},{6,5},{7,0},{8,15},{9,10},{10,... | collective-permute-start | bytes 196616 | tf_op jit(solution)/shard_map/ppermute | solution.py:935
  19.8 3.9 %pair_sort.1 = (s32[2,128,128]{2,1,0:T(8,128)S(1)}, s32[16,128]{1,0:T(8,128)S(1)}) custom-call(s32[1,1]{1,0:T(1,128)} %bitcast.9.live_ref, s32[2,256,128]{2,1,0:T(8,128)S(1)} %bitcast.11), custom_call_target="tpu_custom_call" | custom-call | tf_op jit(solution)/shard_map/pair_sort/pallas_call | solution.py:474
  23.7 0.0 collective-permute-done.one_in
  23.7 5.4 %collective-permute-done.1.other_in = f32[16,8,128]{2,1,0:T(8,128)S(1)} collective-permute-done((f32[16,8,128]{2,1,0:T(8,128)}, f32[16,8,128]{2,1,0:T(8,128)S(1)}, u32[]{:S(2)}, u32[]{:S(2)}) %collective-permute-start.1) | collective-permute-done | bytes 65568 | tf_op jit(solution)/shard_map/ppermute | solution.py:935
  29.1 1.0 %copy-done = s32[576,128]{1,0:T(8,128)S(1)} copy-done((s32[576,128]{1,0:T(8,128)S(1)}, s32[576,128]{1,0:T(8,128)}, u32[]{:S(2)}) %copy-start) | copy-done | bytes 294936
  30.0 8.0 %near_pairs.1 = (f32[3,128,128]{2,1,0:T(8,128)S(1)}, f32[3,16,128]{2,1,0:T(8,128)S(1)}, f32[3,16,128]{2,1,0:T(8,128)S(1)}) custom-call(s32[16,128]{1,0:T(8,128)S(1)} %get-tuple-element.27.ends, s32[2,128,128]{2,1,0:T(8,128)S(1)} %get-tuple-element.28.keys_ref, s32[576,128]{1,0:T(8,128)S(1)} %copy-done, f32[8,128]{1,0:T(8,128)S(1)} %copy-done.4, ...), custom_call_target="tpu_custom_call" | custom-call | tf_op jit(solution)/shard_map/near_pairs/pallas_call | solution.py:679
  38.0 0.0 copy-start.1
  38.0 1.6 %collective-permute-start.2 = (f32[3,16,128]{2,1,0:T(8,128)S(1)}, f32[3,16,128]{2,1,0:T(8,128)S(1)}, u32[]{:S(2)}, u32[]{:S(2)}) collective-permute-start(f32[3,16,128]{2,1,0:T(8,128)S(1)} %get-tuple-element.34), channel_id=1, source_target_pairs={{0,1},{1,0},{2,3},{3,2},{4,5},{5,4},{6,7},{7,6},{8,9},{9,8},{10,11... | collective-permute-start | bytes 73736 | tf_op jit(solution)/shard_map/ppermute | solution.py:935
  39.7 4.6 %collective-permute-start.3 = (f32[3,16,128]{2,1,0:T(8,128)S(1)}, f32[3,16,128]{2,1,0:T(8,128)S(1)}, u32[]{:S(2)}, u32[]{:S(2)}) collective-permute-start(f32[3,16,128]{2,1,0:T(8,128)S(1)} %get-tuple-element.35), channel_id=1, source_target_pairs={{0,7},{1,2},{2,1},{3,4},{4,3},{5,6},{6,5},{7,0},{8,15},{9,10},{10,... | collective-permute-start | bytes 73736 | tf_op jit(solution)/shard_map/ppermute | solution.py:935
  44.3 9.8 %own_pairs.1.corr_ref = f32[3,128,128]{2,1,0:T(8,128)S(1)} custom-call(s32[1,1]{1,0:T(1,128)} %bitcast.10.live_ref, s32[16,128]{1,0:T(8,128)S(1)} %get-tuple-element.27.ends, s32[2,128,128]{2,1,0:T(8,128)S(1)} %get-tuple-element.28.keys_ref, s32[576,128]{1,0:T(8,128)S(1)} %copy-done, f32[8,128]{1,0:T(8,128)S(1)} %copy-done.4, ...), custom_call_target="tpu_custom_call" | custom-call | tf_op jit(solution)/shard_map/own_pairs/pallas_call | solution.py:696
  54.1 0.0 collective-permute-done.2.one_in
  54.1 0.0 collective-permute-done.3.other_in
  54.2 0.6 copy-done.5
  54.8 5.7 %deposits.1 = (f32[3,128,256]{2,1,0:T(8,128)S(1)}, f32[3,128,128]{2,1,0:T(8,128)}, f32[3,32,256]{2,1,0:T(8,128)S(1)}, f32[3,32,256]{2,1,0:T(8,128)S(1)}) custom-call(s32[8,128]{1,0:T(8,128)S(1)} %copy-done.5, s32[128,128]{1,0:T(8,128)S(1)} %copy-done.3, f32[128,8,128]{2,1,0:T(8,128)S(1)} %copy-done.1, f32[3,128,128]{2,1,0:T(8,128)S(1)} %own_pairs.1.corr_ref, ...), custom_call_target="tpu_custom_call" | custom-call | tf_op jit(solution)/shard_map/deposits/pallas_call | solution.py:818
  60.5 4.1 %collective-permute-start.4 = (f32[3,32,256]{2,1,0:T(8,128)S(1)}, f32[3,32,256]{2,1,0:T(8,128)S(1)}, u32[]{:S(2)}, u32[]{:S(2)}) collective-permute-start(f32[3,32,256]{2,1,0:T(8,128)S(1)} %get-tuple-element.38), channel_id=1, source_target_pairs={{0,64},{64,0},{128,192},{192,128},{1,65},{65,1},{129,193},{193,129... | collective-permute-start | bytes 294920 | tf_op jit(solution)/shard_map/ppermute | solution.py:935
  64.6 1.9 %collective-permute-start.5 = (f32[3,32,256]{2,1,0:T(8,128)S(1)}, f32[3,32,256]{2,1,0:T(8,128)S(1)}, u32[]{:S(2)}, u32[]{:S(2)}) collective-permute-start(f32[3,32,256]{2,1,0:T(8,128)S(1)} %get-tuple-element.39), channel_id=1, source_target_pairs={{0,0},{64,128},{128,64},{192,192},{1,1},{65,129},{129,65},{193,193... | collective-permute-start | bytes 294920 | tf_op jit(solution)/shard_map/ppermute | solution.py:935
  66.5 0.7 collective-permute-done.4.one_in
  67.2 3.9 %collective-permute-done.5.other_in = f32[3,32,256]{2,1,0:T(8,128)S(1)} collective-permute-done((f32[3,32,256]{2,1,0:T(8,128)S(1)}, f32[3,32,256]{2,1,0:T(8,128)S(1)}, u32[]{:S(2)}, u32[]{:S(2)}) %collective-permute-start.5) | collective-permute-done | bytes 98336 | tf_op jit(solution)/shard_map/ppermute | solution.py:935
  71.1 0.2 axial_filter.1
  71.3 0.1 collective-permute-start.6
  71.4 1.9 %collective-permute-start.7 = (f32[3,16,256]{2,1,0:T(8,128)S(1)}, f32[3,16,256]{2,1,0:T(8,128)S(1)}, u32[]{:S(2)}, u32[]{:S(2)}) collective-permute-start(f32[3,16,256]{2,1,0:T(8,128)S(1)} %get-tuple-element.42), channel_id=1, source_target_pairs={{0,0},{8,16},{16,8},{24,32},{32,24},{40,48},{48,40},{56,56},{1,1},... | collective-permute-start | bytes 147464 | tf_op jit(solution)/shard_map/ppermute | solution.py:935
  73.4 0.0 collective-permute-done.6.one_in
  73.4 3.5 %collective-permute-done.7.other_in = f32[3,16,256]{2,1,0:T(8,128)S(1)} collective-permute-done((f32[3,16,256]{2,1,0:T(8,128)S(1)}, f32[3,16,256]{2,1,0:T(8,128)S(1)}, u32[]{:S(2)}, u32[]{:S(2)}) %collective-permute-start.7) | collective-permute-done | bytes 49184 | tf_op jit(solution)/shard_map/ppermute | solution.py:935
  76.9 0.5 radial_filter.1
  77.4 0.1 collective-permute-start.8
  77.4 5.0 %collective-permute-start.9 = (f32[8,128]{1,0:T(8,128)S(1)}, f32[8,128]{1,0:T(8,128)S(1)}, u32[]{:S(2)}, u32[]{:S(2)}) collective-permute-start(f32[8,128]{1,0:T(8,128)S(1)} %get-tuple-element.45), channel_id=1, source_target_pairs={{0,7},{1,2},{2,1},{3,4},{4,3},{5,6},{6,5},{7,0},{8,15},{9,10},{10,... | collective-permute-start | bytes 12296 | tf_op jit(solution)/shard_map/ppermute | solution.py:935
  82.4 2.5 %collective-permute-done.8.one_in = f32[8,128]{1,0:T(8,128)S(1)} collective-permute-done((f32[8,128]{1,0:T(8,128)S(1)}, f32[8,128]{1,0:T(8,128)S(1)}, u32[]{:S(2)}, u32[]{:S(2)}) %collective-permute-start.8) | collective-permute-done | bytes 4128 | tf_op jit(solution)/shard_map/ppermute | solution.py:935
  84.9 2.2 %collective-permute-done.9.other_in = f32[8,128]{1,0:T(8,128)S(1)} collective-permute-done((f32[8,128]{1,0:T(8,128)S(1)}, f32[8,128]{1,0:T(8,128)S(1)}, u32[]{:S(2)}, u32[]{:S(2)}) %collective-permute-start.9) | collective-permute-done | bytes 4128 | tf_op jit(solution)/shard_map/ppermute | solution.py:935
  87.1 1.6 %azimuthal_filter.1 = f32[3,128,256]{2,1,0:T(8,128)} custom-call(f32[3,128,256]{2,1,0:T(8,128)S(1)} %get-tuple-element.43.cells_ref, f32[8,128]{1,0:T(8,128)S(1)} %collective-permute-done.8.one_in, f32[8,128]{1,0:T(8,128)S(1)} %collective-permute-done.9.other_in), custom_call_target="tpu_custom_call" | custom-call | tf_op jit(solution)/shard_map/azimuthal_filter/pallas_call | solution.py:919
  (8 shorter events, 0.0 us)
Async XLA Ops:
  0.6 19.2 %copy-start.2 = (s32[2,1,1,32768]{3,2,1,0:T(1,128)S(1)}, s32[2,1,1,32768]{3,2,1,0:T(1,128)}, u32[]{:S(2)}) copy-start(s32[2,1,1,32768]{3,2,1,0:T(1,128)} %param.11) | copy-start | bytes 786436
  11.0 12.7 %collective-permute-start = (f32[16,8,128]{2,1,0:T(8,128)}, f32[16,8,128]{2,1,0:T(8,128)S(1)}, u32[]{:S(2)}, u32[]{:S(2)}) collective-permute-start(f32[16,8,128]{2,1,0:T(8,128)} %get-tuple-element.31), channel_id=1, source_target_pairs={{0,1},{1,0},{2,3},{3,2},{4,5},{5,4},{6,7},{7,6},{8,9},{9,8},{10,11... | collective-permute-start | bytes 196616 | tf_op jit(solution)/shard_map/ppermute | solution.py:935
  17.3 11.7 %collective-permute-start.1 = (f32[16,8,128]{2,1,0:T(8,128)}, f32[16,8,128]{2,1,0:T(8,128)S(1)}, u32[]{:S(2)}, u32[]{:S(2)}) collective-permute-start(f32[16,8,128]{2,1,0:T(8,128)} %get-tuple-element.32), channel_id=1, source_target_pairs={{0,7},{1,2},{2,1},{3,4},{4,3},{5,6},{6,5},{7,0},{8,15},{9,10},{10,... | collective-permute-start | bytes 196616 | tf_op jit(solution)/shard_map/ppermute | solution.py:935
  23.7 5.4 %copy-start.4 = (f32[8,128]{1,0:T(8,128)S(1)}, f32[8,128]{1,0:T(8,128)}, u32[]{:S(2)}) copy-start(f32[8,128]{1,0:T(8,128)} %get-tuple-element.30.largest_ref) | copy-start | bytes 12292
  29.1 1.0 %copy-start = (s32[576,128]{1,0:T(8,128)S(1)}, s32[576,128]{1,0:T(8,128)}, u32[]{:S(2)}) copy-start(s32[576,128]{1,0:T(8,128)} %get-tuple-element.29.words_ref) | copy-start | bytes 884740
  38.0 16.1 %copy-start.1 = (f32[128,8,128]{2,1,0:T(8,128)S(1)}, f32[128,8,128]{2,1,0:T(8,128)}, u32[]{:S(2)}) copy-start(f32[128,8,128]{2,1,0:T(8,128)} %get-tuple-element.26.table_ref) | copy-start | bytes 1572868
  38.0 16.1 %collective-permute-start.2 = (f32[3,16,128]{2,1,0:T(8,128)S(1)}, f32[3,16,128]{2,1,0:T(8,128)S(1)}, u32[]{:S(2)}, u32[]{:S(2)}) collective-permute-start(f32[3,16,128]{2,1,0:T(8,128)S(1)} %get-tuple-element.34), channel_id=1, source_target_pairs={{0,1},{1,0},{2,3},{3,2},{4,5},{5,4},{6,7},{7,6},{8,9},{9,8},{10,11... | collective-permute-start | bytes 73736 | tf_op jit(solution)/shard_map/ppermute | solution.py:935
  39.7 14.5 %collective-permute-start.3 = (f32[3,16,128]{2,1,0:T(8,128)S(1)}, f32[3,16,128]{2,1,0:T(8,128)S(1)}, u32[]{:S(2)}, u32[]{:S(2)}) collective-permute-start(f32[3,16,128]{2,1,0:T(8,128)S(1)} %get-tuple-element.35), channel_id=1, source_target_pairs={{0,7},{1,2},{2,1},{3,4},{4,3},{5,6},{6,5},{7,0},{8,15},{9,10},{10,... | collective-permute-start | bytes 73736 | tf_op jit(solution)/shard_map/ppermute | solution.py:935
  44.3 9.9 %copy-start.3 = (s32[128,128]{1,0:T(8,128)S(1)}, s32[128,128]{1,0:T(8,128)}, u32[]{:S(2)}) copy-start(s32[128,128]{1,0:T(8,128)} %get-tuple-element.25.keys_ref) | copy-start | bytes 196612
  54.1 0.7 copy-start.5
  60.5 6.7 %collective-permute-start.4 = (f32[3,32,256]{2,1,0:T(8,128)S(1)}, f32[3,32,256]{2,1,0:T(8,128)S(1)}, u32[]{:S(2)}, u32[]{:S(2)}) collective-permute-start(f32[3,32,256]{2,1,0:T(8,128)S(1)} %get-tuple-element.38), channel_id=1, source_target_pairs={{0,64},{64,0},{128,192},{192,128},{1,65},{65,1},{129,193},{193,129... | collective-permute-start | bytes 294920 | tf_op jit(solution)/shard_map/ppermute | solution.py:935
  64.6 6.5 %collective-permute-start.5 = (f32[3,32,256]{2,1,0:T(8,128)S(1)}, f32[3,32,256]{2,1,0:T(8,128)S(1)}, u32[]{:S(2)}, u32[]{:S(2)}) collective-permute-start(f32[3,32,256]{2,1,0:T(8,128)S(1)} %get-tuple-element.39), channel_id=1, source_target_pairs={{0,0},{64,128},{128,64},{192,192},{1,1},{65,129},{129,65},{193,193... | collective-permute-start | bytes 294920 | tf_op jit(solution)/shard_map/ppermute | solution.py:935
  71.3 2.0 %collective-permute-start.6 = (f32[3,16,256]{2,1,0:T(8,128)S(1)}, f32[3,16,256]{2,1,0:T(8,128)S(1)}, u32[]{:S(2)}, u32[]{:S(2)}) collective-permute-start(f32[3,16,256]{2,1,0:T(8,128)S(1)} %get-tuple-element.41), channel_id=1, source_target_pairs={{0,8},{8,0},{16,24},{24,16},{32,40},{40,32},{48,56},{56,48},{1,9},... | collective-permute-start | bytes 147464 | tf_op jit(solution)/shard_map/ppermute | solution.py:935
  71.4 5.4 %collective-permute-start.7 = (f32[3,16,256]{2,1,0:T(8,128)S(1)}, f32[3,16,256]{2,1,0:T(8,128)S(1)}, u32[]{:S(2)}, u32[]{:S(2)}) collective-permute-start(f32[3,16,256]{2,1,0:T(8,128)S(1)} %get-tuple-element.42), channel_id=1, source_target_pairs={{0,0},{8,16},{16,8},{24,32},{32,24},{40,48},{48,40},{56,56},{1,1},... | collective-permute-start | bytes 147464 | tf_op jit(solution)/shard_map/ppermute | solution.py:935
  77.4 7.6 %collective-permute-start.8 = (f32[8,128]{1,0:T(8,128)S(1)}, f32[8,128]{1,0:T(8,128)S(1)}, u32[]{:S(2)}, u32[]{:S(2)}) collective-permute-start(f32[8,128]{1,0:T(8,128)S(1)} %get-tuple-element.44), channel_id=1, source_target_pairs={{0,1},{1,0},{2,3},{3,2},{4,5},{5,4},{6,7},{7,6},{8,9},{9,8},{10,11... | collective-permute-start | bytes 12296 | tf_op jit(solution)/shard_map/ppermute | solution.py:935
  77.4 9.7 %collective-permute-start.9 = (f32[8,128]{1,0:T(8,128)S(1)}, f32[8,128]{1,0:T(8,128)S(1)}, u32[]{:S(2)}, u32[]{:S(2)}) collective-permute-start(f32[8,128]{1,0:T(8,128)S(1)} %get-tuple-element.45), channel_id=1, source_target_pairs={{0,7},{1,2},{2,1},{3,4},{4,3},{5,6},{6,5},{7,0},{8,15},{9,10},{10,... | collective-permute-start | bytes 12296 | tf_op jit(solution)/shard_map/ppermute | solution.py:935

commit v2 on v1

--- a/solution.py
+++ b/solution.py
@@ -123,6 +123,22 @@
     hit = rel == iota[0:16, :]
     zero = jnp.zeros((16, LANES), jnp.bfloat16)
     return jnp.concatenate([jnp.where(hit, p, zero) for part in parts for p in part], axis=0)
+
+
+def block_product(rows, hots):
+    zero = jnp.zeros
+    lines = [
+        jnp.concatenate(
+            [x if m == n else zero(x.shape, x.dtype) for m in range(len(rows))], axis=1
+        )
+        for n, x in enumerate(rows)
+    ]
+    return lax.dot_general(
+        jnp.concatenate(lines, axis=0),
+        jnp.concatenate(hots, axis=1),
+        NT,
+        preferred_element_type=jnp.float32,
+    )
 
 
 def spread_add(rows, hots):
@@ -483,25 +499,33 @@
     )(live, pairs)
 
 
+def group_ends(g, ends, part):
+    g = jnp.minimum(g, 2 * LANES - 1)
+    at, lane = 4 * (g & 1), g >> 1
+    low, high, _ = part
+    return (
+        ends[at, lane] & -2,
+        ends[at + 1, lane],
+        jnp.maximum(ends[at + 2, lane], low),
+        jnp.minimum(ends[at + 3, lane], high - 1),
+    )
+
+
 def take_items(state, groups, ends, part):
     low, high, heads = part
     items = []
     for _ in range(ROWS):
-        g, bucket, head = state
-        valid = g < groups
-        seen = jnp.minimum(g, 2 * LANES - 1)
-        at, lane = 4 * (seen & 1), seen >> 1
-        items.append((seen, jnp.where(valid, bucket, -1), head, jnp.minimum(bucket, high) - low))
-        more_heads = head + heads <= ends[at + 1, lane]
-        more_tails = bucket < jnp.minimum(ends[at + 3, lane], high - 1)
-        step = jnp.where(more_heads | more_tails, 0, 1)
-        g = jnp.minimum(g + step, 2 * LANES)
-        seen = jnp.minimum(g, 2 * LANES - 1)
-        at, lane = 4 * (seen & 1), seen >> 1
-        head = jnp.where(more_heads, head + heads, ends[at, lane] & -2)
-        same = jnp.where(more_heads, bucket, bucket + 1)
-        bucket = jnp.where(step == 1, jnp.maximum(ends[at + 2, lane], low), same)
-        state = (g, bucket, head)
+        g, bucket, head, now, later = state
+        place = jnp.minimum(bucket, high) - low
+        items.append((jnp.minimum(g, 2 * LANES - 1), jnp.where(g < groups, bucket, -1), head, place))
+        ahead = group_ends(g + 2, ends, part)
+        more_heads = head + heads <= now[1]
+        stay = more_heads | (bucket < now[3])
+        head = jnp.where(more_heads, head + heads, jnp.where(stay, now[0], later[0]))
+        bucket = jnp.where(more_heads, bucket, jnp.where(stay, bucket + 1, later[2]))
+        now = tuple(jnp.where(stay, x, y) for x, y in zip(now, later))
+        later = tuple(jnp.where(stay, x, y) for x, y in zip(later, ahead))
+        state = (jnp.where(stay, g, g + 1), bucket, head, now, later)
     return items, state
 
 
@@ -563,26 +587,22 @@
 def pair_scatter(k, item, val, head_sum, tail_sum, iota, iota8):
     first, tail_first = item
     parts = [[packed_row(val.at[4 + 3 * n + c], k) for c in range(3)] for n in range(2)]
-    rows = spread_rows(packed_row(val.at[0], k), parts, iota)
-    out = spread_add([rows], [one_hot_rows(packed_row(val.at[1], k), iota)])
-    for c in range(3):
-        head_sum[c, pl.ds(first, 16), :] += out[16 * c : 16 * c + 16]
-
+    heads = spread_rows(packed_row(val.at[0], k), parts, iota)
     hit = packed_row(val.at[2], k) == iota8[...]
     zero = jnp.zeros((16, LANES), jnp.bfloat16)
-    tiles = []
+    tails = []
     for n in range(10, 16, 2):
         both = jnp.concatenate([wide(val, n, k), wide(val, n + 1, k)], axis=0)
-        tiles.append(jnp.where(hit, both.astype(jnp.bfloat16), zero))
-    out = lax.dot_general(
-        jnp.concatenate(tiles, axis=0),
-        one_hot_rows(packed_row(val.at[3], k), iota),
-        NT,
-        preferred_element_type=jnp.float32,
-    )
+        tails.append(jnp.where(hit, both.astype(jnp.bfloat16), zero))
+    tails = jnp.concatenate(tails, axis=0)
+    out = block_product(
+        [heads, tails], [one_hot_rows(packed_row(val.at[n], k), iota) for n in (1, 3)]
+    )
+    for c in range(3):
+        head_sum[c, pl.ds(first, 16), :] += out[16 * c : 16 * c + 16] + out[16 * c + 48 : 16 * c + 64]
     at = pl.ds(pl.multiple_of(tail_first, 8), 8)
     for c in range(3):
-        tail_sum[c, at, :] += out[8 * c : 8 * c + 8] + out[24 + 8 * c : 32 + 8 * c]
+        tail_sum[c, at, :] += out[8 * c + 96 : 8 * c + 104] + out[8 * c + 120 : 8 * c + 128]
 
 
 def run_pairs(groups, start, part, ends, keys_ref, near, far, sums, iota, iota8, scratch):
@@ -601,8 +621,8 @@
                 pair_scatter(k, pending[k], val, *sums, iota, iota8)
         return tuple((item[2], item[3] * 8) for item in items), state, items[0][1] >= 0
 
-    at, lane = 4 * (start & 1), start >> 1
-    state = (start, jnp.maximum(ends[at + 2, lane], part[0]), ends[at, lane] & -2)
+    now, later = group_ends(start, ends, part), group_ends(start + 1, ends, part)
+    state = (start, now[2], now[0], now, later)
 
     def one(carry):
         pending, state, _ = carry
@@ -731,7 +751,7 @@
             val[2 + 2 * c + n] = part
 
 
-def force_add(g, base, slot, cells, iota):
+def force_rows(g, base, slot, iota):
     val = slot[2]
 
     def row(n):
@@ -741,11 +761,19 @@
 
     rel = row(0) - base.astype(jnp.float32).astype(jnp.bfloat16)
     parts = [[row(2 + 2 * c + n) for c in range(3)] for n in range(2)]
-    out = spread_add([spread_rows(rel, parts, iota)], [one_hot_rows(row(1), iota)])
-    for c in range(3):
-        for half in range(2):
-            part = out[16 * c : 16 * c + 16, half * LANES : (half + 1) * LANES]
-            cells[2 * c + half, pl.ds(base, 16), :] += part
+    return spread_rows(rel, parts, iota), one_hot_rows(row(1), iota)
+
+
+def force_add(groups, bases, slot, cells, iota):
+    pieces = [force_rows(g, base, slot, iota) for g, base in zip(groups, bases)]
+    out = block_product([p[0] for p in pieces], [p[1] for p in pieces])
+    for n, base in enumerate(bases):
+        for c in range(3):
+            at = 96 * n + 16 * c
+            total = out[at : at + 16] + out[at + 48 : at + 64]
+            for half in range(2):
+                part = total[:, half * LANES : (half + 1) * LANES]
+                cells[2 * c + half, pl.ds(base, 16), :] += part
 
 
 def force_rest(block, ends, slot, cells, iota):
@@ -755,7 +783,7 @@
             first, most = ends[0, block * 16 + g], ends[1, block * 16 + g]
 
             def trip(t, carry):
-                force_add(g, jnp.minimum(first + 16 * t, LANES), slot, cells, iota)
+                force_add([g], [jnp.minimum(first + 16 * t, LANES)], slot, cells, iota)
                 return carry
 
             lax.fori_loop(1, (most - first) // 16 + 1, trip, 0)
@@ -768,8 +796,9 @@
     if gather:
         force_gather(gather[0], keys_ref, table_ref, total_ref, gather[1])
     if scatter:
-        for g in range(16):
-            force_add(g, ends[0, scatter[0] * 16 + g], scatter[1], cells, iota)
+        for g in range(0, 16, 2):
+            bases = [ends[0, scatter[0] * 16 + n] for n in (g, g + 1)]
+            force_add([g, g + 1], bases, scatter[1], cells, iota)
         force_rest(scatter[0], ends, scatter[1], cells, iota)
 
 

time: 90 us -> 86.3 us (0.959)
  waiting for transfers between devices: 18.2 us -> 15.8 us
  Pallas kernels: 40 us -> 38.4 us
    ppermute x10, waiting for transfers between devices: 18.2 us -> 15.8 us  [swapped(): lax.ppermute(x, axis, [(i, partner(i, odd)) for i in range(count)])]
    pallas_call x1, Pallas kernels: 7.97 us -> 6.22 us  [near_pairs(): pl.pallas_call(near_pairs_kernel, name='near_pairs', out_shape=(jax.Shape...]
where the time goes in v2:
time: 86.3 us; the launch traced here: 85.5 us
  Pallas kernels  38.4 us (44%)
  starting transfers between devices  28.2 us (33%)
  waiting for transfers between devices  15.8 us (18%)
  local copies, waits for them, and re-layouts  1.62 us (2%)
  between operations  1.44 us (2%)
    ppermute x10, starting transfers between devices, swapped(): lax.ppermute(x, axis, [(i, partner(i, odd)) for i in range(count)])  28.2 us
    ppermute x10, waiting for transfers between devices, swapped(): lax.ppermute(x, axis, [(i, partner(i, odd)) for i in range(count)])  15.8 us
    pallas_call x1, Pallas kernels, droplet_states(): pl.pallas_call(states_kernel, name='droplet_states', out_shape=(jax.Shape...  10.8 us
    pallas_call x1, Pallas kernels, own_pairs(): pl.pallas_call(own_pairs_kernel, name='own_pairs', out_shape=jax.ShapeDty...  9.1 us
    pallas_call x1, Pallas kernels, near_pairs(): pl.pallas_call(near_pairs_kernel, name='near_pairs', out_shape=(jax.Shape...  6.22 us
    pallas_call x1, Pallas kernels, deposits(): pl.pallas_call(deposit_kernel, name='deposits', out_shape=(jax.ShapeDtype...  6.02 us
    pallas_call x1, Pallas kernels, pair_sort(): pl.pallas_call(pair_sort_kernel, name='pair_sort', out_shape=(jax.ShapeDt...  3.85 us
  transfers between devices with their start and end apart: 10, of which 6 were waited for; matrix products, arithmetic and copies ran while one was open for 0% of the time, Pallas kernels for 15%

profile of v2, /device:TPU:40, one launch (start us, length us, event | category | flops | bytes accessed | tf_op | source)
XLA Modules:
  0.0 85.5 jit_solution(6196793150052951315)
XLA Ops:
  0.6 10.8 %droplet_states.1 = (s32[128,128]{1,0:T(8,128)}, s32[8,128]{1,0:T(8,128)}, f32[128,8,128]{2,1,0:T(8,128)}, s32[576,128]{1,0:T(8,128)}, f32[8,128]{1,0:T(8,128)},...) custom-call(s32[128,128]{1,0:T(8,128)} %bitcast.16, f32[3,128,256]{2,1,0:T(8,128)} %bitcast.12, f32[3,128,128]{2,1,0:T(8,128)} %bitcast.14, ...), custom_call_target="tpu_custom_call" | custom-call | tf_op jit(solution)/shard_map/droplet_states/pallas_call | solution.py:416
  11.5 4.7 %collective-permute-start = (f32[16,8,128]{2,1,0:T(8,128)}, f32[16,8,128]{2,1,0:T(8,128)S(1)}, u32[]{:S(2)}, u32[]{:S(2)}) collective-permute-start(f32[16,8,128]{2,1,0:T(8,128)} %get-tuple-element.31), channel_id=1, source_target_pairs={{0,1},{1,0},{2,3},{3,2},{4,5},{5,4},{6,7},{7,6},{8,9},{9,8},{10,11... | collective-permute-start | bytes 196616 | tf_op jit(solution)/shard_map/ppermute | solution.py:964
  16.2 4.5 %collective-permute-start.1 = (f32[16,8,128]{2,1,0:T(8,128)}, f32[16,8,128]{2,1,0:T(8,128)S(1)}, u32[]{:S(2)}, u32[]{:S(2)}) collective-permute-start(f32[16,8,128]{2,1,0:T(8,128)} %get-tuple-element.32), channel_id=1, source_target_pairs={{0,7},{1,2},{2,1},{3,4},{4,3},{5,6},{6,5},{7,0},{8,15},{9,10},{10,... | collective-permute-start | bytes 196616 | tf_op jit(solution)/shard_map/ppermute | solution.py:964
  21.4 0.0 copy-done.2
  21.4 3.9 %pair_sort.1 = (s32[2,128,128]{2,1,0:T(8,128)S(1)}, s32[16,128]{1,0:T(8,128)S(1)}) custom-call(s32[1,1]{1,0:T(1,128)} %bitcast.9.live_ref, s32[2,256,128]{2,1,0:T(8,128)S(1)} %bitcast.11), custom_call_target="tpu_custom_call" | custom-call | tf_op jit(solution)/shard_map/pair_sort/pallas_call | solution.py:490
  25.2 0.0 copy-start.4
  25.2 0.0 collective-permute-done.one_in
  25.3 1.8 %collective-permute-done.1.other_in = f32[16,8,128]{2,1,0:T(8,128)S(1)} collective-permute-done((f32[16,8,128]{2,1,0:T(8,128)}, f32[16,8,128]{2,1,0:T(8,128)S(1)}, u32[]{:S(2)}, u32[]{:S(2)}) %collective-permute-start.1) | collective-permute-done | bytes 65568 | tf_op jit(solution)/shard_map/ppermute | solution.py:964
  27.0 1.0 %copy-done = s32[576,128]{1,0:T(8,128)S(1)} copy-done((s32[576,128]{1,0:T(8,128)S(1)}, s32[576,128]{1,0:T(8,128)}, u32[]{:S(2)}) %copy-start) | copy-done | bytes 294936
  28.0 6.2 %near_pairs.1 = (f32[3,128,128]{2,1,0:T(8,128)S(1)}, f32[3,16,128]{2,1,0:T(8,128)S(1)}, f32[3,16,128]{2,1,0:T(8,128)S(1)}) custom-call(s32[16,128]{1,0:T(8,128)S(1)} %get-tuple-element.27.ends, s32[2,128,128]{2,1,0:T(8,128)S(1)} %get-tuple-element.28.keys_ref, s32[576,128]{1,0:T(8,128)S(1)} %copy-done, f32[8,128]{1,0:T(8,128)S(1)} %copy-done.4, ...), custom_call_target="tpu_custom_call" | custom-call | tf_op jit(solution)/shard_map/near_pairs/pallas_call | solution.py:699
  34.2 2.9 %collective-permute-start.2 = (f32[3,16,128]{2,1,0:T(8,128)S(1)}, f32[3,16,128]{2,1,0:T(8,128)S(1)}, u32[]{:S(2)}, u32[]{:S(2)}) collective-permute-start(f32[3,16,128]{2,1,0:T(8,128)S(1)} %get-tuple-element.34), channel_id=1, source_target_pairs={{0,1},{1,0},{2,3},{3,2},{4,5},{5,4},{6,7},{7,6},{8,9},{9,8},{10,11... | collective-permute-start | bytes 73736 | tf_op jit(solution)/shard_map/ppermute | solution.py:964
  37.1 6.7 %collective-permute-start.3 = (f32[3,16,128]{2,1,0:T(8,128)S(1)}, f32[3,16,128]{2,1,0:T(8,128)S(1)}, u32[]{:S(2)}, u32[]{:S(2)}) collective-permute-start(f32[3,16,128]{2,1,0:T(8,128)S(1)} %get-tuple-element.35), channel_id=1, source_target_pairs={{0,7},{1,2},{2,1},{3,4},{4,3},{5,6},{6,5},{7,0},{8,15},{9,10},{10,... | collective-permute-start | bytes 73736 | tf_op jit(solution)/shard_map/ppermute | solution.py:964
  43.8 9.1 %own_pairs.1.corr_ref = f32[3,128,128]{2,1,0:T(8,128)S(1)} custom-call(s32[1,1]{1,0:T(1,128)} %bitcast.10.live_ref, s32[16,128]{1,0:T(8,128)S(1)} %get-tuple-element.27.ends, s32[2,128,128]{2,1,0:T(8,128)S(1)} %get-tuple-element.28.keys_ref, s32[576,128]{1,0:T(8,128)S(1)} %copy-done, f32[8,128]{1,0:T(8,128)S(1)} %copy-done.4, ...), custom_call_target="tpu_custom_call" | custom-call | tf_op jit(solution)/shard_map/own_pairs/pallas_call | solution.py:716
  53.0 0.0 collective-permute-done.2.one_in
  53.0 0.0 collective-permute-done.3.other_in
  53.0 0.6 copy-done.5
  53.6 6.0 %deposits.1 = (f32[3,128,256]{2,1,0:T(8,128)S(1)}, f32[3,128,128]{2,1,0:T(8,128)}, f32[3,32,256]{2,1,0:T(8,128)S(1)}, f32[3,32,256]{2,1,0:T(8,128)S(1)}) custom-call(s32[8,128]{1,0:T(8,128)S(1)} %copy-done.5, s32[128,128]{1,0:T(8,128)S(1)} %copy-done.3, f32[128,8,128]{2,1,0:T(8,128)S(1)} %copy-done.1, f32[3,128,128]{2,1,0:T(8,128)S(1)} %own_pairs.1.corr_ref, ...), custom_call_target="tpu_custom_call" | custom-call | tf_op jit(solution)/shard_map/deposits/pallas_call | solution.py:847
  59.7 0.9 %collective-permute-start.4 = (f32[3,32,256]{2,1,0:T(8,128)S(1)}, f32[3,32,256]{2,1,0:T(8,128)S(1)}, u32[]{:S(2)}, u32[]{:S(2)}) collective-permute-start(f32[3,32,256]{2,1,0:T(8,128)S(1)} %get-tuple-element.38), channel_id=1, source_target_pairs={{0,64},{64,0},{128,192},{192,128},{1,65},{65,1},{129,193},{193,129... | collective-permute-start | bytes 294920 | tf_op jit(solution)/shard_map/ppermute | solution.py:964
  60.6 1.9 %collective-permute-start.5 = (f32[3,32,256]{2,1,0:T(8,128)S(1)}, f32[3,32,256]{2,1,0:T(8,128)S(1)}, u32[]{:S(2)}, u32[]{:S(2)}) collective-permute-start(f32[3,32,256]{2,1,0:T(8,128)S(1)} %get-tuple-element.39), channel_id=1, source_target_pairs={{0,0},{64,128},{128,64},{192,192},{1,1},{65,129},{129,65},{193,193... | collective-permute-start | bytes 294920 | tf_op jit(solution)/shard_map/ppermute | solution.py:964
  62.5 1.8 %collective-permute-done.4.one_in = f32[3,32,256]{2,1,0:T(8,128)S(1)} collective-permute-done((f32[3,32,256]{2,1,0:T(8,128)S(1)}, f32[3,32,256]{2,1,0:T(8,128)S(1)}, u32[]{:S(2)}, u32[]{:S(2)}) %collective-permute-start.4) | collective-permute-done | bytes 98336 | tf_op jit(solution)/shard_map/ppermute | solution.py:964
  64.3 2.8 %collective-permute-done.5.other_in = f32[3,32,256]{2,1,0:T(8,128)S(1)} collective-permute-done((f32[3,32,256]{2,1,0:T(8,128)S(1)}, f32[3,32,256]{2,1,0:T(8,128)S(1)}, u32[]{:S(2)}, u32[]{:S(2)}) %collective-permute-start.5) | collective-permute-done | bytes 98336 | tf_op jit(solution)/shard_map/ppermute | solution.py:964
  67.1 0.2 axial_filter.1
  67.3 0.1 collective-permute-start.6
  67.4 1.9 %collective-permute-start.7 = (f32[3,16,256]{2,1,0:T(8,128)S(1)}, f32[3,16,256]{2,1,0:T(8,128)S(1)}, u32[]{:S(2)}, u32[]{:S(2)}) collective-permute-start(f32[3,16,256]{2,1,0:T(8,128)S(1)} %get-tuple-element.42), channel_id=1, source_target_pairs={{0,0},{8,16},{16,8},{24,32},{32,24},{40,48},{48,40},{56,56},{1,1},... | collective-permute-start | bytes 147464 | tf_op jit(solution)/shard_map/ppermute | solution.py:964
  69.3 0.0 collective-permute-done.6.one_in
  69.3 3.5 %collective-permute-done.7.other_in = f32[3,16,256]{2,1,0:T(8,128)S(1)} collective-permute-done((f32[3,16,256]{2,1,0:T(8,128)S(1)}, f32[3,16,256]{2,1,0:T(8,128)S(1)}, u32[]{:S(2)}, u32[]{:S(2)}) %collective-permute-start.7) | collective-permute-done | bytes 49184 | tf_op jit(solution)/shard_map/ppermute | solution.py:964
  72.8 0.5 radial_filter.1
  73.3 0.9 %collective-permute-start.8 = (f32[8,128]{1,0:T(8,128)S(1)}, f32[8,128]{1,0:T(8,128)S(1)}, u32[]{:S(2)}, u32[]{:S(2)}) collective-permute-start(f32[8,128]{1,0:T(8,128)S(1)} %get-tuple-element.44), channel_id=1, source_target_pairs={{0,1},{1,0},{2,3},{3,2},{4,5},{5,4},{6,7},{7,6},{8,9},{9,8},{10,11... | collective-permute-start | bytes 12296 | tf_op jit(solution)/shard_map/ppermute | solution.py:964
  74.2 3.6 %collective-permute-start.9 = (f32[8,128]{1,0:T(8,128)S(1)}, f32[8,128]{1,0:T(8,128)S(1)}, u32[]{:S(2)}, u32[]{:S(2)}) collective-permute-start(f32[8,128]{1,0:T(8,128)S(1)} %get-tuple-element.45), channel_id=1, source_target_pairs={{0,7},{1,2},{2,1},{3,4},{4,3},{5,6},{6,5},{7,0},{8,15},{9,10},{10,... | collective-permute-start | bytes 12296 | tf_op jit(solution)/shard_map/ppermute | solution.py:964
  77.8 3.1 %collective-permute-done.8.one_in = f32[8,128]{1,0:T(8,128)S(1)} collective-permute-done((f32[8,128]{1,0:T(8,128)S(1)}, f32[8,128]{1,0:T(8,128)S(1)}, u32[]{:S(2)}, u32[]{:S(2)}) %collective-permute-start.8) | collective-permute-done | bytes 4128 | tf_op jit(solution)/shard_map/ppermute | solution.py:964
  80.9 3.0 %collective-permute-done.9.other_in = f32[8,128]{1,0:T(8,128)S(1)} collective-permute-done((f32[8,128]{1,0:T(8,128)S(1)}, f32[8,128]{1,0:T(8,128)S(1)}, u32[]{:S(2)}, u32[]{:S(2)}) %collective-permute-start.9) | collective-permute-done | bytes 4128 | tf_op jit(solution)/shard_map/ppermute | solution.py:964
  83.8 1.6 %azimuthal_filter.1 = f32[3,128,256]{2,1,0:T(8,128)} custom-call(f32[3,128,256]{2,1,0:T(8,128)S(1)} %get-tuple-element.43.cells_ref, f32[8,128]{1,0:T(8,128)S(1)} %collective-permute-done.8.one_in, f32[8,128]{1,0:T(8,128)S(1)} %collective-permute-done.9.other_in), custom_call_target="tpu_custom_call" | custom-call | tf_op jit(solution)/shard_map/azimuthal_filter/pallas_call | solution.py:948
  (8 shorter events, 0.0 us)
Async XLA Ops:
  0.6 20.7 %copy-start.2 = (s32[2,1,1,32768]{3,2,1,0:T(1,128)S(1)}, s32[2,1,1,32768]{3,2,1,0:T(1,128)}, u32[]{:S(2)}) copy-start(s32[2,1,1,32768]{3,2,1,0:T(1,128)} %param.11) | copy-start | bytes 786436
  11.5 13.8 %collective-permute-start = (f32[16,8,128]{2,1,0:T(8,128)}, f32[16,8,128]{2,1,0:T(8,128)S(1)}, u32[]{:S(2)}, u32[]{:S(2)}) collective-permute-start(f32[16,8,128]{2,1,0:T(8,128)} %get-tuple-element.31), channel_id=1, source_target_pairs={{0,1},{1,0},{2,3},{3,2},{4,5},{5,4},{6,7},{7,6},{8,9},{9,8},{10,11... | collective-permute-start | bytes 196616 | tf_op jit(solution)/shard_map/ppermute | solution.py:964
  16.2 10.8 %collective-permute-start.1 = (f32[16,8,128]{2,1,0:T(8,128)}, f32[16,8,128]{2,1,0:T(8,128)S(1)}, u32[]{:S(2)}, u32[]{:S(2)}) collective-permute-start(f32[16,8,128]{2,1,0:T(8,128)} %get-tuple-element.32), channel_id=1, source_target_pairs={{0,7},{1,2},{2,1},{3,4},{4,3},{5,6},{6,5},{7,0},{8,15},{9,10},{10,... | collective-permute-start | bytes 196616 | tf_op jit(solution)/shard_map/ppermute | solution.py:964
  25.2 1.8 %copy-start.4 = (f32[8,128]{1,0:T(8,128)S(1)}, f32[8,128]{1,0:T(8,128)}, u32[]{:S(2)}) copy-start(f32[8,128]{1,0:T(8,128)} %get-tuple-element.30.largest_ref) | copy-start | bytes 12292
  27.0 1.0 %copy-start = (s32[576,128]{1,0:T(8,128)S(1)}, s32[576,128]{1,0:T(8,128)}, u32[]{:S(2)}) copy-start(s32[576,128]{1,0:T(8,128)} %get-tuple-element.29.words_ref) | copy-start | bytes 884740
  34.2 18.8 %copy-start.1 = (f32[128,8,128]{2,1,0:T(8,128)S(1)}, f32[128,8,128]{2,1,0:T(8,128)}, u32[]{:S(2)}) copy-start(f32[128,8,128]{2,1,0:T(8,128)} %get-tuple-element.26.table_ref) | copy-start | bytes 1572868
  34.2 18.8 %collective-permute-start.2 = (f32[3,16,128]{2,1,0:T(8,128)S(1)}, f32[3,16,128]{2,1,0:T(8,128)S(1)}, u32[]{:S(2)}, u32[]{:S(2)}) collective-permute-start(f32[3,16,128]{2,1,0:T(8,128)S(1)} %get-tuple-element.34), channel_id=1, source_target_pairs={{0,1},{1,0},{2,3},{3,2},{4,5},{5,4},{6,7},{7,6},{8,9},{9,8},{10,11... | collective-permute-start | bytes 73736 | tf_op jit(solution)/shard_map/ppermute | solution.py:964
  37.1 15.9 %collective-permute-start.3 = (f32[3,16,128]{2,1,0:T(8,128)S(1)}, f32[3,16,128]{2,1,0:T(8,128)S(1)}, u32[]{:S(2)}, u32[]{:S(2)}) collective-permute-start(f32[3,16,128]{2,1,0:T(8,128)S(1)} %get-tuple-element.35), channel_id=1, source_target_pairs={{0,7},{1,2},{2,1},{3,4},{4,3},{5,6},{6,5},{7,0},{8,15},{9,10},{10,... | collective-permute-start | bytes 73736 | tf_op jit(solution)/shard_map/ppermute | solution.py:964
  43.8 9.2 %copy-start.3 = (s32[128,128]{1,0:T(8,128)S(1)}, s32[128,128]{1,0:T(8,128)}, u32[]{:S(2)}) copy-start(s32[128,128]{1,0:T(8,128)} %get-tuple-element.25.keys_ref) | copy-start | bytes 196612
  53.0 0.7 copy-start.5
  59.7 4.6 %collective-permute-start.4 = (f32[3,32,256]{2,1,0:T(8,128)S(1)}, f32[3,32,256]{2,1,0:T(8,128)S(1)}, u32[]{:S(2)}, u32[]{:S(2)}) collective-permute-start(f32[3,32,256]{2,1,0:T(8,128)S(1)} %get-tuple-element.38), channel_id=1, source_target_pairs={{0,64},{64,0},{128,192},{192,128},{1,65},{65,1},{129,193},{193,129... | collective-permute-start | bytes 294920 | tf_op jit(solution)/shard_map/ppermute | solution.py:964
  60.6 6.5 %collective-permute-start.5 = (f32[3,32,256]{2,1,0:T(8,128)S(1)}, f32[3,32,256]{2,1,0:T(8,128)S(1)}, u32[]{:S(2)}, u32[]{:S(2)}) collective-permute-start(f32[3,32,256]{2,1,0:T(8,128)S(1)} %get-tuple-element.39), channel_id=1, source_target_pairs={{0,0},{64,128},{128,64},{192,192},{1,1},{65,129},{129,65},{193,193... | collective-permute-start | bytes 294920 | tf_op jit(solution)/shard_map/ppermute | solution.py:964
  67.3 2.0 %collective-permute-start.6 = (f32[3,16,256]{2,1,0:T(8,128)S(1)}, f32[3,16,256]{2,1,0:T(8,128)S(1)}, u32[]{:S(2)}, u32[]{:S(2)}) collective-permute-start(f32[3,16,256]{2,1,0:T(8,128)S(1)} %get-tuple-element.41), channel_id=1, source_target_pairs={{0,8},{8,0},{16,24},{24,16},{32,40},{40,32},{48,56},{56,48},{1,9},... | collective-permute-start | bytes 147464 | tf_op jit(solution)/shard_map/ppermute | solution.py:964
  67.4 5.4 %collective-permute-start.7 = (f32[3,16,256]{2,1,0:T(8,128)S(1)}, f32[3,16,256]{2,1,0:T(8,128)S(1)}, u32[]{:S(2)}, u32[]{:S(2)}) collective-permute-start(f32[3,16,256]{2,1,0:T(8,128)S(1)} %get-tuple-element.42), channel_id=1, source_target_pairs={{0,0},{8,16},{16,8},{24,32},{32,24},{40,48},{48,40},{56,56},{1,1},... | collective-permute-start | bytes 147464 | tf_op jit(solution)/shard_map/ppermute | solution.py:964
  73.3 7.6 %collective-permute-start.8 = (f32[8,128]{1,0:T(8,128)S(1)}, f32[8,128]{1,0:T(8,128)S(1)}, u32[]{:S(2)}, u32[]{:S(2)}) collective-permute-start(f32[8,128]{1,0:T(8,128)S(1)} %get-tuple-element.44), channel_id=1, source_target_pairs={{0,1},{1,0},{2,3},{3,2},{4,5},{5,4},{6,7},{7,6},{8,9},{9,8},{10,11... | collective-permute-start | bytes 12296 | tf_op jit(solution)/shard_map/ppermute | solution.py:964
  74.2 9.6 %collective-permute-start.9 = (f32[8,128]{1,0:T(8,128)S(1)}, f32[8,128]{1,0:T(8,128)S(1)}, u32[]{:S(2)}, u32[]{:S(2)}) collective-permute-start(f32[8,128]{1,0:T(8,128)S(1)} %get-tuple-element.45), channel_id=1, source_target_pairs={{0,7},{1,2},{2,1},{3,4},{4,3},{5,6},{6,5},{7,0},{8,15},{9,10},{10,... | collective-permute-start | bytes 12296 | tf_op jit(solution)/shard_map/ppermute | solution.py:964

commit v3 on v2

--- a/solution.py
+++ b/solution.py
@@ -187,6 +187,11 @@
 def by_partner(axis, first, last):
     even = (lax.axis_index(axis) & 1) == 0
     return jnp.where(even, last, first), jnp.where(even, first, last)
+
+
+def neighbours(axis):
+    at, count = lax.axis_index(axis), lax.axis_size(axis)
+    return lax.rem(at + count - 1, count), lax.rem(at + 1, count)
 
 
 def from_partners(axis, one, other, wrap=False):
@@ -636,7 +641,7 @@
 
 def near_pairs_kernel(
     ends, keys_ref, words_ref, largest_ref, one_in, other_in,
-    heads_ref, one_ref, other_ref,
+    heads_ref, sent_ref,
     shell, shell_words, head_sum, tail_sum, iota, iota8, *scratch,
 ):
     shell[0:16], shell[16:32] = from_partners("az", one_in[...], other_in[...], True)
@@ -653,7 +658,8 @@
         (head_sum, tail_sum), iota, iota8, scratch,
     )
     heads_ref[...] = head_sum[:, 0:128, :]
-    one_ref[...], other_ref[...] = by_partner("az", tail_sum[:, 0:16, :], tail_sum[:, 16:32, :])
+    sent_ref[0] = tail_sum[:, 0:16, :]
+    sent_ref[1] = tail_sum[:, 16:32, :]
 
 
 def own_pairs_kernel(
@@ -701,8 +707,7 @@
         name="near_pairs",
         out_shape=(
             jax.ShapeDtypeStruct((3, 128, LANES), f32),
-            jax.ShapeDtypeStruct((3, 16, LANES), f32),
-            jax.ShapeDtypeStruct((3, 16, LANES), f32),
+            jax.ShapeDtypeStruct((2, 3, 16, LANES), f32),
         ),
         in_specs=[smem, vmem, vmem, vmem, vmem, vmem],
         scratch_shapes=[VMEM((32, ROWS, LANES), f32), VMEM((160, LANES), jnp.int32)]
@@ -796,23 +801,22 @@
     if gather:
         force_gather(gather[0], keys_ref, table_ref, total_ref, gather[1])
     if scatter:
-        for g in range(0, 16, 2):
-            bases = [ends[0, scatter[0] * 16 + n] for n in (g, g + 1)]
-            force_add([g, g + 1], bases, scatter[1], cells, iota)
+        for g in range(16):
+            force_add([g], [ends[0, scatter[0] * 16 + g]], scatter[1], cells, iota)
         force_rest(scatter[0], ends, scatter[1], cells, iota)
 
 
 def deposit_kernel(
-    ends, keys_ref, table_ref, corr_ref, one_in, other_in,
+    ends, keys_ref, table_ref, corr_ref, sent_ref,
     out_ref, total_ref, one_ref, other_ref,
     cells, iota, force_a, got_a, val_a, force_b, got_b, val_b,
 ):
     fill_iota(iota)
     cells[...] = jnp.zeros_like(cells)
     total_ref[...] = corr_ref[...]
-    before, after = from_partners("az", one_in[...], other_in[...], True)
-    total_ref[:, 0:16, :] += before
-    total_ref[:, 112:128, :] += after
+    lower, upper = neighbours("az")
+    total_ref[:, 0:16, :] += sent_ref[lower, 1]
+    total_ref[:, 112:128, :] += sent_ref[upper, 0]
     a, b = (force_a, got_a, val_a), (force_b, got_b, val_b)
     step = functools.partial(
         deposit_step, ends=ends, keys_ref=keys_ref, table_ref=table_ref, total_ref=total_ref,
@@ -840,7 +844,7 @@
             other_ref[c, :, columns] = other
 
 
-def deposits(ends, keys, table, corr, one, other):
+def deposits(ends, keys, table, corr, sent):
     f32 = jnp.float32
     smem, vmem = pl.BlockSpec(memory_space=SMEM), pl.BlockSpec(memory_space=VMEM)
     slot = [VMEM((ROWS, ROWS, LANES), f32), VMEM((16, ROWS, LANES), f32), VMEM((8, 16, LANES), f32)]
@@ -853,12 +857,12 @@
             jax.ShapeDtypeStruct((3, 32, 2 * LANES), f32),
             jax.ShapeDtypeStruct((3, 32, 2 * LANES), f32),
         ),
-        in_specs=[smem] + [vmem] * 5,
+        in_specs=[smem] + [vmem] * 4,
         scratch_shapes=[VMEM((6, 144, LANES), f32), VMEM((2 * LANES, LANES), jnp.bfloat16)]
         + slot
         + slot,
         compiler_params=params(),
-    )(ends, keys, table, corr, one, other)
+    )(ends, keys, table, corr, sent)
 
 
 def axial_kernel(taps, cells_ref, one_in, other_in, out_ref, one_ref, other_ref, first_ref, last_ref):
@@ -876,7 +880,7 @@
 
 
 def radial_kernel(
-    taps, cells_ref, one_in, other_in, out_ref, one_ref, other_ref, padded, before_ref, after_ref
+    taps, cells_ref, one_in, other_in, out_ref, edges_ref, padded, before_ref, after_ref
 ):
     lane = lax.broadcasted_iota(jnp.int32, (LANES, LANES), 1)
     edges = jnp.zeros((LANES, LANES), jnp.float32)
@@ -896,30 +900,40 @@
         right = pltpu.roll(right, 10 + 2 * c, 1)
         edges = jnp.where((lane >> 1) == c, left, edges)
         edges = jnp.where((lane >> 1) == 4 + c, right, edges)
-    turned = edges.T
-    one_ref[...], other_ref[...] = by_partner("az", turned[0:8], turned[8:16])
-
-
-def azimuthal_kernel(taps, cells_ref, one_in, other_in, out_ref):
+    edges_ref[...] = edges.T[0:16]
+
+
+def inner_azimuthal_kernel(taps, cells_ref, out_ref):
     lane = lax.broadcasted_iota(jnp.int32, (LANES, LANES), 1)
-    rest = jnp.zeros((LANES - 16, LANES), jnp.float32)
-    before, after = from_partners("az", one_in[...], other_in[...], True)
-    edges = jnp.concatenate([after, before, rest], axis=0).T
-    for c in range(3):
-        ahead = pltpu.roll(edges, LANES - 2 * c, 1) if c else edges
-        halo = jnp.where(lane < 64, ahead, pltpu.roll(edges, 118 - 2 * c, 1))
+    for c in range(3):
         left, right = cells_ref[c, :, 0:LANES], cells_ref[c, :, LANES:]
         out_left, out_right = taps[2] * left, taps[2] * right
         for k in (1, 2):
             tap = taps[2 + k]
             inner = lane < LANES - k
-            x, y, z = (pltpu.roll(v, LANES - k, 1) for v in (left, right, halo))
+            x, y = (pltpu.roll(v, LANES - k, 1) for v in (left, right))
             out_left = out_left + tap * jnp.where(inner, x, y)
-            out_right = out_right + tap * jnp.where(inner, y, z)
+            out_right = out_right + tap * jnp.where(inner, y, 0.0)
             inner = lane >= k
-            x, y, z = (pltpu.roll(v, k, 1) for v in (left, right, halo))
-            out_left = out_left + tap * jnp.where(inner, x, z)
+            x, y = (pltpu.roll(v, k, 1) for v in (left, right))
+            out_left = out_left + tap * jnp.where(inner, x, 0.0)
             out_right = out_right + tap * jnp.where(inner, y, x)
+        out_ref[c, :, 0:LANES] = out_left
+        out_ref[c, :, LANES:] = out_right
+
+
+def azimuthal_kernel(taps, inner_ref, edges_ref, out_ref):
+    lane = lax.broadcasted_iota(jnp.int32, (LANES, LANES), 1)
+    rest = jnp.zeros((LANES - 16, LANES), jnp.float32)
+    lower, upper = neighbours("az")
+    edges = jnp.concatenate([edges_ref[upper, 0:8], edges_ref[lower, 8:16], rest], axis=0).T
+    for c in range(3):
+        out_left, out_right = inner_ref[c, :, 0:LANES], inner_ref[c, :, LANES:]
+        for k in (1, 2):
+            x = pltpu.roll(edges, (118 - 2 * c + k) % LANES, 1)
+            out_left = out_left + taps[2 - k] * jnp.where(lane < k, x, 0.0)
+            y = pltpu.roll(edges, LANES - 2 * c - k, 1)
+            out_right = out_right + taps[2 + k] * jnp.where(lane >= LANES - k, y, 0.0)
         out_ref[c, :, 0:LANES] = out_left
         out_ref[c, :, LANES:] = out_right
 
@@ -930,7 +944,7 @@
     taps = [x / sum(raw) for x in raw]
     whole = jax.ShapeDtypeStruct(deposit.shape, f32)
     radial_face = jax.ShapeDtypeStruct((3, 16, 2 * LANES), f32)
-    edge = jax.ShapeDtypeStruct((8, LANES), f32)
+    edge = jax.ShapeDtypeStruct((16, LANES), f32)
     cells, one, other = pl.pallas_call(
         functools.partial(axial_kernel, taps),
         name="axial_filter",
@@ -938,19 +952,26 @@
         scratch_shapes=[VMEM((16, 2 * LANES), f32)] * 2,
         compiler_params=params(),
     )(deposit, *swapped(one, other, "ax"))
-    cells, one, other = pl.pallas_call(
+    cells, edges = pl.pallas_call(
         functools.partial(radial_kernel, taps),
         name="radial_filter",
-        out_shape=(whole, edge, edge),
+        out_shape=(whole, edge),
         scratch_shapes=[VMEM((24, 2 * LANES), f32)] + [VMEM((16, 2 * LANES), f32)] * 2,
         compiler_params=params(),
     )(cells, *swapped(one, other, "rad"))
+    edges = lax.all_gather(edges, "az")
+    inner = pl.pallas_call(
+        functools.partial(inner_azimuthal_kernel, taps),
+        name="inner_azimuthal_filter",
+        out_shape=whole,
+        compiler_params=params(),
+    )(cells)
     return pl.pallas_call(
         functools.partial(azimuthal_kernel, taps),
         name="azimuthal_filter",
         out_shape=whole,
         compiler_params=params(),
-    )(cells, *swapped(one, other, "az", True))
+    )(inner, edges)
 
 
 def swapped(one, other, axis, wrap=False):
@@ -978,10 +999,10 @@
     )
     one, other = swapped(one, other, "az", True)
     pair_keys, pair_ends = pair_sort(live, pair_list.reshape(2, 256, LANES))
-    heads, one, other = near_pairs(pair_ends, pair_keys, words, largest, one, other)
-    one, other = swapped(one, other, "az", True)
+    heads, sent = near_pairs(pair_ends, pair_keys, words, largest, one, other)
+    sent = lax.all_gather(sent, "az")
     corr = own_pairs(live, pair_ends, pair_keys, words, largest, heads)
-    deposit, correction, one, other = deposits(cell_ends, cell_keys, table, corr, one, other)
+    deposit, correction, one, other = deposits(cell_ends, cell_keys, table, corr, sent)
     smoothed = filtered(deposit, one, other)
     return (correction.reshape(positions.shape), smoothed.reshape(gas_velocity.shape))
 

time: 86.3 us -> 158 us (1.83); the launches traced: 85.5 us -> 159 us
  blocking collectives: 0 us -> 88.8 us
  starting transfers between devices: 28.2 us -> 19 us
  waiting for transfers between devices: 15.8 us -> 10.7 us
    all_gather x0 -> x2, blocking collectives: none -> 88.8 us  [the longest x1 44.9 us: per_device(): sent = lax.all_gather(sent, 'az')]
    ppermute x10 -> x6, starting transfers between devices: 28.2 us -> 19 us  [swapped(): lax.ppermute(x, axis, [(i, partner(i, odd)) for i in range(count)])]
    ppermute x10 -> x6, waiting for transfers between devices: 15.8 us -> 10.7 us  [swapped(): lax.ppermute(x, axis, [(i, partner(i, odd)) for i in range(count)])]
  transfers between devices with their start and end apart: 10 -> 6, of which waited for: 6 -> 4; matrix products, arithmetic and copies ran while one was open for 0% -> 0% of each run, Pallas kernels for 15% -> 2%
where the time goes in v3:
time: 158 us; the launch traced here: 159 us
  blocking collectives  88.8 us (56%)
  Pallas kernels  37.2 us (24%)
  starting transfers between devices  19 us (12%)
  waiting for transfers between devices  10.7 us (7%)
  local copies, waits for them, and re-layouts  1.63 us (1%)
    all_gather x1, blocking collectives, per_device(): sent = lax.all_gather(sent, 'az')  44.9 us
    all_gather x1, blocking collectives, filtered(): edges = lax.all_gather(edges, 'az')  43.8 us
    ppermute x6, starting transfers between devices, swapped(): lax.ppermute(x, axis, [(i, partner(i, odd)) for i in range(count)])  19 us
    pallas_call x1, Pallas kernels, droplet_states(): pl.pallas_call(states_kernel, name='droplet_states', out_shape=(jax.Shape...  10.7 us
    ppermute x6, waiting for transfers between devices, swapped(): lax.ppermute(x, axis, [(i, partner(i, odd)) for i in range(count)])  10.7 us
    pallas_call x1, Pallas kernels, own_pairs(): pl.pallas_call(own_pairs_kernel, name='own_pairs', out_shape=jax.ShapeDty...  8 us
    pallas_call x1, Pallas kernels, near_pairs(): pl.pallas_call(near_pairs_kernel, name='near_pairs', out_shape=(jax.Shape...  6.63 us
    pallas_call x1, Pallas kernels, deposits(): pl.pallas_call(deposit_kernel, name='deposits', out_shape=(jax.ShapeDtype...  5.66 us
  transfers between devices with their start and end apart: 6, of which 4 were waited for; matrix products, arithmetic and copies ran while one was open for 0% of the time, Pallas kernels for 2%

profile of v3, /device:TPU:40, one launch (start us, length us, event | category | flops | bytes accessed | tf_op | source)
XLA Modules:
  0.0 158.8 jit_solution(14419136039102861433)
XLA Ops:
  0.6 0.0 copy-start.2
  0.6 10.7 %droplet_states.1 = (s32[128,128]{1,0:T(8,128)}, s32[8,128]{1,0:T(8,128)}, f32[128,8,128]{2,1,0:T(8,128)}, s32[576,128]{1,0:T(8,128)}, f32[8,128]{1,0:T(8,128)},...) custom-call(s32[128,128]{1,0:T(8,128)} %bitcast.20, f32[3,128,256]{2,1,0:T(8,128)} %bitcast.16, f32[3,128,128]{2,1,0:T(8,128)} %bitcast.18, ...), custom_call_target="tpu_custom_call" | custom-call | tf_op jit(solution)/shard_map/droplet_states/pallas_call | solution.py:421
  11.4 5.3 %collective-permute-start = (f32[16,8,128]{2,1,0:T(8,128)}, f32[16,8,128]{2,1,0:T(8,128)S(1)}, u32[]{:S(2)}, u32[]{:S(2)}) collective-permute-start(f32[16,8,128]{2,1,0:T(8,128)} %get-tuple-element.29), channel_id=1, source_target_pairs={{0,1},{1,0},{2,3},{3,2},{4,5},{5,4},{6,7},{7,6},{8,9},{9,8},{10,11... | collective-permute-start | bytes 196616 | tf_op jit(solution)/shard_map/ppermute | solution.py:985
  16.7 3.4 %collective-permute-start.1 = (f32[16,8,128]{2,1,0:T(8,128)}, f32[16,8,128]{2,1,0:T(8,128)S(1)}, u32[]{:S(2)}, u32[]{:S(2)}) collective-permute-start(f32[16,8,128]{2,1,0:T(8,128)} %get-tuple-element.30), channel_id=1, source_target_pairs={{0,7},{1,2},{2,1},{3,4},{4,3},{5,6},{6,5},{7,0},{8,15},{9,10},{10,... | collective-permute-start | bytes 196616 | tf_op jit(solution)/shard_map/ppermute | solution.py:985
  20.8 0.0 copy-done.2
  20.8 3.9 %pair_sort.1 = (s32[2,128,128]{2,1,0:T(8,128)S(1)}, s32[16,128]{1,0:T(8,128)S(1)}) custom-call(s32[1,1]{1,0:T(1,128)} %bitcast.11.live_ref, s32[2,256,128]{2,1,0:T(8,128)S(1)} %bitcast.14), custom_call_target="tpu_custom_call" | custom-call | tf_op jit(solution)/shard_map/pair_sort/pallas_call | solution.py:495
  24.6 0.0 copy-start.4
  24.7 0.0 collective-permute-done.one_in
  24.7 2.7 %collective-permute-done.1.other_in = f32[16,8,128]{2,1,0:T(8,128)S(1)} collective-permute-done((f32[16,8,128]{2,1,0:T(8,128)}, f32[16,8,128]{2,1,0:T(8,128)S(1)}, u32[]{:S(2)}, u32[]{:S(2)}) %collective-permute-start.1) | collective-permute-done | bytes 65568 | tf_op jit(solution)/shard_map/ppermute | solution.py:985
  27.3 0.0 copy-done.4
  27.3 1.0 copy-done
  28.3 6.6 %near_pairs.1 = (f32[3,128,128]{2,1,0:T(8,128)S(1)}, f32[2,3,16,128]{3,2,1,0:T(8,128)S(1)}) custom-call(s32[16,128]{1,0:T(8,128)S(1)} %get-tuple-element.25.ends, s32[2,128,128]{2,1,0:T(8,128)S(1)} %get-tuple-element.26.keys_ref, s32[576,128]{1,0:T(8,128)S(1)} %copy-done, f32[8,128]{1,0:T(8,128)S(1)} %copy-done.4, ...), custom_call_target="tpu_custom_call" | custom-call | tf_op jit(solution)/shard_map/near_pairs/pallas_call | solution.py:705
  34.9 44.9 %all-gather = f32[16,3,16,128]{3,2,1,0:T(8,128)S(1)} all-gather(f32[2,3,16,128]{3,2,1,0:T(8,128)S(1)} %get-tuple-element.32), channel_id=2, replica_groups=mesh['ax'=4,'rad'=8,'az'=8] {'az'}, dimensions={0}, use_global_device_ids=true | all-gather | bytes 442368 | tf_op jit(solution)/shard_map/all_gather | solution.py:1003
  79.9 8.0 %own_pairs.1.corr_ref = f32[3,128,128]{2,1,0:T(8,128)S(1)} custom-call(s32[1,1]{1,0:T(1,128)} %bitcast.12.live_ref, s32[16,128]{1,0:T(8,128)S(1)} %get-tuple-element.25.ends, s32[2,128,128]{2,1,0:T(8,128)S(1)} %get-tuple-element.26.keys_ref, s32[576,128]{1,0:T(8,128)S(1)} %copy-done, f32[8,128]{1,0:T(8,128)S(1)} %copy-done.4, ...), custom_call_target="tpu_custom_call" | custom-call | tf_op jit(solution)/shard_map/own_pairs/pallas_call | solution.py:721
  87.9 0.0 copy-start.5
  87.9 0.0 copy-done.1
  87.9 0.0 copy-done.3
  87.9 0.6 copy-done.5
  88.5 5.7 %deposits.1 = (f32[3,128,256]{2,1,0:T(8,128)S(1)}, f32[3,128,128]{2,1,0:T(8,128)}, f32[3,32,256]{2,1,0:T(8,128)S(1)}, f32[3,32,256]{2,1,0:T(8,128)S(1)}) custom-call(s32[8,128]{1,0:T(8,128)S(1)} %copy-done.5, s32[128,128]{1,0:T(8,128)S(1)} %copy-done.3, f32[128,8,128]{2,1,0:T(8,128)S(1)} %copy-done.1, f32[3,128,128]{2,1,0:T(8,128)S(1)} %own_pairs.1.corr_ref, ...), custom_call_target="tpu_custom_call" | custom-call | tf_op jit(solution)/shard_map/deposits/pallas_call | solution.py:851
  94.2 6.4 %collective-permute-start.2 = (f32[3,32,256]{2,1,0:T(8,128)S(1)}, f32[3,32,256]{2,1,0:T(8,128)S(1)}, u32[]{:S(2)}, u32[]{:S(2)}) collective-permute-start(f32[3,32,256]{2,1,0:T(8,128)S(1)} %get-tuple-element.35), channel_id=1, source_target_pairs={{0,64},{64,0},{128,192},{192,128},{1,65},{65,1},{129,193},{193,129... | collective-permute-start | bytes 294920 | tf_op jit(solution)/shard_map/ppermute | solution.py:985
  100.6 1.9 %collective-permute-start.3 = (f32[3,32,256]{2,1,0:T(8,128)S(1)}, f32[3,32,256]{2,1,0:T(8,128)S(1)}, u32[]{:S(2)}, u32[]{:S(2)}) collective-permute-start(f32[3,32,256]{2,1,0:T(8,128)S(1)} %get-tuple-element.36), channel_id=1, source_target_pairs={{0,0},{64,128},{128,64},{192,192},{1,1},{65,129},{129,65},{193,193... | collective-permute-start | bytes 294920 | tf_op jit(solution)/shard_map/ppermute | solution.py:985
  102.5 0.7 collective-permute-done.2.one_in
  103.2 3.9 %collective-permute-done.3.other_in = f32[3,32,256]{2,1,0:T(8,128)S(1)} collective-permute-done((f32[3,32,256]{2,1,0:T(8,128)S(1)}, f32[3,32,256]{2,1,0:T(8,128)S(1)}, u32[]{:S(2)}, u32[]{:S(2)}) %collective-permute-start.3) | collective-permute-done | bytes 98336 | tf_op jit(solution)/shard_map/ppermute | solution.py:985
  107.1 0.2 axial_filter.1
  107.3 0.1 collective-permute-start.4
  107.4 1.9 %collective-permute-start.5 = (f32[3,16,256]{2,1,0:T(8,128)S(1)}, f32[3,16,256]{2,1,0:T(8,128)S(1)}, u32[]{:S(2)}, u32[]{:S(2)}) collective-permute-start(f32[3,16,256]{2,1,0:T(8,128)S(1)} %get-tuple-element.39), channel_id=1, source_target_pairs={{0,0},{8,16},{16,8},{24,32},{32,24},{40,48},{48,40},{56,56},{1,1},... | collective-permute-start | bytes 147464 | tf_op jit(solution)/shard_map/ppermute | solution.py:985
  109.3 0.0 collective-permute-done.4.one_in
  109.3 3.5 %collective-permute-done.5.other_in = f32[3,16,256]{2,1,0:T(8,128)S(1)} collective-permute-done((f32[3,16,256]{2,1,0:T(8,128)S(1)}, f32[3,16,256]{2,1,0:T(8,128)S(1)}, u32[]{:S(2)}, u32[]{:S(2)}) %collective-permute-start.5) | collective-permute-done | bytes 49184 | tf_op jit(solution)/shard_map/ppermute | solution.py:985
  112.8 0.5 radial_filter.1
  113.3 0.5 inner_azimuthal_filter.1.inner_ref
  113.8 43.8 %all-gather.1 = f32[128,128]{1,0:T(8,128)S(1)} all-gather(f32[16,128]{1,0:T(8,128)S(1)} %get-tuple-element.41), channel_id=3, replica_groups=mesh['ax'=4,'rad'=8,'az'=8] {'az'}, dimensions={0}, use_global_device_ids=true | all-gather | bytes 73728 | tf_op jit(solution)/shard_map/all_gather | solution.py:962
  157.7 1.1 azimuthal_filter.1
  (3 shorter events, 0.0 us)
Async XLA Ops:
  0.6 20.1 %copy-start.2 = (s32[2,1,1,32768]{3,2,1,0:T(1,128)S(1)}, s32[2,1,1,32768]{3,2,1,0:T(1,128)}, u32[]{:S(2)}) copy-start(s32[2,1,1,32768]{3,2,1,0:T(1,128)} %param.11) | copy-start | bytes 786436
  11.4 13.3 %collective-permute-start = (f32[16,8,128]{2,1,0:T(8,128)}, f32[16,8,128]{2,1,0:T(8,128)S(1)}, u32[]{:S(2)}, u32[]{:S(2)}) collective-permute-start(f32[16,8,128]{2,1,0:T(8,128)} %get-tuple-element.29), channel_id=1, source_target_pairs={{0,1},{1,0},{2,3},{3,2},{4,5},{5,4},{6,7},{7,6},{8,9},{9,8},{10,11... | collective-permute-start | bytes 196616 | tf_op jit(solution)/shard_map/ppermute | solution.py:985
  16.7 10.6 %collective-permute-start.1 = (f32[16,8,128]{2,1,0:T(8,128)}, f32[16,8,128]{2,1,0:T(8,128)S(1)}, u32[]{:S(2)}, u32[]{:S(2)}) collective-permute-start(f32[16,8,128]{2,1,0:T(8,128)} %get-tuple-element.30), channel_id=1, source_target_pairs={{0,7},{1,2},{2,1},{3,4},{4,3},{5,6},{6,5},{7,0},{8,15},{9,10},{10,... | collective-permute-start | bytes 196616 | tf_op jit(solution)/shard_map/ppermute | solution.py:985
  24.6 2.7 %copy-start.4 = (f32[8,128]{1,0:T(8,128)S(1)}, f32[8,128]{1,0:T(8,128)}, u32[]{:S(2)}) copy-start(f32[8,128]{1,0:T(8,128)} %get-tuple-element.28.largest_ref) | copy-start | bytes 12292
  27.3 1.0 copy-start
  79.9 8.0 %copy-start.1 = (f32[128,8,128]{2,1,0:T(8,128)S(1)}, f32[128,8,128]{2,1,0:T(8,128)}, u32[]{:S(2)}) copy-start(f32[128,8,128]{2,1,0:T(8,128)} %get-tuple-element.24.table_ref) | copy-start | bytes 1572868
  79.9 8.0 %copy-start.3 = (s32[128,128]{1,0:T(8,128)S(1)}, s32[128,128]{1,0:T(8,128)}, u32[]{:S(2)}) copy-start(s32[128,128]{1,0:T(8,128)} %get-tuple-element.23.keys_ref) | copy-start | bytes 196612
  87.9 0.7 copy-start.5
  94.2 9.0 %collective-permute-start.2 = (f32[3,32,256]{2,1,0:T(8,128)S(1)}, f32[3,32,256]{2,1,0:T(8,128)S(1)}, u32[]{:S(2)}, u32[]{:S(2)}) collective-permute-start(f32[3,32,256]{2,1,0:T(8,128)S(1)} %get-tuple-element.35), channel_id=1, source_target_pairs={{0,64},{64,0},{128,192},{192,128},{1,65},{65,1},{129,193},{193,129... | collective-permute-start | bytes 294920 | tf_op jit(solution)/shard_map/ppermute | solution.py:985
  100.6 6.5 %collective-permute-start.3 = (f32[3,32,256]{2,1,0:T(8,128)S(1)}, f32[3,32,256]{2,1,0:T(8,128)S(1)}, u32[]{:S(2)}, u32[]{:S(2)}) collective-permute-start(f32[3,32,256]{2,1,0:T(8,128)S(1)} %get-tuple-element.36), channel_id=1, source_target_pairs={{0,0},{64,128},{128,64},{192,192},{1,1},{65,129},{129,65},{193,193... | collective-permute-start | bytes 294920 | tf_op jit(solution)/shard_map/ppermute | solution.py:985
  107.3 2.0 %collective-permute-start.4 = (f32[3,16,256]{2,1,0:T(8,128)S(1)}, f32[3,16,256]{2,1,0:T(8,128)S(1)}, u32[]{:S(2)}, u32[]{:S(2)}) collective-permute-start(f32[3,16,256]{2,1,0:T(8,128)S(1)} %get-tuple-element.38), channel_id=1, source_target_pairs={{0,8},{8,0},{16,24},{24,16},{32,40},{40,32},{48,56},{56,48},{1,9},... | collective-permute-start | bytes 147464 | tf_op jit(solution)/shard_map/ppermute | solution.py:985
  107.4 5.4 %collective-permute-start.5 = (f32[3,16,256]{2,1,0:T(8,128)S(1)}, f32[3,16,256]{2,1,0:T(8,128)S(1)}, u32[]{:S(2)}, u32[]{:S(2)}) collective-permute-start(f32[3,16,256]{2,1,0:T(8,128)S(1)} %get-tuple-element.39), channel_id=1, source_target_pairs={{0,0},{8,16},{16,8},{24,32},{32,24},{40,48},{48,40},{56,56},{1,1},... | collective-permute-start | bytes 147464 | tf_op jit(solution)/shard_map/ppermute | solution.py:985

commit v4 on v2

--- a/solution.py
+++ b/solution.py
@@ -14,7 +14,7 @@
 LANES = 128
 ROWS = 8
 BLOCK = 2048
-GAS_WINDOW = 10
+GAS_WINDOW = 12
 BUCKET = 1024
 BUCKETS = 20
 NEAR_BUCKETS = 4
@@ -430,8 +430,8 @@
         + [VMEM((144, ROWS, LANES), f32), VMEM((LANES, LANES), jnp.bfloat16), SMEM((ROWS, LANES), i32)]
         + slots(16, 11)
         + [pltpu.SemaphoreType.DMA((6,))],
-        compiler_params=params(60),
-    )(*arrays)
+        compiler_params=params(),
+    )(*[pltpu.with_memory_space_constraint(x, pltpu.HBM) for x in arrays])
 
 
 def pair_sort_kernel(live_ref, pairs_ref, keys_ref, ends_ref):
@@ -796,9 +796,8 @@
     if gather:
         force_gather(gather[0], keys_ref, table_ref, total_ref, gather[1])
     if scatter:
-        for g in range(0, 16, 2):
-            bases = [ends[0, scatter[0] * 16 + n] for n in (g, g + 1)]
-            force_add([g, g + 1], bases, scatter[1], cells, iota)
+        for g in range(16):
+            force_add([g], [ends[0, scatter[0] * 16 + g]], scatter[1], cells, iota)
         force_rest(scatter[0], ends, scatter[1], cells, iota)
 
 
@@ -900,26 +899,37 @@
     one_ref[...], other_ref[...] = by_partner("az", turned[0:8], turned[8:16])
 
 
-def azimuthal_kernel(taps, cells_ref, one_in, other_in, out_ref):
+def inner_azimuthal_kernel(taps, cells_ref, out_ref):
     lane = lax.broadcasted_iota(jnp.int32, (LANES, LANES), 1)
-    rest = jnp.zeros((LANES - 16, LANES), jnp.float32)
-    before, after = from_partners("az", one_in[...], other_in[...], True)
-    edges = jnp.concatenate([after, before, rest], axis=0).T
-    for c in range(3):
-        ahead = pltpu.roll(edges, LANES - 2 * c, 1) if c else edges
-        halo = jnp.where(lane < 64, ahead, pltpu.roll(edges, 118 - 2 * c, 1))
+    for c in range(3):
         left, right = cells_ref[c, :, 0:LANES], cells_ref[c, :, LANES:]
         out_left, out_right = taps[2] * left, taps[2] * right
         for k in (1, 2):
             tap = taps[2 + k]
             inner = lane < LANES - k
-            x, y, z = (pltpu.roll(v, LANES - k, 1) for v in (left, right, halo))
+            x, y = (pltpu.roll(v, LANES - k, 1) for v in (left, right))
             out_left = out_left + tap * jnp.where(inner, x, y)
-            out_right = out_right + tap * jnp.where(inner, y, z)
+            out_right = out_right + tap * jnp.where(inner, y, 0.0)
             inner = lane >= k
-            x, y, z = (pltpu.roll(v, k, 1) for v in (left, right, halo))
-            out_left = out_left + tap * jnp.where(inner, x, z)
+            x, y = (pltpu.roll(v, k, 1) for v in (left, right))
+            out_left = out_left + tap * jnp.where(inner, x, 0.0)
             out_right = out_right + tap * jnp.where(inner, y, x)
+        out_ref[c, :, 0:LANES] = out_left
+        out_ref[c, :, LANES:] = out_right
+
+
+def azimuthal_kernel(taps, inner_ref, one_in, other_in, out_ref):
+    lane = lax.broadcasted_iota(jnp.int32, (LANES, LANES), 1)
+    rest = jnp.zeros((LANES - 16, LANES), jnp.float32)
+    before, after = from_partners("az", one_in[...], other_in[...], True)
+    edges = jnp.concatenate([after, before, rest], axis=0).T
+    for c in range(3):
+        out_left, out_right = inner_ref[c, :, 0:LANES], inner_ref[c, :, LANES:]
+        for k in (1, 2):
+            x = pltpu.roll(edges, (118 - 2 * c + k) % LANES, 1)
+            out_left = out_left + taps[2 - k] * jnp.where(lane < k, x, 0.0)
+            y = pltpu.roll(edges, LANES - 2 * c - k, 1)
+            out_right = out_right + taps[2 + k] * jnp.where(lane >= LANES - k, y, 0.0)
         out_ref[c, :, 0:LANES] = out_left
         out_ref[c, :, LANES:] = out_right
 
@@ -945,12 +955,19 @@
         scratch_shapes=[VMEM((24, 2 * LANES), f32)] + [VMEM((16, 2 * LANES), f32)] * 2,
         compiler_params=params(),
     )(cells, *swapped(one, other, "rad"))
+    one, other = swapped(one, other, "az", True)
+    inner = pl.pallas_call(
+        functools.partial(inner_azimuthal_kernel, taps),
+        name="inner_azimuthal_filter",
+        out_shape=whole,
+        compiler_params=params(),
+    )(cells)
     return pl.pallas_call(
         functools.partial(azimuthal_kernel, taps),
         name="azimuthal_filter",
         out_shape=whole,
         compiler_params=params(),
-    )(cells, *swapped(one, other, "az", True))
+    )(inner, one, other)
 
 
 def swapped(one, other, axis, wrap=False):

time: 86.3 us -> 81 us (0.939)
  Pallas kernels: 38.4 us -> 36.2 us
  waiting for transfers between devices: 15.8 us -> 13.8 us
  local copies, waits for them, and re-layouts: 1.62 us -> 0.01 us
    pallas_call x1, Pallas kernels: 10.8 us -> 8.53 us  [droplet_states(): pl.pallas_call(states_kernel, name='droplet_states', out_shape=(jax.Shape...]
    ppermute x10, waiting for transfers between devices: 15.8 us -> 13.8 us  [swapped(): lax.ppermute(x, axis, [(i, partner(i, odd)) for i in range(count)])]
    unnamed x12 -> x2, local copies, waits for them, and re-layouts: 1.62 us -> 0.01 us
  transfers between devices with their start and end apart: 10 -> 10, of which waited for: 6 -> 5; matrix products, arithmetic and copies ran while one was open for 0% -> 0% of each run, Pallas kernels for 15% -> 16%
where the time goes in v4:
time: 81 us; the launch traced here: 80.2 us
  Pallas kernels  36.2 us (45%)
  starting transfers between devices  28.7 us (35%)
  waiting for transfers between devices  13.8 us (17%)
  between operations  1.41 us (2%)
    ppermute x10, starting transfers between devices, swapped(): lax.ppermute(x, axis, [(i, partner(i, odd)) for i in range(count)])  28.7 us
    ppermute x10, waiting for transfers between devices, swapped(): lax.ppermute(x, axis, [(i, partner(i, odd)) for i in range(count)])  13.8 us
    pallas_call x1, Pallas kernels, own_pairs(): pl.pallas_call(own_pairs_kernel, name='own_pairs', out_shape=jax.ShapeDty...  8.88 us
    pallas_call x1, Pallas kernels, droplet_states(): pl.pallas_call(states_kernel, name='droplet_states', out_shape=(jax.Shape...  8.53 us
    pallas_call x1, Pallas kernels, near_pairs(): pl.pallas_call(near_pairs_kernel, name='near_pairs', out_shape=(jax.Shape...  6.98 us
    pallas_call x1, Pallas kernels, deposits(): pl.pallas_call(deposit_kernel, name='deposits', out_shape=(jax.ShapeDtype...  5.67 us
    pallas_call x1, Pallas kernels, pair_sort(): pl.pallas_call(pair_sort_kernel, name='pair_sort', out_shape=(jax.ShapeDt...  3.85 us
  transfers between devices with their start and end apart: 10, of which 5 were waited for; matrix products, arithmetic and copies ran while one was open for 0% of the time, Pallas kernels for 16%

profile of v4, /device:TPU:40, one launch (start us, length us, event | category | flops | bytes accessed | tf_op | source)
XLA Modules:
  0.0 80.2 jit_solution(13748405157417385729)
XLA Ops:
  0.6 0.0 copy-start
  0.6 8.5 %droplet_states.1 = (s32[128,128]{1,0:T(8,128)S(1)}, s32[8,128]{1,0:T(8,128)S(1)}, f32[128,8,128]{2,1,0:T(8,128)S(1)}, s32[576,128]{1,0:T(8,128)S(1)}, f32[8,128...) custom-call(s32[128,128]{1,0:T(8,128)} %bitcast.16, f32[3,128,256]{2,1,0:T(8,128)} %bitcast.12, ...), custom_call_target="tpu_custom_call" | custom-call | tf_op jit(solution)/shard_map/droplet_states/pallas_call | solution.py:416
  9.2 6.4 %collective-permute-start = (f32[16,8,128]{2,1,0:T(8,128)S(1)}, f32[16,8,128]{2,1,0:T(8,128)S(1)}, u32[]{:S(2)}, u32[]{:S(2)}) collective-permute-start(f32[16,8,128]{2,1,0:T(8,128)S(1)} %get-tuple-element.31), channel_id=1, source_target_pairs={{0,1},{1,0},{2,3},{3,2},{4,5},{5,4},{6,7},{7,6},{8,9},{9,8},{10,11... | collective-permute-start | bytes 196616 | tf_op jit(solution)/shard_map/ppermute | solution.py:981
  15.5 2.3 %collective-permute-start.1 = (f32[16,8,128]{2,1,0:T(8,128)S(1)}, f32[16,8,128]{2,1,0:T(8,128)S(1)}, u32[]{:S(2)}, u32[]{:S(2)}) collective-permute-start(f32[16,8,128]{2,1,0:T(8,128)S(1)} %get-tuple-element.32), channel_id=1, source_target_pairs={{0,7},{1,2},{2,1},{3,4},{4,3},{5,6},{6,5},{7,0},{8,15},{9,10},{10,... | collective-permute-start | bytes 196616 | tf_op jit(solution)/shard_map/ppermute | solution.py:981
  18.5 0.0 copy-done
  18.5 3.9 %pair_sort.1 = (s32[2,128,128]{2,1,0:T(8,128)S(1)}, s32[16,128]{1,0:T(8,128)S(1)}) custom-call(s32[1,1]{1,0:T(1,128)} %bitcast.9.live_ref, s32[2,256,128]{2,1,0:T(8,128)S(1)} %bitcast.11), custom_call_target="tpu_custom_call" | custom-call | tf_op jit(solution)/shard_map/pair_sort/pallas_call | solution.py:490
  22.4 0.0 collective-permute-done.one_in
  22.4 4.6 %collective-permute-done.1.other_in = f32[16,8,128]{2,1,0:T(8,128)S(1)} collective-permute-done((f32[16,8,128]{2,1,0:T(8,128)S(1)}, f32[16,8,128]{2,1,0:T(8,128)S(1)}, u32[]{:S(2)}, u32[]{:S(2)}) %collective-permute-start.1) | collective-permute-done | bytes 65568 | tf_op jit(solution)/shard_map/ppermute | solution.py:981
  27.0 7.0 %near_pairs.1 = (f32[3,128,128]{2,1,0:T(8,128)S(1)}, f32[3,16,128]{2,1,0:T(8,128)S(1)}, f32[3,16,128]{2,1,0:T(8,128)S(1)}) custom-call(s32[16,128]{1,0:T(8,128)S(1)} %get-tuple-element.27.ends, s32[2,128,128]{2,1,0:T(8,128)S(1)} %get-tuple-element.28.keys_ref, s32[576,128]{1,0:T(8,128)S(1)} %get-tuple-element.29.words_ref, ...), custom_call_target="tpu_custom_call" | custom-call | tf_op jit(solution)/shard_map/near_pairs/pallas_call | solution.py:699
  34.0 1.2 %collective-permute-start.2 = (f32[3,16,128]{2,1,0:T(8,128)S(1)}, f32[3,16,128]{2,1,0:T(8,128)S(1)}, u32[]{:S(2)}, u32[]{:S(2)}) collective-permute-start(f32[3,16,128]{2,1,0:T(8,128)S(1)} %get-tuple-element.34), channel_id=1, source_target_pairs={{0,1},{1,0},{2,3},{3,2},{4,5},{5,4},{6,7},{7,6},{8,9},{9,8},{10,11... | collective-permute-start | bytes 73736 | tf_op jit(solution)/shard_map/ppermute | solution.py:981
  35.2 4.1 %collective-permute-start.3 = (f32[3,16,128]{2,1,0:T(8,128)S(1)}, f32[3,16,128]{2,1,0:T(8,128)S(1)}, u32[]{:S(2)}, u32[]{:S(2)}) collective-permute-start(f32[3,16,128]{2,1,0:T(8,128)S(1)} %get-tuple-element.35), channel_id=1, source_target_pairs={{0,7},{1,2},{2,1},{3,4},{4,3},{5,6},{6,5},{7,0},{8,15},{9,10},{10,... | collective-permute-start | bytes 73736 | tf_op jit(solution)/shard_map/ppermute | solution.py:981
  39.2 8.9 %own_pairs.1.corr_ref = f32[3,128,128]{2,1,0:T(8,128)S(1)} custom-call(s32[1,1]{1,0:T(1,128)} %bitcast.10.live_ref, s32[16,128]{1,0:T(8,128)S(1)} %get-tuple-element.27.ends, s32[2,128,128]{2,1,0:T(8,128)S(1)} %get-tuple-element.28.keys_ref, s32[576,128]{1,0:T(8,128)S(1)} %get-tuple-element.29.words_ref, f32[8,128]{1,0:T(8,128)S(1)} %get-tuple-element.30.largest_ref, ...), custom_call_target="tpu_custom_call" | custom-call | tf_op jit(solution)/shard_map/own_pairs/pallas_call | solution.py:716
  48.1 0.0 collective-permute-done.2.one_in
  48.1 0.0 collective-permute-done.3.other_in
  48.2 5.7 %deposits.1 = (f32[3,128,256]{2,1,0:T(8,128)S(1)}, f32[3,128,128]{2,1,0:T(8,128)}, f32[3,32,256]{2,1,0:T(8,128)S(1)}, f32[3,32,256]{2,1,0:T(8,128)S(1)}) custom-call(s32[8,128]{1,0:T(8,128)S(1)} %get-tuple-element.24.ends, s32[128,128]{1,0:T(8,128)S(1)} %get-tuple-element.25.keys_ref, f32[128,8,128]{2,1,0:T(8,128)S(1)} %get-tuple-element.26.table_ref, ...), custom_call_target="tpu_custom_call" | custom-call | tf_op jit(solution)/shard_map/deposits/pallas_call | solution.py:846
  53.8 0.0 collective-permute-start.4
  53.8 3.5 %collective-permute-start.5 = (f32[3,32,256]{2,1,0:T(8,128)S(1)}, f32[3,32,256]{2,1,0:T(8,128)S(1)}, u32[]{:S(2)}, u32[]{:S(2)}) collective-permute-start(f32[3,32,256]{2,1,0:T(8,128)S(1)} %get-tuple-element.39), channel_id=1, source_target_pairs={{0,0},{64,128},{128,64},{192,192},{1,1},{65,129},{129,65},{193,193... | collective-permute-start | bytes 294920 | tf_op jit(solution)/shard_map/ppermute | solution.py:981
  57.4 1.1 %collective-permute-done.4.one_in = f32[3,32,256]{2,1,0:T(8,128)S(1)} collective-permute-done((f32[3,32,256]{2,1,0:T(8,128)S(1)}, f32[3,32,256]{2,1,0:T(8,128)S(1)}, u32[]{:S(2)}, u32[]{:S(2)}) %collective-permute-start.4) | collective-permute-done | bytes 98336 | tf_op jit(solution)/shard_map/ppermute | solution.py:981
  58.4 1.9 %collective-permute-done.5.other_in = f32[3,32,256]{2,1,0:T(8,128)S(1)} collective-permute-done((f32[3,32,256]{2,1,0:T(8,128)S(1)}, f32[3,32,256]{2,1,0:T(8,128)S(1)}, u32[]{:S(2)}, u32[]{:S(2)}) %collective-permute-start.5) | collective-permute-done | bytes 98336 | tf_op jit(solution)/shard_map/ppermute | solution.py:981
  60.3 0.2 axial_filter.1
  60.5 0.1 collective-permute-start.6
  60.6 4.0 %collective-permute-start.7 = (f32[3,16,256]{2,1,0:T(8,128)S(1)}, f32[3,16,256]{2,1,0:T(8,128)S(1)}, u32[]{:S(2)}, u32[]{:S(2)}) collective-permute-start(f32[3,16,256]{2,1,0:T(8,128)S(1)} %get-tuple-element.42), channel_id=1, source_target_pairs={{0,0},{8,16},{16,8},{24,32},{32,24},{40,48},{48,40},{56,56},{1,1},... | collective-permute-start | bytes 147464 | tf_op jit(solution)/shard_map/ppermute | solution.py:981
  64.7 0.0 collective-permute-done.6.one_in
  64.7 1.7 %collective-permute-done.7.other_in = f32[3,16,256]{2,1,0:T(8,128)S(1)} collective-permute-done((f32[3,16,256]{2,1,0:T(8,128)S(1)}, f32[3,16,256]{2,1,0:T(8,128)S(1)}, u32[]{:S(2)}, u32[]{:S(2)}) %collective-permute-start.7) | collective-permute-done | bytes 49184 | tf_op jit(solution)/shard_map/ppermute | solution.py:981
  66.4 0.5 radial_filter.1
  66.9 2.5 %collective-permute-start.8 = (f32[8,128]{1,0:T(8,128)S(1)}, f32[8,128]{1,0:T(8,128)S(1)}, u32[]{:S(2)}, u32[]{:S(2)}) collective-permute-start(f32[8,128]{1,0:T(8,128)S(1)} %get-tuple-element.44), channel_id=1, source_target_pairs={{0,1},{1,0},{2,3},{3,2},{4,5},{5,4},{6,7},{7,6},{8,9},{9,8},{10,11... | collective-permute-start | bytes 12296 | tf_op jit(solution)/shard_map/ppermute | solution.py:981
  69.4 4.7 %collective-permute-start.9 = (f32[8,128]{1,0:T(8,128)S(1)}, f32[8,128]{1,0:T(8,128)S(1)}, u32[]{:S(2)}, u32[]{:S(2)}) collective-permute-start(f32[8,128]{1,0:T(8,128)S(1)} %get-tuple-element.45), channel_id=1, source_target_pairs={{0,7},{1,2},{2,1},{3,4},{4,3},{5,6},{6,5},{7,0},{8,15},{9,10},{10,... | collective-permute-start | bytes 12296 | tf_op jit(solution)/shard_map/ppermute | solution.py:981
  74.1 0.5 inner_azimuthal_filter.1.inner_ref
  74.6 0.0 collective-permute-done.8.one_in
  74.6 4.5 %collective-permute-done.9.other_in = f32[8,128]{1,0:T(8,128)S(1)} collective-permute-done((f32[8,128]{1,0:T(8,128)S(1)}, f32[8,128]{1,0:T(8,128)S(1)}, u32[]{:S(2)}, u32[]{:S(2)}) %collective-permute-start.9) | collective-permute-done | bytes 4128 | tf_op jit(solution)/shard_map/ppermute | solution.py:981
  79.0 1.1 %azimuthal_filter.1 = f32[3,128,256]{2,1,0:T(8,128)} custom-call(f32[3,128,256]{2,1,0:T(8,128)S(1)} %inner_azimuthal_filter.1.inner_ref, f32[8,128]{1,0:T(8,128)S(1)} %collective-permute-done.8.one_in, f32[8,128]{1,0:T(8,128)S(1)} %collective-permute-done.9.other_in), custom_call_target="tpu_custom_call" | custom-call | tf_op jit(solution)/shard_map/azimuthal_filter/pallas_call | solution.py:965
Async XLA Ops:
  0.6 17.9 %copy-start = (s32[2,1,1,32768]{3,2,1,0:T(1,128)S(1)}, s32[2,1,1,32768]{3,2,1,0:T(1,128)}, u32[]{:S(2)}) copy-start(s32[2,1,1,32768]{3,2,1,0:T(1,128)} %param.11) | copy-start | bytes 786436
  9.2 13.2 %collective-permute-start = (f32[16,8,128]{2,1,0:T(8,128)S(1)}, f32[16,8,128]{2,1,0:T(8,128)S(1)}, u32[]{:S(2)}, u32[]{:S(2)}) collective-permute-start(f32[16,8,128]{2,1,0:T(8,128)S(1)} %get-tuple-element.31), channel_id=1, source_target_pairs={{0,1},{1,0},{2,3},{3,2},{4,5},{5,4},{6,7},{7,6},{8,9},{9,8},{10,11... | collective-permute-start | bytes 196616 | tf_op jit(solution)/shard_map/ppermute | solution.py:981
  15.5 11.5 %collective-permute-start.1 = (f32[16,8,128]{2,1,0:T(8,128)S(1)}, f32[16,8,128]{2,1,0:T(8,128)S(1)}, u32[]{:S(2)}, u32[]{:S(2)}) collective-permute-start(f32[16,8,128]{2,1,0:T(8,128)S(1)} %get-tuple-element.32), channel_id=1, source_target_pairs={{0,7},{1,2},{2,1},{3,4},{4,3},{5,6},{6,5},{7,0},{8,15},{9,10},{10,... | collective-permute-start | bytes 196616 | tf_op jit(solution)/shard_map/ppermute | solution.py:981
  34.0 14.1 %collective-permute-start.2 = (f32[3,16,128]{2,1,0:T(8,128)S(1)}, f32[3,16,128]{2,1,0:T(8,128)S(1)}, u32[]{:S(2)}, u32[]{:S(2)}) collective-permute-start(f32[3,16,128]{2,1,0:T(8,128)S(1)} %get-tuple-element.34), channel_id=1, source_target_pairs={{0,1},{1,0},{2,3},{3,2},{4,5},{5,4},{6,7},{7,6},{8,9},{9,8},{10,11... | collective-permute-start | bytes 73736 | tf_op jit(solution)/shard_map/ppermute | solution.py:981
  35.2 13.0 %collective-permute-start.3 = (f32[3,16,128]{2,1,0:T(8,128)S(1)}, f32[3,16,128]{2,1,0:T(8,128)S(1)}, u32[]{:S(2)}, u32[]{:S(2)}) collective-permute-start(f32[3,16,128]{2,1,0:T(8,128)S(1)} %get-tuple-element.35), channel_id=1, source_target_pairs={{0,7},{1,2},{2,1},{3,4},{4,3},{5,6},{6,5},{7,0},{8,15},{9,10},{10,... | collective-permute-start | bytes 73736 | tf_op jit(solution)/shard_map/ppermute | solution.py:981
  53.8 4.6 %collective-permute-start.4 = (f32[3,32,256]{2,1,0:T(8,128)S(1)}, f32[3,32,256]{2,1,0:T(8,128)S(1)}, u32[]{:S(2)}, u32[]{:S(2)}) collective-permute-start(f32[3,32,256]{2,1,0:T(8,128)S(1)} %get-tuple-element.38), channel_id=1, source_target_pairs={{0,64},{64,0},{128,192},{192,128},{1,65},{65,1},{129,193},{193,129... | collective-permute-start | bytes 294920 | tf_op jit(solution)/shard_map/ppermute | solution.py:981
  53.8 6.5 %collective-permute-start.5 = (f32[3,32,256]{2,1,0:T(8,128)S(1)}, f32[3,32,256]{2,1,0:T(8,128)S(1)}, u32[]{:S(2)}, u32[]{:S(2)}) collective-permute-start(f32[3,32,256]{2,1,0:T(8,128)S(1)} %get-tuple-element.39), channel_id=1, source_target_pairs={{0,0},{64,128},{128,64},{192,192},{1,1},{65,129},{129,65},{193,193... | collective-permute-start | bytes 294920 | tf_op jit(solution)/shard_map/ppermute | solution.py:981
  60.5 4.1 %collective-permute-start.6 = (f32[3,16,256]{2,1,0:T(8,128)S(1)}, f32[3,16,256]{2,1,0:T(8,128)S(1)}, u32[]{:S(2)}, u32[]{:S(2)}) collective-permute-start(f32[3,16,256]{2,1,0:T(8,128)S(1)} %get-tuple-element.41), channel_id=1, source_target_pairs={{0,8},{8,0},{16,24},{24,16},{32,40},{40,32},{48,56},{56,48},{1,9},... | collective-permute-start | bytes 147464 | tf_op jit(solution)/shard_map/ppermute | solution.py:981
  60.6 5.8 %collective-permute-start.7 = (f32[3,16,256]{2,1,0:T(8,128)S(1)}, f32[3,16,256]{2,1,0:T(8,128)S(1)}, u32[]{:S(2)}, u32[]{:S(2)}) collective-permute-start(f32[3,16,256]{2,1,0:T(8,128)S(1)} %get-tuple-element.42), channel_id=1, source_target_pairs={{0,0},{8,16},{16,8},{24,32},{32,24},{40,48},{48,40},{56,56},{1,1},... | collective-permute-start | bytes 147464 | tf_op jit(solution)/shard_map/ppermute | solution.py:981
  66.9 7.6 %collective-permute-start.8 = (f32[8,128]{1,0:T(8,128)S(1)}, f32[8,128]{1,0:T(8,128)S(1)}, u32[]{:S(2)}, u32[]{:S(2)}) collective-permute-start(f32[8,128]{1,0:T(8,128)S(1)} %get-tuple-element.44), channel_id=1, source_target_pairs={{0,1},{1,0},{2,3},{3,2},{4,5},{5,4},{6,7},{7,6},{8,9},{9,8},{10,11... | collective-permute-start | bytes 12296 | tf_op jit(solution)/shard_map/ppermute | solution.py:981
  69.4 9.6 %collective-permute-start.9 = (f32[8,128]{1,0:T(8,128)S(1)}, f32[8,128]{1,0:T(8,128)S(1)}, u32[]{:S(2)}, u32[]{:S(2)}) collective-permute-start(f32[8,128]{1,0:T(8,128)S(1)} %get-tuple-element.45), channel_id=1, source_target_pairs={{0,7},{1,2},{2,1},{3,4},{4,3},{5,6},{6,5},{7,0},{8,15},{9,10},{10,... | collective-permute-start | bytes 12296 | tf_op jit(solution)/shard_map/ppermute | solution.py:981

commit v5 on v4

--- a/solution.py
+++ b/solution.py
@@ -344,7 +344,7 @@
 
 def states_kernel(
     cell_hbm, gas_hbm, pos_hbm, vel_hbm, diam_hbm,
-    keys_ref, ends_ref, table_ref, words_ref, largest_ref, one_ref, other_ref,
+    keys_ref, ends_ref, table_ref, words_ref, largest_ref, sent_ref,
     cell_ref, gas_ref, pos_ref, vel_ref, diam_ref,
     gas_rows, iota, ends, idx_a, found_a, val_a, idx_b, found_b, val_b, sems,
 ):
@@ -402,7 +402,7 @@
     for n in range(16):
         code_rows(table_ref, n, largest, words_ref)
     words_ref[512:576, :] = jnp.zeros((64, LANES), jnp.int32)
-    one_ref[...], other_ref[...] = by_partner("az", table_ref[0:16], table_ref[112:128])
+    sent_ref[0], sent_ref[1] = by_partner("az", table_ref[0:16], table_ref[112:128])
 
 
 def slots(rows, parts, dtype=jnp.float32):
@@ -422,8 +422,7 @@
             jax.ShapeDtypeStruct((128, ROWS, LANES), f32),
             jax.ShapeDtypeStruct((576, LANES), i32),
             jax.ShapeDtypeStruct((ROWS, LANES), f32),
-            jax.ShapeDtypeStruct((16, ROWS, LANES), f32),
-            jax.ShapeDtypeStruct((16, ROWS, LANES), f32),
+            jax.ShapeDtypeStruct((2, 16, ROWS, LANES), f32),
         ),
         in_specs=[pl.BlockSpec(memory_space=pltpu.HBM)] * 5,
         scratch_shapes=[VMEM(x.shape, x.dtype) for x in arrays]
@@ -639,7 +638,7 @@
     heads_ref, one_ref, other_ref,
     shell, shell_words, head_sum, tail_sum, iota, iota8, *scratch,
 ):
-    shell[0:16], shell[16:32] = from_partners("az", one_in[...], other_in[...], True)
+    shell[0:16], shell[16:32] = from_partners("az", one_in[0], other_in[...], True)
     shell_largest = largest_slip(shell, 32)
     for n in range(4):
         code_rows(shell, n, shell_largest, shell_words)
@@ -875,7 +874,7 @@
 
 
 def radial_kernel(
-    taps, cells_ref, one_in, other_in, out_ref, one_ref, other_ref, padded, before_ref, after_ref
+    taps, cells_ref, one_in, other_in, out_ref, sent_ref, padded, before_ref, after_ref
 ):
     lane = lax.broadcasted_iota(jnp.int32, (LANES, LANES), 1)
     edges = jnp.zeros((LANES, LANES), jnp.float32)
@@ -896,7 +895,7 @@
         edges = jnp.where((lane >> 1) == c, left, edges)
         edges = jnp.where((lane >> 1) == 4 + c, right, edges)
     turned = edges.T
-    one_ref[...], other_ref[...] = by_partner("az", turned[0:8], turned[8:16])
+    sent_ref[0], sent_ref[1] = by_partner("az", turned[0:8], turned[8:16])
 
 
 def inner_azimuthal_kernel(taps, cells_ref, out_ref):
@@ -921,7 +920,7 @@
 def azimuthal_kernel(taps, inner_ref, one_in, other_in, out_ref):
     lane = lax.broadcasted_iota(jnp.int32, (LANES, LANES), 1)
     rest = jnp.zeros((LANES - 16, LANES), jnp.float32)
-    before, after = from_partners("az", one_in[...], other_in[...], True)
+    before, after = from_partners("az", one_in[0], other_in[...], True)
     edges = jnp.concatenate([after, before, rest], axis=0).T
     for c in range(3):
         out_left, out_right = inner_ref[c, :, 0:LANES], inner_ref[c, :, LANES:]
@@ -940,7 +939,7 @@
     taps = [x / sum(raw) for x in raw]
     whole = jax.ShapeDtypeStruct(deposit.shape, f32)
     radial_face = jax.ShapeDtypeStruct((3, 16, 2 * LANES), f32)
-    edge = jax.ShapeDtypeStruct((8, LANES), f32)
+    edges = jax.ShapeDtypeStruct((2, 8, LANES), f32)
     cells, one, other = pl.pallas_call(
         functools.partial(axial_kernel, taps),
         name="axial_filter",
@@ -948,14 +947,14 @@
         scratch_shapes=[VMEM((16, 2 * LANES), f32)] * 2,
         compiler_params=params(),
     )(deposit, *swapped(one, other, "ax"))
-    cells, one, other = pl.pallas_call(
+    cells, sent = pl.pallas_call(
         functools.partial(radial_kernel, taps),
         name="radial_filter",
-        out_shape=(whole, edge, edge),
+        out_shape=(whole, edges),
         scratch_shapes=[VMEM((24, 2 * LANES), f32)] + [VMEM((16, 2 * LANES), f32)] * 2,
         compiler_params=params(),
     )(cells, *swapped(one, other, "rad"))
-    one, other = swapped(one, other, "az", True)
+    one, other, _ = passed_on(sent, "az")
     inner = pl.pallas_call(
         functools.partial(inner_azimuthal_kernel, taps),
         name="inner_azimuthal_filter",
@@ -983,6 +982,15 @@
     ]
 
 
+def passed_on(both, axis, beside=None):
+    count = lax.axis_size(axis)
+    came = lax.ppermute(both, axis, [(i, i ^ 1) for i in range(count)])
+    if beside is not None:
+        came, beside = lax.optimization_barrier((came, beside))
+    further = [(i, (i + (-2 if i % 2 else 2)) % count) for i in range(count)]
+    return came, lax.ppermute(came[1], axis, further), beside
+
+
 def per_device(positions, velocity, diameter, cell_index, pair_list, live_pairs, gas_velocity):
     live = live_pairs.reshape(1, 1)
     cells = cell_index.reshape(128, LANES)
@@ -990,11 +998,9 @@
     pos = positions.reshape(3, 128, LANES)
     vel = velocity.reshape(3, 128, LANES)
     diam = diameter.reshape(128, LANES)
-    cell_keys, cell_ends, table, words, largest, one, other = droplet_states(
-        cells, gas, pos, vel, diam
-    )
-    one, other = swapped(one, other, "az", True)
-    pair_keys, pair_ends = pair_sort(live, pair_list.reshape(2, 256, LANES))
+    cell_keys, cell_ends, table, words, largest, sent = droplet_states(cells, gas, pos, vel, diam)
+    sorted_pairs = pair_sort(live, pair_list.reshape(2, 256, LANES))
+    one, other, (pair_keys, pair_ends) = passed_on(sent, "az", sorted_pairs)
     heads, one, other = near_pairs(pair_ends, pair_keys, words, largest, one, other)
     one, other = swapped(one, other, "az", True)
     corr = own_pairs(live, pair_ends, pair_keys, words, largest, heads)

time: 81 us -> 83.7 us (1.033)
  waiting for transfers between devices: 13.8 us -> 17.3 us
  starting transfers between devices: 28.7 us -> 27.4 us
    ppermute x10 -> x6, starting transfers between devices: 28.7 us -> 14.7 us  [swapped(): lax.ppermute(x, axis, [(i, partner(i, odd)) for i in range(count)])]
    ppermute x0 -> x4, waiting for transfers between devices: none -> 12.9 us  [the longest x2 8.24 us: passed_on(): return (came, lax.ppermute(came[1], axis, further), beside)]
    ppermute x0 -> x4, starting transfers between devices: none -> 12.7 us  [the longest x2 11.1 us: passed_on(): came = lax.ppermute(both, axis, [(i, i ^ 1) for i in range(count)])]
    ppermute x10 -> x6, waiting for transfers between devices: 13.8 us -> 4.33 us  [swapped(): lax.ppermute(x, axis, [(i, partner(i, odd)) for i in range(count)])]
  transfers between devices with their start and end apart: 10 -> 10, of which waited for: 5 -> 6; matrix products, arithmetic and copies ran while one was open for 0% -> 0% of each run, Pallas kernels for 16% -> 16%
where the time goes in v5:
time: 83.7 us; the launch traced here: 83.1 us
  Pallas kernels  37 us (44%)
  starting transfers between devices  27.4 us (33%)
  waiting for transfers between devices  17.3 us (21%)
  between operations  1.4 us (2%)
    ppermute x6, starting transfers between devices, swapped(): lax.ppermute(x, axis, [(i, partner(i, odd)) for i in range(count)])  14.7 us
    ppermute x2, starting transfers between devices, passed_on(): came = lax.ppermute(both, axis, [(i, i ^ 1) for i in range(count)])  11.1 us
    pallas_call x1, Pallas kernels, own_pairs(): pl.pallas_call(own_pairs_kernel, name='own_pairs', out_shape=jax.ShapeDty...  8.85 us
    pallas_call x1, Pallas kernels, droplet_states(): pl.pallas_call(states_kernel, name='droplet_states', out_shape=(jax.Shape...  8.51 us
    ppermute x2, waiting for transfers between devices, passed_on(): return (came, lax.ppermute(came[1], axis, further), beside)  8.24 us
    pallas_call x1, Pallas kernels, near_pairs(): pl.pallas_call(near_pairs_kernel, name='near_pairs', out_shape=(jax.Shape...  7.76 us
    pallas_call x1, Pallas kernels, deposits(): pl.pallas_call(deposit_kernel, name='deposits', out_shape=(jax.ShapeDtype...  5.67 us
    ppermute x2, waiting for transfers between devices, passed_on(): came = lax.ppermute(both, axis, [(i, i ^ 1) for i in range(count)])  4.71 us
  transfers between devices with their start and end apart: 10, of which 6 were waited for; matrix products, arithmetic and copies ran while one was open for 0% of the time, Pallas kernels for 16%

profile of v5, /device:TPU:40, one launch (start us, length us, event | category | flops | bytes accessed | tf_op | source)
XLA Modules:
  0.0 83.1 jit_solution(5157621076566588489)
XLA Ops:
  0.6 0.0 copy-start
  0.6 8.5 %droplet_states.1 = (s32[128,128]{1,0:T(8,128)S(1)}, s32[8,128]{1,0:T(8,128)S(1)}, f32[128,8,128]{2,1,0:T(8,128)S(1)}, s32[576,128]{1,0:T(8,128)S(1)}, f32[8,128...) custom-call(s32[128,128]{1,0:T(8,128)} %bitcast.20, f32[3,128,256]{2,1,0:T(8,128)} %bitcast.16, f32[3,128,128]{2,1,0:T(8,128)} %bitcast.18, ...), custom_call_target="tpu_custom_call" | custom-call | tf_op jit(solution)/shard_map/droplet_states/pallas_call | solution.py:416
  9.2 6.4 %collective-permute-start = (f32[2,16,8,128]{3,2,1,0:T(8,128)S(1)}, f32[2,16,8,128]{3,2,1,0:T(8,128)S(1)}, u32[]{:S(2)}, u32[]{:S(2)}) collective-permute-start(f32[2,16,8,128]{3,2,1,0:T(8,128)S(1)} %get-tuple-element.28), channel_id=1, source_target_pairs={{0,1},{1,0},{2,3},{3,2},{4,5},{5,4},{6,7},{7,6},{8,9},{9,8},{10,11... | collective-permute-start | bytes 393224 | tf_op jit(solution)/shard_map/ppermute | solution.py:987
  16.2 0.0 copy-done
  16.2 3.9 %pair_sort.1 = (s32[2,128,128]{2,1,0:T(8,128)S(1)}, s32[16,128]{1,0:T(8,128)S(1)}) custom-call(s32[1,1]{1,0:T(1,128)} %bitcast.13.live_ref, s32[2,256,128]{2,1,0:T(8,128)S(1)} %bitcast.15), custom_call_target="tpu_custom_call" | custom-call | tf_op jit(solution)/shard_map/pair_sort/pallas_call | solution.py:489
  20.1 1.8 %collective-permute-done.one_in = f32[2,16,8,128]{3,2,1,0:T(8,128)S(1)} collective-permute-done((f32[2,16,8,128]{3,2,1,0:T(8,128)S(1)}, f32[2,16,8,128]{3,2,1,0:T(8,128)S(1)}, u32[]{:S(2)}, u32[]{:S(2)}) %collective-permute-start) | collective-permute-done | bytes 131104 | tf_op jit(solution)/shard_map/ppermute | solution.py:987
  21.9 1.5 %collective-permute-start.1 = (f32[16,8,128]{2,1,0:T(8,128)S(1)}, f32[16,8,128]{2,1,0:T(8,128)S(1)}, u32[]{:S(2)}, u32[]{:S(2)}) collective-permute-start(f32[16,8,128]{2,1,0:T(8,128)S(1)} %slice_bitcast_fusion), channel_id=1, source_target_pairs={{0,2},{1,7},{2,4},{3,1},{4,6},{5,3},{6,0},{7,5},{8,10},{9,15},{10,... | collective-permute-start | bytes 196616 | tf_op jit(solution)/shard_map/ppermute | solution.py:991
  23.4 4.0 %collective-permute-done.1.other_in = f32[16,8,128]{2,1,0:T(8,128)S(1)} collective-permute-done((f32[16,8,128]{2,1,0:T(8,128)S(1)}, f32[16,8,128]{2,1,0:T(8,128)S(1)}, u32[]{:S(2)}, u32[]{:S(2)}) %collective-permute-start.1) | collective-permute-done | bytes 65568 | tf_op jit(solution)/shard_map/ppermute | solution.py:991
  27.4 7.8 %near_pairs.1 = (f32[3,128,128]{2,1,0:T(8,128)S(1)}, f32[3,16,128]{2,1,0:T(8,128)S(1)}, f32[3,16,128]{2,1,0:T(8,128)S(1)}) custom-call(s32[16,128]{1,0:T(8,128)S(1)} %get-tuple-element.31.ends, s32[2,128,128]{2,1,0:T(8,128)S(1)} %get-tuple-element.32.keys_ref, s32[576,128]{1,0:T(8,128)S(1)} %get-tuple-element.33.words_ref, ...), custom_call_target="tpu_custom_call" | custom-call | tf_op jit(solution)/shard_map/near_pairs/pallas_call | solution.py:698
  35.1 3.4 %collective-permute-start.2 = (f32[3,16,128]{2,1,0:T(8,128)S(1)}, f32[3,16,128]{2,1,0:T(8,128)S(1)}, u32[]{:S(2)}, u32[]{:S(2)}) collective-permute-start(f32[3,16,128]{2,1,0:T(8,128)S(1)} %get-tuple-element.37), channel_id=1, source_target_pairs={{0,1},{1,0},{2,3},{3,2},{4,5},{5,4},{6,7},{7,6},{8,9},{9,8},{10,11... | collective-permute-start | bytes 73736 | tf_op jit(solution)/shard_map/ppermute | solution.py:980
  38.5 2.7 %collective-permute-start.3 = (f32[3,16,128]{2,1,0:T(8,128)S(1)}, f32[3,16,128]{2,1,0:T(8,128)S(1)}, u32[]{:S(2)}, u32[]{:S(2)}) collective-permute-start(f32[3,16,128]{2,1,0:T(8,128)S(1)} %get-tuple-element.38), channel_id=1, source_target_pairs={{0,7},{1,2},{2,1},{3,4},{4,3},{5,6},{6,5},{7,0},{8,15},{9,10},{10,... | collective-permute-start | bytes 73736 | tf_op jit(solution)/shard_map/ppermute | solution.py:980
  41.2 8.8 %own_pairs.1.corr_ref = f32[3,128,128]{2,1,0:T(8,128)S(1)} custom-call(s32[1,1]{1,0:T(1,128)} %bitcast.14.live_ref, s32[16,128]{1,0:T(8,128)S(1)} %get-tuple-element.31.ends, s32[2,128,128]{2,1,0:T(8,128)S(1)} %get-tuple-element.32.keys_ref, s32[576,128]{1,0:T(8,128)S(1)} %get-tuple-element.33.words_ref, f32[8,128]{1,0:T(8,128)S(1)} %get-tuple-element.34.largest_ref, ...), custom_call_target="tpu_custom_call" | custom-call | tf_op jit(solution)/shard_map/own_pairs/pallas_call | solution.py:715
  50.1 0.0 collective-permute-done.2.one_in
  50.1 0.0 collective-permute-done.3.other_in
  50.1 5.7 %deposits.1 = (f32[3,128,256]{2,1,0:T(8,128)S(1)}, f32[3,128,128]{2,1,0:T(8,128)}, f32[3,32,256]{2,1,0:T(8,128)S(1)}, f32[3,32,256]{2,1,0:T(8,128)S(1)}) custom-call(s32[8,128]{1,0:T(8,128)S(1)} %get-tuple-element.25.ends, s32[128,128]{1,0:T(8,128)S(1)} %get-tuple-element.26.keys_ref, f32[128,8,128]{2,1,0:T(8,128)S(1)} %get-tuple-element.27.table_ref, ...), custom_call_target="tpu_custom_call" | custom-call | tf_op jit(solution)/shard_map/deposits/pallas_call | solution.py:845
  55.8 0.7 collective-permute-start.4
  56.5 4.0 %collective-permute-start.5 = (f32[3,32,256]{2,1,0:T(8,128)S(1)}, f32[3,32,256]{2,1,0:T(8,128)S(1)}, u32[]{:S(2)}, u32[]{:S(2)}) collective-permute-start(f32[3,32,256]{2,1,0:T(8,128)S(1)} %get-tuple-element.42), channel_id=1, source_target_pairs={{0,0},{64,128},{128,64},{192,192},{1,1},{65,129},{129,65},{193,193... | collective-permute-start | bytes 294920 | tf_op jit(solution)/shard_map/ppermute | solution.py:980
  60.5 0.0 collective-permute-done.4.one_in
  60.5 2.6 %collective-permute-done.5.other_in = f32[3,32,256]{2,1,0:T(8,128)S(1)} collective-permute-done((f32[3,32,256]{2,1,0:T(8,128)S(1)}, f32[3,32,256]{2,1,0:T(8,128)S(1)}, u32[]{:S(2)}, u32[]{:S(2)}) %collective-permute-start.5) | collective-permute-done | bytes 98336 | tf_op jit(solution)/shard_map/ppermute | solution.py:980
  63.1 0.2 axial_filter.1
  63.3 0.1 collective-permute-start.6
  63.4 3.9 %collective-permute-start.7 = (f32[3,16,256]{2,1,0:T(8,128)S(1)}, f32[3,16,256]{2,1,0:T(8,128)S(1)}, u32[]{:S(2)}, u32[]{:S(2)}) collective-permute-start(f32[3,16,256]{2,1,0:T(8,128)S(1)} %get-tuple-element.45), channel_id=1, source_target_pairs={{0,0},{8,16},{16,8},{24,32},{32,24},{40,48},{48,40},{56,56},{1,1},... | collective-permute-start | bytes 147464 | tf_op jit(solution)/shard_map/ppermute | solution.py:980
  67.2 0.0 collective-permute-done.6.one_in
  67.3 1.7 %collective-permute-done.7.other_in = f32[3,16,256]{2,1,0:T(8,128)S(1)} collective-permute-done((f32[3,16,256]{2,1,0:T(8,128)S(1)}, f32[3,16,256]{2,1,0:T(8,128)S(1)}, u32[]{:S(2)}, u32[]{:S(2)}) %collective-permute-start.7) | collective-permute-done | bytes 49184 | tf_op jit(solution)/shard_map/ppermute | solution.py:980
  69.0 0.5 radial_filter.1
  69.5 4.7 %collective-permute-start.8 = (f32[2,8,128]{2,1,0:T(8,128)S(1)}, f32[2,8,128]{2,1,0:T(8,128)S(1)}, u32[]{:S(2)}, u32[]{:S(2)}) collective-permute-start(f32[2,8,128]{2,1,0:T(8,128)S(1)} %get-tuple-element.47), channel_id=1, source_target_pairs={{0,1},{1,0},{2,3},{3,2},{4,5},{5,4},{6,7},{7,6},{8,9},{9,8},{10,11... | collective-permute-start | bytes 24584 | tf_op jit(solution)/shard_map/ppermute | solution.py:987
  74.2 2.9 %collective-permute-done.8.one_in = f32[2,8,128]{2,1,0:T(8,128)S(1)} collective-permute-done((f32[2,8,128]{2,1,0:T(8,128)S(1)}, f32[2,8,128]{2,1,0:T(8,128)S(1)}, u32[]{:S(2)}, u32[]{:S(2)}) %collective-permute-start.8) | collective-permute-done | bytes 8224 | tf_op jit(solution)/shard_map/ppermute | solution.py:987
  77.1 0.1 collective-permute-start.9
  77.2 0.5 inner_azimuthal_filter.1.inner_ref
  77.7 4.3 %collective-permute-done.9.other_in = f32[8,128]{1,0:T(8,128)S(1)} collective-permute-done((f32[8,128]{1,0:T(8,128)S(1)}, f32[8,128]{1,0:T(8,128)S(1)}, u32[]{:S(2)}, u32[]{:S(2)}) %collective-permute-start.9) | collective-permute-done | bytes 4128 | tf_op jit(solution)/shard_map/ppermute | solution.py:991
  82.0 1.1 %azimuthal_filter.1 = f32[3,128,256]{2,1,0:T(8,128)} custom-call(f32[3,128,256]{2,1,0:T(8,128)S(1)} %inner_azimuthal_filter.1.inner_ref, f32[2,8,128]{2,1,0:T(8,128)S(1)} %collective-permute-done.8.one_in, f32[8,128]{1,0:T(8,128)S(1)} %collective-permute-done.9.other_in), custom_call_target="tpu_custom_call" | custom-call | tf_op jit(solution)/shard_map/azimuthal_filter/pallas_call | solution.py:964
  (2 shorter events, 0.0 us)
Async XLA Ops:
  0.6 15.6 %copy-start = (s32[2,1,1,32768]{3,2,1,0:T(1,128)S(1)}, s32[2,1,1,32768]{3,2,1,0:T(1,128)}, u32[]{:S(2)}) copy-start(s32[2,1,1,32768]{3,2,1,0:T(1,128)} %param.11) | copy-start | bytes 786436
  9.2 12.7 %collective-permute-start = (f32[2,16,8,128]{3,2,1,0:T(8,128)S(1)}, f32[2,16,8,128]{3,2,1,0:T(8,128)S(1)}, u32[]{:S(2)}, u32[]{:S(2)}) collective-permute-start(f32[2,16,8,128]{3,2,1,0:T(8,128)S(1)} %get-tuple-element.28), channel_id=1, source_target_pairs={{0,1},{1,0},{2,3},{3,2},{4,5},{5,4},{6,7},{7,6},{8,9},{9,8},{10,11... | collective-permute-start | bytes 393224 | tf_op jit(solution)/shard_map/ppermute | solution.py:987
  21.9 5.5 %collective-permute-start.1 = (f32[16,8,128]{2,1,0:T(8,128)S(1)}, f32[16,8,128]{2,1,0:T(8,128)S(1)}, u32[]{:S(2)}, u32[]{:S(2)}) collective-permute-start(f32[16,8,128]{2,1,0:T(8,128)S(1)} %slice_bitcast_fusion), channel_id=1, source_target_pairs={{0,2},{1,7},{2,4},{3,1},{4,6},{5,3},{6,0},{7,5},{8,10},{9,15},{10,... | collective-permute-start | bytes 196616 | tf_op jit(solution)/shard_map/ppermute | solution.py:991
  35.1 14.9 %collective-permute-start.2 = (f32[3,16,128]{2,1,0:T(8,128)S(1)}, f32[3,16,128]{2,1,0:T(8,128)S(1)}, u32[]{:S(2)}, u32[]{:S(2)}) collective-permute-start(f32[3,16,128]{2,1,0:T(8,128)S(1)} %get-tuple-element.37), channel_id=1, source_target_pairs={{0,1},{1,0},{2,3},{3,2},{4,5},{5,4},{6,7},{7,6},{8,9},{9,8},{10,11... | collective-permute-start | bytes 73736 | tf_op jit(solution)/shard_map/ppermute | solution.py:980
  38.5 11.6 %collective-permute-start.3 = (f32[3,16,128]{2,1,0:T(8,128)S(1)}, f32[3,16,128]{2,1,0:T(8,128)S(1)}, u32[]{:S(2)}, u32[]{:S(2)}) collective-permute-start(f32[3,16,128]{2,1,0:T(8,128)S(1)} %get-tuple-element.38), channel_id=1, source_target_pairs={{0,7},{1,2},{2,1},{3,4},{4,3},{5,6},{6,5},{7,0},{8,15},{9,10},{10,... | collective-permute-start | bytes 73736 | tf_op jit(solution)/shard_map/ppermute | solution.py:980
  55.8 4.7 %collective-permute-start.4 = (f32[3,32,256]{2,1,0:T(8,128)S(1)}, f32[3,32,256]{2,1,0:T(8,128)S(1)}, u32[]{:S(2)}, u32[]{:S(2)}) collective-permute-start(f32[3,32,256]{2,1,0:T(8,128)S(1)} %get-tuple-element.41), channel_id=1, source_target_pairs={{0,64},{64,0},{128,192},{192,128},{1,65},{65,1},{129,193},{193,129... | collective-permute-start | bytes 294920 | tf_op jit(solution)/shard_map/ppermute | solution.py:980
  56.5 6.6 %collective-permute-start.5 = (f32[3,32,256]{2,1,0:T(8,128)S(1)}, f32[3,32,256]{2,1,0:T(8,128)S(1)}, u32[]{:S(2)}, u32[]{:S(2)}) collective-permute-start(f32[3,32,256]{2,1,0:T(8,128)S(1)} %get-tuple-element.42), channel_id=1, source_target_pairs={{0,0},{64,128},{128,64},{192,192},{1,1},{65,129},{129,65},{193,193... | collective-permute-start | bytes 294920 | tf_op jit(solution)/shard_map/ppermute | solution.py:980
  63.3 4.0 %collective-permute-start.6 = (f32[3,16,256]{2,1,0:T(8,128)S(1)}, f32[3,16,256]{2,1,0:T(8,128)S(1)}, u32[]{:S(2)}, u32[]{:S(2)}) collective-permute-start(f32[3,16,256]{2,1,0:T(8,128)S(1)} %get-tuple-element.44), channel_id=1, source_target_pairs={{0,8},{8,0},{16,24},{24,16},{32,40},{40,32},{48,56},{56,48},{1,9},... | collective-permute-start | bytes 147464 | tf_op jit(solution)/shard_map/ppermute | solution.py:980
  63.4 5.6 %collective-permute-start.7 = (f32[3,16,256]{2,1,0:T(8,128)S(1)}, f32[3,16,256]{2,1,0:T(8,128)S(1)}, u32[]{:S(2)}, u32[]{:S(2)}) collective-permute-start(f32[3,16,256]{2,1,0:T(8,128)S(1)} %get-tuple-element.45), channel_id=1, source_target_pairs={{0,0},{8,16},{16,8},{24,32},{32,24},{40,48},{48,40},{56,56},{1,1},... | collective-permute-start | bytes 147464 | tf_op jit(solution)/shard_map/ppermute | solution.py:980
  69.5 7.6 %collective-permute-start.8 = (f32[2,8,128]{2,1,0:T(8,128)S(1)}, f32[2,8,128]{2,1,0:T(8,128)S(1)}, u32[]{:S(2)}, u32[]{:S(2)}) collective-permute-start(f32[2,8,128]{2,1,0:T(8,128)S(1)} %get-tuple-element.47), channel_id=1, source_target_pairs={{0,1},{1,0},{2,3},{3,2},{4,5},{5,4},{6,7},{7,6},{8,9},{9,8},{10,11... | collective-permute-start | bytes 24584 | tf_op jit(solution)/shard_map/ppermute | solution.py:987
  77.1 4.8 %collective-permute-start.9 = (f32[8,128]{1,0:T(8,128)S(1)}, f32[8,128]{1,0:T(8,128)S(1)}, u32[]{:S(2)}, u32[]{:S(2)}) collective-permute-start(f32[8,128]{1,0:T(8,128)S(1)} %slice_bitcast_fusion.1), channel_id=1, source_target_pairs={{0,2},{1,7},{2,4},{3,1},{4,6},{5,3},{6,0},{7,5},{8,10},{9,15},{10,... | collective-permute-start | bytes 12296 | tf_op jit(solution)/shard_map/ppermute | solution.py:991

commit v6 on v4

--- a/solution.py
+++ b/solution.py
@@ -110,19 +110,19 @@
     return jnp.broadcast_to(ref[row : row + 1, :], (16, LANES)).astype(jnp.bfloat16)
 
 
+def one_hot(x, k):
+    return jnp.maximum(jnp.minimum((x + 1) - k, k - (x - 1)), 0)
+
+
 def one_hot_rows(low, iota):
-    one = jnp.ones((16, LANES), jnp.bfloat16)
-    zero = jnp.zeros((16, LANES), jnp.bfloat16)
     return jnp.concatenate(
-        [jnp.where(low == iota[k : k + 16, :], one, zero) for k in range(0, iota.shape[0], 16)],
-        axis=0,
+        [one_hot(low, iota[k : k + 16, :]) for k in range(0, iota.shape[0], 16)], axis=0
     )
 
 
 def spread_rows(rel, parts, iota):
-    hit = rel == iota[0:16, :]
-    zero = jnp.zeros((16, LANES), jnp.bfloat16)
-    return jnp.concatenate([jnp.where(hit, p, zero) for part in parts for p in part], axis=0)
+    hit = one_hot(rel, iota[0:16, :])
+    return jnp.concatenate([hit * p for part in parts for p in part], axis=0)
 
 
 def block_product(rows, hots):
@@ -365,7 +365,6 @@
         regs.append(cells[v * ROWS : (v + 1) * ROWS] * BLOCK + own)
     place = [("v", k) for k in range(4)] + [("s", k) for k in range(3)] + [("l", k) for k in range(4)]
     regs = sort_network(regs, place, 11)
-    keys_ref[...] = jnp.concatenate(regs, axis=0).T
     least = functools.reduce(jnp.minimum, regs)
     most = functools.reduce(jnp.maximum, regs)
     least = lax.shift_right_logical(jnp.min(least, axis=0, keepdims=True), 19)
@@ -375,12 +374,13 @@
     ends_ref[2:8, :] = running_max(most - least, 16)[0:6]
     copy = pltpu.make_async_copy(ends_ref, ends, sems.at[5])
     copy.start()
+    keys_ref[...] = jnp.concatenate(regs, axis=0).T
+    fill_iota(iota)
     copies[1].wait()
     fill_gas_rows(gas_ref, gas_rows)
     for other in copies[2:]:
         other.wait()
     copy.wait()
-    fill_iota(iota)
     a, b = (idx_a, found_a, val_a), (idx_b, found_b, val_b)
     step = functools.partial(
         states_step, keys_ref=keys_ref, ends=ends, gas_rows=gas_rows, iota=iota,
@@ -588,12 +588,11 @@
     first, tail_first = item
     parts = [[packed_row(val.at[4 + 3 * n + c], k) for c in range(3)] for n in range(2)]
     heads = spread_rows(packed_row(val.at[0], k), parts, iota)
-    hit = packed_row(val.at[2], k) == iota8[...]
-    zero = jnp.zeros((16, LANES), jnp.bfloat16)
+    hit = one_hot(packed_row(val.at[2], k), iota8[...])
     tails = []
     for n in range(10, 16, 2):
         both = jnp.concatenate([wide(val, n, k), wide(val, n + 1, k)], axis=0)
-        tails.append(jnp.where(hit, both.astype(jnp.bfloat16), zero))
+        tails.append(hit * both.astype(jnp.bfloat16))
     tails = jnp.concatenate(tails, axis=0)
     out = block_product(
         [heads, tails], [one_hot_rows(packed_row(val.at[n], k), iota) for n in (1, 3)]

time: 81 us -> 84.4 us (1.042)
  starting transfers between devices: 28.7 us -> 30 us
  waiting for transfers between devices: 13.8 us -> 15.1 us
    ppermute x10, starting transfers between devices: 28.7 us -> 30 us  [swapped(): lax.ppermute(x, axis, [(i, partner(i, odd)) for i in range(count)])]
    ppermute x10, waiting for transfers between devices: 13.8 us -> 15.1 us  [swapped(): lax.ppermute(x, axis, [(i, partner(i, odd)) for i in range(count)])]
    pallas_call x1, Pallas kernels: 6.98 us -> 6.07 us  [near_pairs(): pl.pallas_call(near_pairs_kernel, name='near_pairs', out_shape=(jax.Shape...]
  transfers between devices with their start and end apart: 10 -> 10, of which waited for: 5 -> 6; matrix products, arithmetic and copies ran while one was open for 0% -> 0% of each run, Pallas kernels for 16% -> 17%
where the time goes in v6:
time: 84.4 us; the launch traced here: 83.4 us
  Pallas kernels  36.9 us (44%)
  starting transfers between devices  30 us (36%)
  waiting for transfers between devices  15.1 us (18%)
  between operations  1.4 us (2%)
    ppermute x10, starting transfers between devices, swapped(): lax.ppermute(x, axis, [(i, partner(i, odd)) for i in range(count)])  30 us
    ppermute x10, waiting for transfers between devices, swapped(): lax.ppermute(x, axis, [(i, partner(i, odd)) for i in range(count)])  15.1 us
    pallas_call x1, Pallas kernels, own_pairs(): pl.pallas_call(own_pairs_kernel, name='own_pairs', out_shape=jax.ShapeDty...  9.49 us
    pallas_call x1, Pallas kernels, droplet_states(): pl.pallas_call(states_kernel, name='droplet_states', out_shape=(jax.Shape...  8.64 us
    pallas_call x1, Pallas kernels, deposits(): pl.pallas_call(deposit_kernel, name='deposits', out_shape=(jax.ShapeDtype...  6.48 us
    pallas_call x1, Pallas kernels, near_pairs(): pl.pallas_call(near_pairs_kernel, name='near_pairs', out_shape=(jax.Shape...  6.07 us
    pallas_call x1, Pallas kernels, pair_sort(): pl.pallas_call(pair_sort_kernel, name='pair_sort', out_shape=(jax.ShapeDt...  3.85 us
  transfers between devices with their start and end apart: 10, of which 6 were waited for; matrix products, arithmetic and copies ran while one was open for 0% of the time, Pallas kernels for 17%

profile of v6, /device:TPU:40, one launch (start us, length us, event | category | flops | bytes accessed | tf_op | source)
XLA Modules:
  0.0 83.4 jit_solution(11569626141388979335)
XLA Ops:
  0.6 0.0 copy-start
  0.6 8.6 %droplet_states.1 = (s32[128,128]{1,0:T(8,128)S(1)}, s32[8,128]{1,0:T(8,128)S(1)}, f32[128,8,128]{2,1,0:T(8,128)S(1)}, s32[576,128]{1,0:T(8,128)S(1)}, f32[8,128...) custom-call(s32[128,128]{1,0:T(8,128)} %bitcast.16, f32[3,128,256]{2,1,0:T(8,128)} %bitcast.12, ...), custom_call_target="tpu_custom_call" | custom-call | tf_op jit(solution)/shard_map/droplet_states/pallas_call | solution.py:416
  9.3 6.4 %collective-permute-start = (f32[16,8,128]{2,1,0:T(8,128)S(1)}, f32[16,8,128]{2,1,0:T(8,128)S(1)}, u32[]{:S(2)}, u32[]{:S(2)}) collective-permute-start(f32[16,8,128]{2,1,0:T(8,128)S(1)} %get-tuple-element.31), channel_id=1, source_target_pairs={{0,1},{1,0},{2,3},{3,2},{4,5},{5,4},{6,7},{7,6},{8,9},{9,8},{10,11... | collective-permute-start | bytes 196616 | tf_op jit(solution)/shard_map/ppermute | solution.py:980
  15.7 2.3 %collective-permute-start.1 = (f32[16,8,128]{2,1,0:T(8,128)S(1)}, f32[16,8,128]{2,1,0:T(8,128)S(1)}, u32[]{:S(2)}, u32[]{:S(2)}) collective-permute-start(f32[16,8,128]{2,1,0:T(8,128)S(1)} %get-tuple-element.32), channel_id=1, source_target_pairs={{0,7},{1,2},{2,1},{3,4},{4,3},{5,6},{6,5},{7,0},{8,15},{9,10},{10,... | collective-permute-start | bytes 196616 | tf_op jit(solution)/shard_map/ppermute | solution.py:980
  18.6 0.0 copy-done
  18.6 3.9 %pair_sort.1 = (s32[2,128,128]{2,1,0:T(8,128)S(1)}, s32[16,128]{1,0:T(8,128)S(1)}) custom-call(s32[1,1]{1,0:T(1,128)} %bitcast.9.live_ref, s32[2,256,128]{2,1,0:T(8,128)S(1)} %bitcast.11), custom_call_target="tpu_custom_call" | custom-call | tf_op jit(solution)/shard_map/pair_sort/pallas_call | solution.py:490
  22.5 0.0 collective-permute-done.one_in
  22.5 4.6 %collective-permute-done.1.other_in = f32[16,8,128]{2,1,0:T(8,128)S(1)} collective-permute-done((f32[16,8,128]{2,1,0:T(8,128)S(1)}, f32[16,8,128]{2,1,0:T(8,128)S(1)}, u32[]{:S(2)}, u32[]{:S(2)}) %collective-permute-start.1) | collective-permute-done | bytes 65568 | tf_op jit(solution)/shard_map/ppermute | solution.py:980
  27.1 6.1 %near_pairs.1 = (f32[3,128,128]{2,1,0:T(8,128)S(1)}, f32[3,16,128]{2,1,0:T(8,128)S(1)}, f32[3,16,128]{2,1,0:T(8,128)S(1)}) custom-call(s32[16,128]{1,0:T(8,128)S(1)} %get-tuple-element.27.ends, s32[2,128,128]{2,1,0:T(8,128)S(1)} %get-tuple-element.28.keys_ref, s32[576,128]{1,0:T(8,128)S(1)} %get-tuple-element.29.words_ref, ...), custom_call_target="tpu_custom_call" | custom-call | tf_op jit(solution)/shard_map/near_pairs/pallas_call | solution.py:698
  33.2 2.0 %collective-permute-start.2 = (f32[3,16,128]{2,1,0:T(8,128)S(1)}, f32[3,16,128]{2,1,0:T(8,128)S(1)}, u32[]{:S(2)}, u32[]{:S(2)}) collective-permute-start(f32[3,16,128]{2,1,0:T(8,128)S(1)} %get-tuple-element.34), channel_id=1, source_target_pairs={{0,1},{1,0},{2,3},{3,2},{4,5},{5,4},{6,7},{7,6},{8,9},{9,8},{10,11... | collective-permute-start | bytes 73736 | tf_op jit(solution)/shard_map/ppermute | solution.py:980
  35.3 5.3 %collective-permute-start.3 = (f32[3,16,128]{2,1,0:T(8,128)S(1)}, f32[3,16,128]{2,1,0:T(8,128)S(1)}, u32[]{:S(2)}, u32[]{:S(2)}) collective-permute-start(f32[3,16,128]{2,1,0:T(8,128)S(1)} %get-tuple-element.35), channel_id=1, source_target_pairs={{0,7},{1,2},{2,1},{3,4},{4,3},{5,6},{6,5},{7,0},{8,15},{9,10},{10,... | collective-permute-start | bytes 73736 | tf_op jit(solution)/shard_map/ppermute | solution.py:980
  40.6 9.5 %own_pairs.1.corr_ref = f32[3,128,128]{2,1,0:T(8,128)S(1)} custom-call(s32[1,1]{1,0:T(1,128)} %bitcast.10.live_ref, s32[16,128]{1,0:T(8,128)S(1)} %get-tuple-element.27.ends, s32[2,128,128]{2,1,0:T(8,128)S(1)} %get-tuple-element.28.keys_ref, s32[576,128]{1,0:T(8,128)S(1)} %get-tuple-element.29.words_ref, f32[8,128]{1,0:T(8,128)S(1)} %get-tuple-element.30.largest_ref, ...), custom_call_target="tpu_custom_call" | custom-call | tf_op jit(solution)/shard_map/own_pairs/pallas_call | solution.py:715
  50.1 0.0 collective-permute-done.2.one_in
  50.1 0.0 collective-permute-done.3.other_in
  50.1 6.5 %deposits.1 = (f32[3,128,256]{2,1,0:T(8,128)S(1)}, f32[3,128,128]{2,1,0:T(8,128)}, f32[3,32,256]{2,1,0:T(8,128)S(1)}, f32[3,32,256]{2,1,0:T(8,128)S(1)}) custom-call(s32[8,128]{1,0:T(8,128)S(1)} %get-tuple-element.24.ends, s32[128,128]{1,0:T(8,128)S(1)} %get-tuple-element.25.keys_ref, f32[128,8,128]{2,1,0:T(8,128)S(1)} %get-tuple-element.26.table_ref, ...), custom_call_target="tpu_custom_call" | custom-call | tf_op jit(solution)/shard_map/deposits/pallas_call | solution.py:845
  56.6 1.6 %collective-permute-start.4 = (f32[3,32,256]{2,1,0:T(8,128)S(1)}, f32[3,32,256]{2,1,0:T(8,128)S(1)}, u32[]{:S(2)}, u32[]{:S(2)}) collective-permute-start(f32[3,32,256]{2,1,0:T(8,128)S(1)} %get-tuple-element.38), channel_id=1, source_target_pairs={{0,64},{64,0},{128,192},{192,128},{1,65},{65,1},{129,193},{193,129... | collective-permute-start | bytes 294920 | tf_op jit(solution)/shard_map/ppermute | solution.py:980
  58.2 2.9 %collective-permute-start.5 = (f32[3,32,256]{2,1,0:T(8,128)S(1)}, f32[3,32,256]{2,1,0:T(8,128)S(1)}, u32[]{:S(2)}, u32[]{:S(2)}) collective-permute-start(f32[3,32,256]{2,1,0:T(8,128)S(1)} %get-tuple-element.39), channel_id=1, source_target_pairs={{0,0},{64,128},{128,64},{192,192},{1,1},{65,129},{129,65},{193,193... | collective-permute-start | bytes 294920 | tf_op jit(solution)/shard_map/ppermute | solution.py:980
  61.2 0.1 collective-permute-done.4.one_in
  61.2 3.5 %collective-permute-done.5.other_in = f32[3,32,256]{2,1,0:T(8,128)S(1)} collective-permute-done((f32[3,32,256]{2,1,0:T(8,128)S(1)}, f32[3,32,256]{2,1,0:T(8,128)S(1)}, u32[]{:S(2)}, u32[]{:S(2)}) %collective-permute-start.5) | collective-permute-done | bytes 98336 | tf_op jit(solution)/shard_map/ppermute | solution.py:980
  64.7 0.2 axial_filter.1
  65.0 0.1 collective-permute-start.6
  65.1 2.9 %collective-permute-start.7 = (f32[3,16,256]{2,1,0:T(8,128)S(1)}, f32[3,16,256]{2,1,0:T(8,128)S(1)}, u32[]{:S(2)}, u32[]{:S(2)}) collective-permute-start(f32[3,16,256]{2,1,0:T(8,128)S(1)} %get-tuple-element.42), channel_id=1, source_target_pairs={{0,0},{8,16},{16,8},{24,32},{32,24},{40,48},{48,40},{56,56},{1,1},... | collective-permute-start | bytes 147464 | tf_op jit(solution)/shard_map/ppermute | solution.py:980
  68.0 0.0 collective-permute-done.6.one_in
  68.0 2.5 %collective-permute-done.7.other_in = f32[3,16,256]{2,1,0:T(8,128)S(1)} collective-permute-done((f32[3,16,256]{2,1,0:T(8,128)S(1)}, f32[3,16,256]{2,1,0:T(8,128)S(1)}, u32[]{:S(2)}, u32[]{:S(2)}) %collective-permute-start.7) | collective-permute-done | bytes 49184 | tf_op jit(solution)/shard_map/ppermute | solution.py:980
  70.5 0.5 radial_filter.1
  71.0 1.6 %collective-permute-start.8 = (f32[8,128]{1,0:T(8,128)S(1)}, f32[8,128]{1,0:T(8,128)S(1)}, u32[]{:S(2)}, u32[]{:S(2)}) collective-permute-start(f32[8,128]{1,0:T(8,128)S(1)} %get-tuple-element.44), channel_id=1, source_target_pairs={{0,1},{1,0},{2,3},{3,2},{4,5},{5,4},{6,7},{7,6},{8,9},{9,8},{10,11... | collective-permute-start | bytes 12296 | tf_op jit(solution)/shard_map/ppermute | solution.py:980
  72.6 4.7 %collective-permute-start.9 = (f32[8,128]{1,0:T(8,128)S(1)}, f32[8,128]{1,0:T(8,128)S(1)}, u32[]{:S(2)}, u32[]{:S(2)}) collective-permute-start(f32[8,128]{1,0:T(8,128)S(1)} %get-tuple-element.45), channel_id=1, source_target_pairs={{0,7},{1,2},{2,1},{3,4},{4,3},{5,6},{6,5},{7,0},{8,15},{9,10},{10,... | collective-permute-start | bytes 12296 | tf_op jit(solution)/shard_map/ppermute | solution.py:980
  77.3 0.5 inner_azimuthal_filter.1.inner_ref
  77.8 0.7 collective-permute-done.8.one_in
  78.5 3.7 %collective-permute-done.9.other_in = f32[8,128]{1,0:T(8,128)S(1)} collective-permute-done((f32[8,128]{1,0:T(8,128)S(1)}, f32[8,128]{1,0:T(8,128)S(1)}, u32[]{:S(2)}, u32[]{:S(2)}) %collective-permute-start.9) | collective-permute-done | bytes 4128 | tf_op jit(solution)/shard_map/ppermute | solution.py:980
  82.2 1.1 %azimuthal_filter.1 = f32[3,128,256]{2,1,0:T(8,128)} custom-call(f32[3,128,256]{2,1,0:T(8,128)S(1)} %inner_azimuthal_filter.1.inner_ref, f32[8,128]{1,0:T(8,128)S(1)} %collective-permute-done.8.one_in, f32[8,128]{1,0:T(8,128)S(1)} %collective-permute-done.9.other_in), custom_call_target="tpu_custom_call" | custom-call | tf_op jit(solution)/shard_map/azimuthal_filter/pallas_call | solution.py:964
Async XLA Ops:
  0.6 18.0 %copy-start = (s32[2,1,1,32768]{3,2,1,0:T(1,128)S(1)}, s32[2,1,1,32768]{3,2,1,0:T(1,128)}, u32[]{:S(2)}) copy-start(s32[2,1,1,32768]{3,2,1,0:T(1,128)} %param.11) | copy-start | bytes 786436
  9.3 13.2 %collective-permute-start = (f32[16,8,128]{2,1,0:T(8,128)S(1)}, f32[16,8,128]{2,1,0:T(8,128)S(1)}, u32[]{:S(2)}, u32[]{:S(2)}) collective-permute-start(f32[16,8,128]{2,1,0:T(8,128)S(1)} %get-tuple-element.31), channel_id=1, source_target_pairs={{0,1},{1,0},{2,3},{3,2},{4,5},{5,4},{6,7},{7,6},{8,9},{9,8},{10,11... | collective-permute-start | bytes 196616 | tf_op jit(solution)/shard_map/ppermute | solution.py:980
  15.7 11.5 %collective-permute-start.1 = (f32[16,8,128]{2,1,0:T(8,128)S(1)}, f32[16,8,128]{2,1,0:T(8,128)S(1)}, u32[]{:S(2)}, u32[]{:S(2)}) collective-permute-start(f32[16,8,128]{2,1,0:T(8,128)S(1)} %get-tuple-element.32), channel_id=1, source_target_pairs={{0,7},{1,2},{2,1},{3,4},{4,3},{5,6},{6,5},{7,0},{8,15},{9,10},{10,... | collective-permute-start | bytes 196616 | tf_op jit(solution)/shard_map/ppermute | solution.py:980
  33.2 16.9 %collective-permute-start.2 = (f32[3,16,128]{2,1,0:T(8,128)S(1)}, f32[3,16,128]{2,1,0:T(8,128)S(1)}, u32[]{:S(2)}, u32[]{:S(2)}) collective-permute-start(f32[3,16,128]{2,1,0:T(8,128)S(1)} %get-tuple-element.34), channel_id=1, source_target_pairs={{0,1},{1,0},{2,3},{3,2},{4,5},{5,4},{6,7},{7,6},{8,9},{9,8},{10,11... | collective-permute-start | bytes 73736 | tf_op jit(solution)/shard_map/ppermute | solution.py:980
  35.3 14.9 %collective-permute-start.3 = (f32[3,16,128]{2,1,0:T(8,128)S(1)}, f32[3,16,128]{2,1,0:T(8,128)S(1)}, u32[]{:S(2)}, u32[]{:S(2)}) collective-permute-start(f32[3,16,128]{2,1,0:T(8,128)S(1)} %get-tuple-element.35), channel_id=1, source_target_pairs={{0,7},{1,2},{2,1},{3,4},{4,3},{5,6},{6,5},{7,0},{8,15},{9,10},{10,... | collective-permute-start | bytes 73736 | tf_op jit(solution)/shard_map/ppermute | solution.py:980
  56.6 4.6 %collective-permute-start.4 = (f32[3,32,256]{2,1,0:T(8,128)S(1)}, f32[3,32,256]{2,1,0:T(8,128)S(1)}, u32[]{:S(2)}, u32[]{:S(2)}) collective-permute-start(f32[3,32,256]{2,1,0:T(8,128)S(1)} %get-tuple-element.38), channel_id=1, source_target_pairs={{0,64},{64,0},{128,192},{192,128},{1,65},{65,1},{129,193},{193,129... | collective-permute-start | bytes 294920 | tf_op jit(solution)/shard_map/ppermute | solution.py:980
  58.2 6.5 %collective-permute-start.5 = (f32[3,32,256]{2,1,0:T(8,128)S(1)}, f32[3,32,256]{2,1,0:T(8,128)S(1)}, u32[]{:S(2)}, u32[]{:S(2)}) collective-permute-start(f32[3,32,256]{2,1,0:T(8,128)S(1)} %get-tuple-element.39), channel_id=1, source_target_pairs={{0,0},{64,128},{128,64},{192,192},{1,1},{65,129},{129,65},{193,193... | collective-permute-start | bytes 294920 | tf_op jit(solution)/shard_map/ppermute | solution.py:980
  65.0 3.0 %collective-permute-start.6 = (f32[3,16,256]{2,1,0:T(8,128)S(1)}, f32[3,16,256]{2,1,0:T(8,128)S(1)}, u32[]{:S(2)}, u32[]{:S(2)}) collective-permute-start(f32[3,16,256]{2,1,0:T(8,128)S(1)} %get-tuple-element.41), channel_id=1, source_target_pairs={{0,8},{8,0},{16,24},{24,16},{32,40},{40,32},{48,56},{56,48},{1,9},... | collective-permute-start | bytes 147464 | tf_op jit(solution)/shard_map/ppermute | solution.py:980
  65.1 5.4 %collective-permute-start.7 = (f32[3,16,256]{2,1,0:T(8,128)S(1)}, f32[3,16,256]{2,1,0:T(8,128)S(1)}, u32[]{:S(2)}, u32[]{:S(2)}) collective-permute-start(f32[3,16,256]{2,1,0:T(8,128)S(1)} %get-tuple-element.42), channel_id=1, source_target_pairs={{0,0},{8,16},{16,8},{24,32},{32,24},{40,48},{48,40},{56,56},{1,1},... | collective-permute-start | bytes 147464 | tf_op jit(solution)/shard_map/ppermute | solution.py:980
  71.0 7.6 %collective-permute-start.8 = (f32[8,128]{1,0:T(8,128)S(1)}, f32[8,128]{1,0:T(8,128)S(1)}, u32[]{:S(2)}, u32[]{:S(2)}) collective-permute-start(f32[8,128]{1,0:T(8,128)S(1)} %get-tuple-element.44), channel_id=1, source_target_pairs={{0,1},{1,0},{2,3},{3,2},{4,5},{5,4},{6,7},{7,6},{8,9},{9,8},{10,11... | collective-permute-start | bytes 12296 | tf_op jit(solution)/shard_map/ppermute | solution.py:980
  72.6 9.6 %collective-permute-start.9 = (f32[8,128]{1,0:T(8,128)S(1)}, f32[8,128]{1,0:T(8,128)S(1)}, u32[]{:S(2)}, u32[]{:S(2)}) collective-permute-start(f32[8,128]{1,0:T(8,128)S(1)} %get-tuple-element.45), channel_id=1, source_target_pairs={{0,7},{1,2},{2,1},{3,4},{4,3},{5,6},{6,5},{7,0},{8,15},{9,10},{10,... | collective-permute-start | bytes 12296 | tf_op jit(solution)/shard_map/ppermute | solution.py:980

commit v7 on v4

--- a/solution.py
+++ b/solution.py
@@ -342,9 +342,9 @@
         gas_rest(gather[0], ends, gas_rows, gather[1])
 
 
-def states_kernel(
+def edge_states_kernel(
     cell_hbm, gas_hbm, pos_hbm, vel_hbm, diam_hbm,
-    keys_ref, ends_ref, table_ref, words_ref, largest_ref, one_ref, other_ref,
+    keys_ref, ends_ref, edges_ref, one_ref, other_ref,
     cell_ref, gas_ref, pos_ref, vel_ref, diam_ref,
     gas_rows, iota, ends, idx_a, found_a, val_a, idx_b, found_b, val_b, sems,
 ):
@@ -386,23 +386,54 @@
         states_step, keys_ref=keys_ref, ends=ends, gas_rows=gas_rows, iota=iota,
         arrays=(pos_ref, vel_ref, diam_ref),
     )
+    whole = slice(0, 16)
     step((0, a), None)
+    step((7, b), (0, a, edges_ref.at[0], whole))
+    step(None, (7, b, edges_ref.at[1], whole))
+    one_ref[...], other_ref[...] = by_partner("az", edges_ref[0], edges_ref[1])
+
+
+def inner_states_kernel(
+    live_ref, ends, pairs_ref, keys_ref, edges_ref, gas_hbm, pos_hbm, vel_hbm, diam_hbm,
+    pair_keys_ref, pair_ends_ref, table_ref, words_ref, largest_ref,
+    gas_ref, pos_ref, vel_ref, diam_ref,
+    gas_rows, iota, idx_a, found_a, val_a, idx_b, found_b, val_b, sems,
+):
+    sources = (gas_hbm, pos_hbm, vel_hbm, diam_hbm)
+    places = (gas_ref, pos_ref, vel_ref, diam_ref)
+    copies = [
+        pltpu.make_async_copy(x, y, sems.at[n]) for n, (x, y) in enumerate(zip(sources, places))
+    ]
+    for copy in copies:
+        copy.start()
+    pair_sort(live_ref, pairs_ref, pair_keys_ref, pair_ends_ref)
+    for copy in copies:
+        copy.wait()
+    fill_gas_rows(gas_ref, gas_rows)
+    fill_iota(iota)
+    a, b = (idx_a, found_a, val_a), (idx_b, found_b, val_b)
+    step = functools.partial(
+        states_step, keys_ref=keys_ref, ends=ends, gas_rows=gas_rows, iota=iota,
+        arrays=(pos_ref, vel_ref, diam_ref),
+    )
+    table_ref[0:16] = edges_ref[0]
+    table_ref[112:128] = edges_ref[1]
+    step((1, a), None)
 
     def two(k, carry):
-        block = 2 * k
+        block = 2 * k + 1
         step((block + 1, b), (block, a, table_ref, rows_of(block)))
         step((block + 2, a), (block + 1, b, table_ref, rows_of(block + 1)))
         return carry
 
-    lax.fori_loop(0, 3, two, 0)
-    step((7, b), (6, a, table_ref, rows_of(6)))
-    step(None, (7, b, table_ref, rows_of(7)))
+    lax.fori_loop(0, 2, two, 0)
+    step((6, b), (5, a, table_ref, rows_of(5)))
+    step(None, (6, b, table_ref, rows_of(6)))
     largest = largest_slip(table_ref, 128)
     largest_ref[...] = largest
     for n in range(16):
         code_rows(table_ref, n, largest, words_ref)
     words_ref[512:576, :] = jnp.zeros((64, LANES), jnp.int32)
-    one_ref[...], other_ref[...] = by_partner("az", table_ref[0:16], table_ref[112:128])
 
 
 def slots(rows, parts, dtype=jnp.float32):
@@ -410,18 +441,20 @@
     return one + one
 
 
-def droplet_states(cells, gas, pos, vel, diam):
+def in_hbm(arrays):
+    return [pltpu.with_memory_space_constraint(x, pltpu.HBM) for x in arrays]
+
+
+def edge_states(cells, gas, pos, vel, diam):
     f32, i32 = jnp.float32, jnp.int32
     arrays = (cells, gas, pos, vel, diam)
     return pl.pallas_call(
-        states_kernel,
-        name="droplet_states",
+        edge_states_kernel,
+        name="edge_states",
         out_shape=(
             jax.ShapeDtypeStruct((128, LANES), i32),
             jax.ShapeDtypeStruct((ROWS, LANES), i32),
-            jax.ShapeDtypeStruct((128, ROWS, LANES), f32),
-            jax.ShapeDtypeStruct((576, LANES), i32),
-            jax.ShapeDtypeStruct((ROWS, LANES), f32),
+            jax.ShapeDtypeStruct((2, 16, ROWS, LANES), f32),
             jax.ShapeDtypeStruct((16, ROWS, LANES), f32),
             jax.ShapeDtypeStruct((16, ROWS, LANES), f32),
         ),
@@ -431,10 +464,32 @@
         + slots(16, 11)
         + [pltpu.SemaphoreType.DMA((6,))],
         compiler_params=params(),
-    )(*[pltpu.with_memory_space_constraint(x, pltpu.HBM) for x in arrays])
-
-
-def pair_sort_kernel(live_ref, pairs_ref, keys_ref, ends_ref):
+    )(*in_hbm(arrays))
+
+
+def inner_states(live, ends, pairs, keys, edges, *arrays):
+    f32, i32 = jnp.float32, jnp.int32
+    smem, vmem = pl.BlockSpec(memory_space=SMEM), pl.BlockSpec(memory_space=VMEM)
+    return pl.pallas_call(
+        inner_states_kernel,
+        name="inner_states",
+        out_shape=(
+            jax.ShapeDtypeStruct((2, LANES, LANES), i32),
+            jax.ShapeDtypeStruct((16, LANES), i32),
+            jax.ShapeDtypeStruct((128, ROWS, LANES), f32),
+            jax.ShapeDtypeStruct((576, LANES), i32),
+            jax.ShapeDtypeStruct((ROWS, LANES), f32),
+        ),
+        in_specs=[smem, smem, vmem, vmem, vmem] + [pl.BlockSpec(memory_space=pltpu.HBM)] * 4,
+        scratch_shapes=[VMEM(x.shape, x.dtype) for x in arrays]
+        + [VMEM((144, ROWS, LANES), f32), VMEM((LANES, LANES), jnp.bfloat16)]
+        + slots(16, 11)
+        + [pltpu.SemaphoreType.DMA((4,))],
+        compiler_params=params(),
+    )(live, ends, pairs, keys, edges, *in_hbm(arrays))
+
+
+def pair_sort(live_ref, pairs_ref, keys_ref, ends_ref):
     live = live_ref[0, 0]
     sub = lax.broadcasted_iota(jnp.int32, (ROWS, LANES), 0)
     lane = lax.broadcasted_iota(jnp.int32, (ROWS, LANES), 1)
@@ -484,19 +539,6 @@
             row = 4 * half + n
             bound = (LANES, LANES, BUCKETS, BUCKETS)[n]
             ends_ref[row : row + 1, :] = jnp.minimum(reduce(x, axis=0, keepdims=True), bound)
-
-
-def pair_sort(live, pairs):
-    return pl.pallas_call(
-        pair_sort_kernel,
-        name="pair_sort",
-        out_shape=(
-            jax.ShapeDtypeStruct((2, LANES, LANES), jnp.int32),
-            jax.ShapeDtypeStruct((16, LANES), jnp.int32),
-        ),
-        in_specs=[pl.BlockSpec(memory_space=SMEM), pl.BlockSpec(memory_space=VMEM)],
-        compiler_params=params(),
-    )(live, pairs)
 
 
 def group_ends(g, ends, part):
@@ -990,11 +1032,12 @@
     pos = positions.reshape(3, 128, LANES)
     vel = velocity.reshape(3, 128, LANES)
     diam = diameter.reshape(128, LANES)
-    cell_keys, cell_ends, table, words, largest, one, other = droplet_states(
-        cells, gas, pos, vel, diam
-    )
+    cell_keys, cell_ends, edges, one, other = edge_states(cells, gas, pos, vel, diam)
     one, other = swapped(one, other, "az", True)
-    pair_keys, pair_ends = pair_sort(live, pair_list.reshape(2, 256, LANES))
+    pairs = pair_list.reshape(2, 256, LANES)
+    pair_keys, pair_ends, table, words, largest = inner_states(
+        live, cell_ends, pairs, cell_keys, edges, gas, pos, vel, diam
+    )
     heads, one, other = near_pairs(pair_ends, pair_keys, words, largest, one, other)
     one, other = swapped(one, other, "az", True)
     corr = own_pairs(live, pair_ends, pair_keys, words, largest, heads)

time: 81 us -> 81.7 us (level)
  waiting for transfers between devices: 13.8 us -> 11.8 us
  Pallas kernels: 36.2 us -> 37.9 us
  starting transfers between devices: 28.7 us -> 30.2 us
    ppermute x10, waiting for transfers between devices: 13.8 us -> 11.8 us  [swapped(): lax.ppermute(x, axis, [(i, partner(i, odd)) for i in range(count)])]
    pallas_call x2, Pallas kernels: 12.4 us -> 14.3 us  [the longest x1 9.92 us: inner_states(): pl.pallas_call(inner_states_kernel, name='inner_states', out_shape=(jax.S...]
    ppermute x10, starting transfers between devices: 28.7 us -> 30.2 us  [swapped(): lax.ppermute(x, axis, [(i, partner(i, odd)) for i in range(count)])]
  transfers between devices with their start and end apart: 10 -> 10, of which waited for: 5 -> 4; matrix products, arithmetic and copies ran while one was open for 0% -> 0% of each run, Pallas kernels for 16% -> 23%
where the time goes in v7:
time: 81.7 us; the launch traced here: 81.2 us
  Pallas kernels  37.9 us (46%)
  starting transfers between devices  30.2 us (37%)
  waiting for transfers between devices  11.8 us (14%)
  between operations  1.41 us (2%)
    ppermute x10, starting transfers between devices, swapped(): lax.ppermute(x, axis, [(i, partner(i, odd)) for i in range(count)])  30.2 us
    ppermute x10, waiting for transfers between devices, swapped(): lax.ppermute(x, axis, [(i, partner(i, odd)) for i in range(count)])  11.8 us
    pallas_call x1, Pallas kernels, inner_states(): pl.pallas_call(inner_states_kernel, name='inner_states', out_shape=(jax.S...  9.92 us
    pallas_call x1, Pallas kernels, own_pairs(): pl.pallas_call(own_pairs_kernel, name='own_pairs', out_shape=jax.ShapeDty...  8.61 us
    pallas_call x1, Pallas kernels, near_pairs(): pl.pallas_call(near_pairs_kernel, name='near_pairs', out_shape=(jax.Shape...  6.99 us
    pallas_call x1, Pallas kernels, deposits(): pl.pallas_call(deposit_kernel, name='deposits', out_shape=(jax.ShapeDtype...  5.67 us
    pallas_call x1, Pallas kernels, edge_states(): pl.pallas_call(edge_states_kernel, name='edge_states', out_shape=(jax.Sha...  4.34 us
  transfers between devices with their start and end apart: 10, of which 4 were waited for; matrix products, arithmetic and copies ran while one was open for 0% of the time, Pallas kernels for 23%

profile of v7, /device:TPU:40, one launch (start us, length us, event | category | flops | bytes accessed | tf_op | source)
XLA Modules:
  0.0 81.2 jit_solution(7520610854284823056)
XLA Ops:
  0.6 0.0 copy-start
  0.6 4.3 %edge_states.1 = (s32[128,128]{1,0:T(8,128)S(1)}, s32[8,128]{1,0:T(8,128)S(1)}, f32[2,16,8,128]{3,2,1,0:T(8,128)S(1)}, f32[16,8,128]{2,1,0:T(8,128)S(1)}, f32[16,8,128]{2,1,0:T(8,128)S(1)}) custom-call(s32[128,128]{1,0:T(8,128)} %bitcast.21, f32[3,128,256]{2,1,0:T(8,128)} %bitcast.12, f32[3,128,128]{2,1,0:T(8,128)} %bitcast.14, f32[3,128,128]{2,1,0:T(8,128)} %bitcast.16, ...), custom_call_target="tpu_custom_call" | custom-call | tf_op jit(solution)/shard_map/edge_states/pallas_call | solution.py:451
  5.0 6.4 %collective-permute-start = (f32[16,8,128]{2,1,0:T(8,128)S(1)}, f32[16,8,128]{2,1,0:T(8,128)S(1)}, u32[]{:S(2)}, u32[]{:S(2)}) collective-permute-start(f32[16,8,128]{2,1,0:T(8,128)S(1)} %get-tuple-element.33), channel_id=1, source_target_pairs={{0,1},{1,0},{2,3},{3,2},{4,5},{5,4},{6,7},{7,6},{8,9},{9,8},{10,11... | collective-permute-start | bytes 196616 | tf_op jit(solution)/shard_map/ppermute | solution.py:1023
  11.4 2.3 %collective-permute-start.1 = (f32[16,8,128]{2,1,0:T(8,128)S(1)}, f32[16,8,128]{2,1,0:T(8,128)S(1)}, u32[]{:S(2)}, u32[]{:S(2)}) collective-permute-start(f32[16,8,128]{2,1,0:T(8,128)S(1)} %get-tuple-element.34), channel_id=1, source_target_pairs={{0,7},{1,2},{2,1},{3,4},{4,3},{5,6},{6,5},{7,0},{8,15},{9,10},{10,... | collective-permute-start | bytes 196616 | tf_op jit(solution)/shard_map/ppermute | solution.py:1023
  14.3 0.0 copy-done
  14.3 9.9 %inner_states.1 = (s32[2,128,128]{2,1,0:T(8,128)S(1)}, s32[16,128]{1,0:T(8,128)S(1)}, f32[128,8,128]{2,1,0:T(8,128)S(1)}, s32[576,128]{1,0:T(8,128)S(1)}, f32[8,128]{1,0:T(8,128)S(1)}) custom-call(s32[1,1]{1,0:T(1,128)} %bitcast.9.live_ref, s32[8,128]{1,0:T(8,128)S(1)} %get-tuple-element.25.ends, s32[2,256,128]{2,1,0:T(8,128)S(1)} %bitcast.11, ...), custom_call_target="tpu_custom_call" | custom-call | tf_op jit(solution)/shard_map/inner_states/pallas_call | solution.py:473
  24.3 0.0 collective-permute-done.one_in
  24.3 0.0 collective-permute-done.1.other_in
  24.3 7.0 %near_pairs.1 = (f32[3,128,128]{2,1,0:T(8,128)S(1)}, f32[3,16,128]{2,1,0:T(8,128)S(1)}, f32[3,16,128]{2,1,0:T(8,128)S(1)}) custom-call(s32[16,128]{1,0:T(8,128)S(1)} %get-tuple-element.29.ends, s32[2,128,128]{2,1,0:T(8,128)S(1)} %get-tuple-element.30.keys_ref, s32[576,128]{1,0:T(8,128)S(1)} %get-tuple-element.31.words_ref, ...), custom_call_target="tpu_custom_call" | custom-call | tf_op jit(solution)/shard_map/near_pairs/pallas_call | solution.py:741
  31.3 4.6 %collective-permute-start.2 = (f32[3,16,128]{2,1,0:T(8,128)S(1)}, f32[3,16,128]{2,1,0:T(8,128)S(1)}, u32[]{:S(2)}, u32[]{:S(2)}) collective-permute-start(f32[3,16,128]{2,1,0:T(8,128)S(1)} %get-tuple-element.36), channel_id=1, source_target_pairs={{0,1},{1,0},{2,3},{3,2},{4,5},{5,4},{6,7},{7,6},{8,9},{9,8},{10,11... | collective-permute-start | bytes 73736 | tf_op jit(solution)/shard_map/ppermute | solution.py:1023
  35.9 1.3 %collective-permute-start.3 = (f32[3,16,128]{2,1,0:T(8,128)S(1)}, f32[3,16,128]{2,1,0:T(8,128)S(1)}, u32[]{:S(2)}, u32[]{:S(2)}) collective-permute-start(f32[3,16,128]{2,1,0:T(8,128)S(1)} %get-tuple-element.37), channel_id=1, source_target_pairs={{0,7},{1,2},{2,1},{3,4},{4,3},{5,6},{6,5},{7,0},{8,15},{9,10},{10,... | collective-permute-start | bytes 73736 | tf_op jit(solution)/shard_map/ppermute | solution.py:1023
  37.2 8.6 %own_pairs.1.corr_ref = f32[3,128,128]{2,1,0:T(8,128)S(1)} custom-call(s32[1,1]{1,0:T(1,128)} %bitcast.10.live_ref, s32[16,128]{1,0:T(8,128)S(1)} %get-tuple-element.29.ends, s32[2,128,128]{2,1,0:T(8,128)S(1)} %get-tuple-element.30.keys_ref, s32[576,128]{1,0:T(8,128)S(1)} %get-tuple-element.31.words_ref, f32[8,128]{1,0:T(8,128)S(1)} %get-tuple-element.32.largest_ref, ...), custom_call_target="tpu_custom_call" | custom-call | tf_op jit(solution)/shard_map/own_pairs/pallas_call | solution.py:758
  45.8 0.0 collective-permute-done.2.one_in
  45.8 0.0 collective-permute-done.3.other_in
  45.8 5.7 %deposits.1 = (f32[3,128,256]{2,1,0:T(8,128)S(1)}, f32[3,128,128]{2,1,0:T(8,128)}, f32[3,32,256]{2,1,0:T(8,128)S(1)}, f32[3,32,256]{2,1,0:T(8,128)S(1)}) custom-call(s32[8,128]{1,0:T(8,128)S(1)} %get-tuple-element.25.ends, s32[128,128]{1,0:T(8,128)S(1)} %get-tuple-element.26.keys_ref, f32[128,8,128]{2,1,0:T(8,128)S(1)} %get-tuple-element.28.table_ref, ...), custom_call_target="tpu_custom_call" | custom-call | tf_op jit(solution)/shard_map/deposits/pallas_call | solution.py:888
  51.5 1.0 %collective-permute-start.4 = (f32[3,32,256]{2,1,0:T(8,128)S(1)}, f32[3,32,256]{2,1,0:T(8,128)S(1)}, u32[]{:S(2)}, u32[]{:S(2)}) collective-permute-start(f32[3,32,256]{2,1,0:T(8,128)S(1)} %get-tuple-element.40), channel_id=1, source_target_pairs={{0,64},{64,0},{128,192},{192,128},{1,65},{65,1},{129,193},{193,129... | collective-permute-start | bytes 294920 | tf_op jit(solution)/shard_map/ppermute | solution.py:1023
  52.5 5.8 %collective-permute-start.5 = (f32[3,32,256]{2,1,0:T(8,128)S(1)}, f32[3,32,256]{2,1,0:T(8,128)S(1)}, u32[]{:S(2)}, u32[]{:S(2)}) collective-permute-start(f32[3,32,256]{2,1,0:T(8,128)S(1)} %get-tuple-element.41), channel_id=1, source_target_pairs={{0,0},{64,128},{128,64},{192,192},{1,1},{65,129},{129,65},{193,193... | collective-permute-start | bytes 294920 | tf_op jit(solution)/shard_map/ppermute | solution.py:1023
  58.3 0.0 collective-permute-done.4.one_in
  58.3 2.6 %collective-permute-done.5.other_in = f32[3,32,256]{2,1,0:T(8,128)S(1)} collective-permute-done((f32[3,32,256]{2,1,0:T(8,128)S(1)}, f32[3,32,256]{2,1,0:T(8,128)S(1)}, u32[]{:S(2)}, u32[]{:S(2)}) %collective-permute-start.5) | collective-permute-done | bytes 98336 | tf_op jit(solution)/shard_map/ppermute | solution.py:1023
  60.9 0.2 axial_filter.1
  61.1 0.1 collective-permute-start.6
  61.2 1.9 %collective-permute-start.7 = (f32[3,16,256]{2,1,0:T(8,128)S(1)}, f32[3,16,256]{2,1,0:T(8,128)S(1)}, u32[]{:S(2)}, u32[]{:S(2)}) collective-permute-start(f32[3,16,256]{2,1,0:T(8,128)S(1)} %get-tuple-element.44), channel_id=1, source_target_pairs={{0,0},{8,16},{16,8},{24,32},{32,24},{40,48},{48,40},{56,56},{1,1},... | collective-permute-start | bytes 147464 | tf_op jit(solution)/shard_map/ppermute | solution.py:1023
  63.1 0.0 collective-permute-done.6.one_in
  63.1 3.5 %collective-permute-done.7.other_in = f32[3,16,256]{2,1,0:T(8,128)S(1)} collective-permute-done((f32[3,16,256]{2,1,0:T(8,128)S(1)}, f32[3,16,256]{2,1,0:T(8,128)S(1)}, u32[]{:S(2)}, u32[]{:S(2)}) %collective-permute-start.7) | collective-permute-done | bytes 49184 | tf_op jit(solution)/shard_map/ppermute | solution.py:1023
  66.6 0.5 radial_filter.1
  67.1 3.4 %collective-permute-start.8 = (f32[8,128]{1,0:T(8,128)S(1)}, f32[8,128]{1,0:T(8,128)S(1)}, u32[]{:S(2)}, u32[]{:S(2)}) collective-permute-start(f32[8,128]{1,0:T(8,128)S(1)} %get-tuple-element.46), channel_id=1, source_target_pairs={{0,1},{1,0},{2,3},{3,2},{4,5},{5,4},{6,7},{7,6},{8,9},{9,8},{10,11... | collective-permute-start | bytes 12296 | tf_op jit(solution)/shard_map/ppermute | solution.py:1023
  70.5 3.4 %collective-permute-start.9 = (f32[8,128]{1,0:T(8,128)S(1)}, f32[8,128]{1,0:T(8,128)S(1)}, u32[]{:S(2)}, u32[]{:S(2)}) collective-permute-start(f32[8,128]{1,0:T(8,128)S(1)} %get-tuple-element.47), channel_id=1, source_target_pairs={{0,7},{1,2},{2,1},{3,4},{4,3},{5,6},{6,5},{7,0},{8,15},{9,10},{10,... | collective-permute-start | bytes 12296 | tf_op jit(solution)/shard_map/ppermute | solution.py:1023
  73.9 0.5 inner_azimuthal_filter.1.inner_ref
  74.4 0.3 collective-permute-done.8.one_in
  74.7 5.4 %collective-permute-done.9.other_in = f32[8,128]{1,0:T(8,128)S(1)} collective-permute-done((f32[8,128]{1,0:T(8,128)S(1)}, f32[8,128]{1,0:T(8,128)S(1)}, u32[]{:S(2)}, u32[]{:S(2)}) %collective-permute-start.9) | collective-permute-done | bytes 4128 | tf_op jit(solution)/shard_map/ppermute | solution.py:1023
  80.1 1.1 %azimuthal_filter.1 = f32[3,128,256]{2,1,0:T(8,128)} custom-call(f32[3,128,256]{2,1,0:T(8,128)S(1)} %inner_azimuthal_filter.1.inner_ref, f32[8,128]{1,0:T(8,128)S(1)} %collective-permute-done.8.one_in, f32[8,128]{1,0:T(8,128)S(1)} %collective-permute-done.9.other_in), custom_call_target="tpu_custom_call" | custom-call | tf_op jit(solution)/shard_map/azimuthal_filter/pallas_call | solution.py:1007
Async XLA Ops:
  0.6 13.7 %copy-start = (s32[2,1,1,32768]{3,2,1,0:T(1,128)S(1)}, s32[2,1,1,32768]{3,2,1,0:T(1,128)}, u32[]{:S(2)}) copy-start(s32[2,1,1,32768]{3,2,1,0:T(1,128)} %param.11) | copy-start | bytes 786436
  5.0 19.3 %collective-permute-start = (f32[16,8,128]{2,1,0:T(8,128)S(1)}, f32[16,8,128]{2,1,0:T(8,128)S(1)}, u32[]{:S(2)}, u32[]{:S(2)}) collective-permute-start(f32[16,8,128]{2,1,0:T(8,128)S(1)} %get-tuple-element.33), channel_id=1, source_target_pairs={{0,1},{1,0},{2,3},{3,2},{4,5},{5,4},{6,7},{7,6},{8,9},{9,8},{10,11... | collective-permute-start | bytes 196616 | tf_op jit(solution)/shard_map/ppermute | solution.py:1023
  11.4 12.9 %collective-permute-start.1 = (f32[16,8,128]{2,1,0:T(8,128)S(1)}, f32[16,8,128]{2,1,0:T(8,128)S(1)}, u32[]{:S(2)}, u32[]{:S(2)}) collective-permute-start(f32[16,8,128]{2,1,0:T(8,128)S(1)} %get-tuple-element.34), channel_id=1, source_target_pairs={{0,7},{1,2},{2,1},{3,4},{4,3},{5,6},{6,5},{7,0},{8,15},{9,10},{10,... | collective-permute-start | bytes 196616 | tf_op jit(solution)/shard_map/ppermute | solution.py:1023
  31.3 14.5 %collective-permute-start.2 = (f32[3,16,128]{2,1,0:T(8,128)S(1)}, f32[3,16,128]{2,1,0:T(8,128)S(1)}, u32[]{:S(2)}, u32[]{:S(2)}) collective-permute-start(f32[3,16,128]{2,1,0:T(8,128)S(1)} %get-tuple-element.36), channel_id=1, source_target_pairs={{0,1},{1,0},{2,3},{3,2},{4,5},{5,4},{6,7},{7,6},{8,9},{9,8},{10,11... | collective-permute-start | bytes 73736 | tf_op jit(solution)/shard_map/ppermute | solution.py:1023
  35.9 9.9 %collective-permute-start.3 = (f32[3,16,128]{2,1,0:T(8,128)S(1)}, f32[3,16,128]{2,1,0:T(8,128)S(1)}, u32[]{:S(2)}, u32[]{:S(2)}) collective-permute-start(f32[3,16,128]{2,1,0:T(8,128)S(1)} %get-tuple-element.37), channel_id=1, source_target_pairs={{0,7},{1,2},{2,1},{3,4},{4,3},{5,6},{6,5},{7,0},{8,15},{9,10},{10,... | collective-permute-start | bytes 73736 | tf_op jit(solution)/shard_map/ppermute | solution.py:1023
  51.5 6.8 %collective-permute-start.4 = (f32[3,32,256]{2,1,0:T(8,128)S(1)}, f32[3,32,256]{2,1,0:T(8,128)S(1)}, u32[]{:S(2)}, u32[]{:S(2)}) collective-permute-start(f32[3,32,256]{2,1,0:T(8,128)S(1)} %get-tuple-element.40), channel_id=1, source_target_pairs={{0,64},{64,0},{128,192},{192,128},{1,65},{65,1},{129,193},{193,129... | collective-permute-start | bytes 294920 | tf_op jit(solution)/shard_map/ppermute | solution.py:1023
  52.5 8.4 %collective-permute-start.5 = (f32[3,32,256]{2,1,0:T(8,128)S(1)}, f32[3,32,256]{2,1,0:T(8,128)S(1)}, u32[]{:S(2)}, u32[]{:S(2)}) collective-permute-start(f32[3,32,256]{2,1,0:T(8,128)S(1)} %get-tuple-element.41), channel_id=1, source_target_pairs={{0,0},{64,128},{128,64},{192,192},{1,1},{65,129},{129,65},{193,193... | collective-permute-start | bytes 294920 | tf_op jit(solution)/shard_map/ppermute | solution.py:1023
  61.1 2.0 %collective-permute-start.6 = (f32[3,16,256]{2,1,0:T(8,128)S(1)}, f32[3,16,256]{2,1,0:T(8,128)S(1)}, u32[]{:S(2)}, u32[]{:S(2)}) collective-permute-start(f32[3,16,256]{2,1,0:T(8,128)S(1)} %get-tuple-element.43), channel_id=1, source_target_pairs={{0,8},{8,0},{16,24},{24,16},{32,40},{40,32},{48,56},{56,48},{1,9},... | collective-permute-start | bytes 147464 | tf_op jit(solution)/shard_map/ppermute | solution.py:1023
  61.2 5.4 %collective-permute-start.7 = (f32[3,16,256]{2,1,0:T(8,128)S(1)}, f32[3,16,256]{2,1,0:T(8,128)S(1)}, u32[]{:S(2)}, u32[]{:S(2)}) collective-permute-start(f32[3,16,256]{2,1,0:T(8,128)S(1)} %get-tuple-element.44), channel_id=1, source_target_pairs={{0,0},{8,16},{16,8},{24,32},{32,24},{40,48},{48,40},{56,56},{1,1},... | collective-permute-start | bytes 147464 | tf_op jit(solution)/shard_map/ppermute | solution.py:1023
  67.1 7.6 %collective-permute-start.8 = (f32[8,128]{1,0:T(8,128)S(1)}, f32[8,128]{1,0:T(8,128)S(1)}, u32[]{:S(2)}, u32[]{:S(2)}) collective-permute-start(f32[8,128]{1,0:T(8,128)S(1)} %get-tuple-element.46), channel_id=1, source_target_pairs={{0,1},{1,0},{2,3},{3,2},{4,5},{5,4},{6,7},{7,6},{8,9},{9,8},{10,11... | collective-permute-start | bytes 12296 | tf_op jit(solution)/shard_map/ppermute | solution.py:1023
  70.5 9.6 %collective-permute-start.9 = (f32[8,128]{1,0:T(8,128)S(1)}, f32[8,128]{1,0:T(8,128)S(1)}, u32[]{:S(2)}, u32[]{:S(2)}) collective-permute-start(f32[8,128]{1,0:T(8,128)S(1)} %get-tuple-element.47), channel_id=1, source_target_pairs={{0,7},{1,2},{2,1},{3,4},{4,3},{5,6},{6,5},{7,0},{8,15},{9,10},{10,... | collective-permute-start | bytes 12296 | tf_op jit(solution)/shard_map/ppermute | solution.py:1023

commit v8 on v4

--- a/solution.py
+++ b/solution.py
@@ -344,7 +344,7 @@
 
 def states_kernel(
     cell_hbm, gas_hbm, pos_hbm, vel_hbm, diam_hbm,
-    keys_ref, ends_ref, table_ref, words_ref, largest_ref, one_ref, other_ref,
+    keys_ref, ends_ref, table_ref, one_ref, other_ref,
     cell_ref, gas_ref, pos_ref, vel_ref, diam_ref,
     gas_rows, iota, ends, idx_a, found_a, val_a, idx_b, found_b, val_b, sems,
 ):
@@ -365,7 +365,6 @@
         regs.append(cells[v * ROWS : (v + 1) * ROWS] * BLOCK + own)
     place = [("v", k) for k in range(4)] + [("s", k) for k in range(3)] + [("l", k) for k in range(4)]
     regs = sort_network(regs, place, 11)
-    keys_ref[...] = jnp.concatenate(regs, axis=0).T
     least = functools.reduce(jnp.minimum, regs)
     most = functools.reduce(jnp.maximum, regs)
     least = lax.shift_right_logical(jnp.min(least, axis=0, keepdims=True), 19)
@@ -375,6 +374,7 @@
     ends_ref[2:8, :] = running_max(most - least, 16)[0:6]
     copy = pltpu.make_async_copy(ends_ref, ends, sems.at[5])
     copy.start()
+    keys_ref[...] = jnp.concatenate(regs, axis=0).T
     copies[1].wait()
     fill_gas_rows(gas_ref, gas_rows)
     for other in copies[2:]:
@@ -397,11 +397,6 @@
     lax.fori_loop(0, 3, two, 0)
     step((7, b), (6, a, table_ref, rows_of(6)))
     step(None, (7, b, table_ref, rows_of(7)))
-    largest = largest_slip(table_ref, 128)
-    largest_ref[...] = largest
-    for n in range(16):
-        code_rows(table_ref, n, largest, words_ref)
-    words_ref[512:576, :] = jnp.zeros((64, LANES), jnp.int32)
     one_ref[...], other_ref[...] = by_partner("az", table_ref[0:16], table_ref[112:128])
 
 
@@ -420,8 +415,6 @@
             jax.ShapeDtypeStruct((128, LANES), i32),
             jax.ShapeDtypeStruct((ROWS, LANES), i32),
             jax.ShapeDtypeStruct((128, ROWS, LANES), f32),
-            jax.ShapeDtypeStruct((576, LANES), i32),
-            jax.ShapeDtypeStruct((ROWS, LANES), f32),
             jax.ShapeDtypeStruct((16, ROWS, LANES), f32),
             jax.ShapeDtypeStruct((16, ROWS, LANES), f32),
         ),
@@ -434,7 +427,12 @@
     )(*[pltpu.with_memory_space_constraint(x, pltpu.HBM) for x in arrays])
 
 
-def pair_sort_kernel(live_ref, pairs_ref, keys_ref, ends_ref):
+def pair_sort_kernel(live_ref, pairs_ref, table_ref, keys_ref, ends_ref, words_ref, largest_ref):
+    largest = largest_slip(table_ref, 128)
+    largest_ref[...] = largest
+    for n in range(16):
+        code_rows(table_ref, n, largest, words_ref)
+    words_ref[512:576, :] = jnp.zeros((64, LANES), jnp.int32)
     live = live_ref[0, 0]
     sub = lax.broadcasted_iota(jnp.int32, (ROWS, LANES), 0)
     lane = lax.broadcasted_iota(jnp.int32, (ROWS, LANES), 1)
@@ -486,17 +484,19 @@
             ends_ref[row : row + 1, :] = jnp.minimum(reduce(x, axis=0, keepdims=True), bound)
 
 
-def pair_sort(live, pairs):
+def pair_sort(live, pairs, table):
     return pl.pallas_call(
         pair_sort_kernel,
         name="pair_sort",
         out_shape=(
             jax.ShapeDtypeStruct((2, LANES, LANES), jnp.int32),
             jax.ShapeDtypeStruct((16, LANES), jnp.int32),
+            jax.ShapeDtypeStruct((576, LANES), jnp.int32),
+            jax.ShapeDtypeStruct((ROWS, LANES), jnp.float32),
         ),
-        in_specs=[pl.BlockSpec(memory_space=SMEM), pl.BlockSpec(memory_space=VMEM)],
+        in_specs=[pl.BlockSpec(memory_space=SMEM)] + [pl.BlockSpec(memory_space=VMEM)] * 2,
         compiler_params=params(),
-    )(live, pairs)
+    )(live, pairs, table)
 
 
 def group_ends(g, ends, part):
@@ -990,11 +990,12 @@
     pos = positions.reshape(3, 128, LANES)
     vel = velocity.reshape(3, 128, LANES)
     diam = diameter.reshape(128, LANES)
-    cell_keys, cell_ends, table, words, largest, one, other = droplet_states(
+    cell_keys, cell_ends, table, one, other = droplet_states(
         cells, gas, pos, vel, diam
     )
     one, other = swapped(one, other, "az", True)
-    pair_keys, pair_ends = pair_sort(live, pair_list.reshape(2, 256, LANES))
+    pairs = pair_list.reshape(2, 256, LANES)
+    pair_keys, pair_ends, words, largest = pair_sort(live, pairs, table)
     heads, one, other = near_pairs(pair_ends, pair_keys, words, largest, one, other)
     one, other = swapped(one, other, "az", True)
     corr = own_pairs(live, pair_ends, pair_keys, words, largest, heads)

time: 81 us -> 80.1 us (0.989)
  waiting for transfers between devices: 13.8 us -> 15.3 us
  starting transfers between devices: 28.7 us -> 27.5 us
    ppermute x10, waiting for transfers between devices: 13.8 us -> 15.3 us  [swapped(): lax.ppermute(x, axis, [(i, partner(i, odd)) for i in range(count)])]
    pallas_call x1, Pallas kernels: 8.53 us -> 7.28 us  [droplet_states(): pl.pallas_call(states_kernel, name='droplet_states', out_shape=(jax.Shape...]
    ppermute x10, starting transfers between devices: 28.7 us -> 27.5 us  [swapped(): lax.ppermute(x, axis, [(i, partner(i, odd)) for i in range(count)])]
    pallas_call x1, Pallas kernels: 3.85 us -> 5.03 us  [pair_sort(): pl.pallas_call(pair_sort_kernel, name='pair_sort', out_shape=(jax.ShapeDt...]
  transfers between devices with their start and end apart: 10 -> 10, of which waited for: 5 -> 6; matrix products, arithmetic and copies ran while one was open for 0% -> 0% of each run, Pallas kernels for 16% -> 18%
where the time goes in v8:
time: 80.1 us; the launch traced here: 79.6 us
  Pallas kernels  35.4 us (44%)
  starting transfers between devices  27.5 us (34%)
  waiting for transfers between devices  15.3 us (19%)
  between operations  1.4 us (2%)
    ppermute x10, starting transfers between devices, swapped(): lax.ppermute(x, axis, [(i, partner(i, odd)) for i in range(count)])  27.5 us
    ppermute x10, waiting for transfers between devices, swapped(): lax.ppermute(x, axis, [(i, partner(i, odd)) for i in range(count)])  15.3 us
    pallas_call x1, Pallas kernels, own_pairs(): pl.pallas_call(own_pairs_kernel, name='own_pairs', out_shape=jax.ShapeDty...  8.48 us
    pallas_call x1, Pallas kernels, droplet_states(): pl.pallas_call(states_kernel, name='droplet_states', out_shape=(jax.Shape...  7.28 us
    pallas_call x1, Pallas kernels, near_pairs(): pl.pallas_call(near_pairs_kernel, name='near_pairs', out_shape=(jax.Shape...  6.66 us
    pallas_call x1, Pallas kernels, deposits(): pl.pallas_call(deposit_kernel, name='deposits', out_shape=(jax.ShapeDtype...  5.66 us
    pallas_call x1, Pallas kernels, pair_sort(): pl.pallas_call(pair_sort_kernel, name='pair_sort', out_shape=(jax.ShapeDt...  5.03 us
  transfers between devices with their start and end apart: 10, of which 6 were waited for; matrix products, arithmetic and copies ran while one was open for 0% of the time, Pallas kernels for 18%

profile of v8, /device:TPU:40, one launch (start us, length us, event | category | flops | bytes accessed | tf_op | source)
XLA Modules:
  0.0 79.6 jit_solution(2665094333429961315)
XLA Ops:
  0.6 0.0 copy-start
  0.6 7.3 %droplet_states.1 = (s32[128,128]{1,0:T(8,128)S(1)}, s32[8,128]{1,0:T(8,128)S(1)}, f32[128,8,128]{2,1,0:T(8,128)S(1)}, f32[16,8,128]{2,1,0:T(8,128)S(1)}, f32[16,8,128]{2,1,0:T(8,128)S(1)}) custom-call(s32[128,128]{1,0:T(8,128)} %bitcast.16, f32[3,128,256]{2,1,0:T(8,128)} %bitcast.12, f32[3,128,128]{2,1,0:T(8,128)} %bitcast.14, f32[3,128,128]{2,1,0:T(8,128)} %bitcast.15, ...), custom_call_target="tpu_custom_call" | custom-call | tf_op jit(solution)/shard_map/droplet_states/pallas_call | solution.py:411
  7.9 6.4 %collective-permute-start = (f32[16,8,128]{2,1,0:T(8,128)S(1)}, f32[16,8,128]{2,1,0:T(8,128)S(1)}, u32[]{:S(2)}, u32[]{:S(2)}) collective-permute-start(f32[16,8,128]{2,1,0:T(8,128)S(1)} %get-tuple-element.31), channel_id=1, source_target_pairs={{0,1},{1,0},{2,3},{3,2},{4,5},{5,4},{6,7},{7,6},{8,9},{9,8},{10,11... | collective-permute-start | bytes 196616 | tf_op jit(solution)/shard_map/ppermute | solution.py:981
  14.3 2.3 %collective-permute-start.1 = (f32[16,8,128]{2,1,0:T(8,128)S(1)}, f32[16,8,128]{2,1,0:T(8,128)S(1)}, u32[]{:S(2)}, u32[]{:S(2)}) collective-permute-start(f32[16,8,128]{2,1,0:T(8,128)S(1)} %get-tuple-element.32), channel_id=1, source_target_pairs={{0,7},{1,2},{2,1},{3,4},{4,3},{5,6},{6,5},{7,0},{8,15},{9,10},{10,... | collective-permute-start | bytes 196616 | tf_op jit(solution)/shard_map/ppermute | solution.py:981
  17.3 0.0 copy-done
  17.3 5.0 %pair_sort.1 = (s32[2,128,128]{2,1,0:T(8,128)S(1)}, s32[16,128]{1,0:T(8,128)S(1)}, s32[576,128]{1,0:T(8,128)S(1)}, f32[8,128]{1,0:T(8,128)S(1)}) custom-call(s32[1,1]{1,0:T(1,128)} %bitcast.9.live_ref, s32[2,256,128]{2,1,0:T(8,128)S(1)} %bitcast.11, f32[128,8,128]{2,1,0:T(8,128)S(1)} %get-tuple-element.26.table_ref), custom_call_target="tpu_custom_call" | custom-call | tf_op jit(solution)/shard_map/pair_sort/pallas_call | solution.py:488
  22.3 0.0 collective-permute-done.one_in
  22.3 3.5 %collective-permute-done.1.other_in = f32[16,8,128]{2,1,0:T(8,128)S(1)} collective-permute-done((f32[16,8,128]{2,1,0:T(8,128)S(1)}, f32[16,8,128]{2,1,0:T(8,128)S(1)}, u32[]{:S(2)}, u32[]{:S(2)}) %collective-permute-start.1) | collective-permute-done | bytes 65568 | tf_op jit(solution)/shard_map/ppermute | solution.py:981
  25.8 6.7 %near_pairs.1 = (f32[3,128,128]{2,1,0:T(8,128)S(1)}, f32[3,16,128]{2,1,0:T(8,128)S(1)}, f32[3,16,128]{2,1,0:T(8,128)S(1)}) custom-call(s32[16,128]{1,0:T(8,128)S(1)} %get-tuple-element.27.ends, s32[2,128,128]{2,1,0:T(8,128)S(1)} %get-tuple-element.28.keys_ref, s32[576,128]{1,0:T(8,128)S(1)} %get-tuple-element.29.words_ref, ...), custom_call_target="tpu_custom_call" | custom-call | tf_op jit(solution)/shard_map/near_pairs/pallas_call | solution.py:699
  32.4 1.9 %collective-permute-start.2 = (f32[3,16,128]{2,1,0:T(8,128)S(1)}, f32[3,16,128]{2,1,0:T(8,128)S(1)}, u32[]{:S(2)}, u32[]{:S(2)}) collective-permute-start(f32[3,16,128]{2,1,0:T(8,128)S(1)} %get-tuple-element.34), channel_id=1, source_target_pairs={{0,1},{1,0},{2,3},{3,2},{4,5},{5,4},{6,7},{7,6},{8,9},{9,8},{10,11... | collective-permute-start | bytes 73736 | tf_op jit(solution)/shard_map/ppermute | solution.py:981
  34.3 4.1 %collective-permute-start.3 = (f32[3,16,128]{2,1,0:T(8,128)S(1)}, f32[3,16,128]{2,1,0:T(8,128)S(1)}, u32[]{:S(2)}, u32[]{:S(2)}) collective-permute-start(f32[3,16,128]{2,1,0:T(8,128)S(1)} %get-tuple-element.35), channel_id=1, source_target_pairs={{0,7},{1,2},{2,1},{3,4},{4,3},{5,6},{6,5},{7,0},{8,15},{9,10},{10,... | collective-permute-start | bytes 73736 | tf_op jit(solution)/shard_map/ppermute | solution.py:981
  38.4 8.5 %own_pairs.1.corr_ref = f32[3,128,128]{2,1,0:T(8,128)S(1)} custom-call(s32[1,1]{1,0:T(1,128)} %bitcast.10.live_ref, s32[16,128]{1,0:T(8,128)S(1)} %get-tuple-element.27.ends, s32[2,128,128]{2,1,0:T(8,128)S(1)} %get-tuple-element.28.keys_ref, s32[576,128]{1,0:T(8,128)S(1)} %get-tuple-element.29.words_ref, f32[8,128]{1,0:T(8,128)S(1)} %get-tuple-element.30.largest_ref, ...), custom_call_target="tpu_custom_call" | custom-call | tf_op jit(solution)/shard_map/own_pairs/pallas_call | solution.py:716
  46.9 0.0 collective-permute-done.2.one_in
  46.9 0.0 collective-permute-done.3.other_in
  46.9 5.7 %deposits.1 = (f32[3,128,256]{2,1,0:T(8,128)S(1)}, f32[3,128,128]{2,1,0:T(8,128)}, f32[3,32,256]{2,1,0:T(8,128)S(1)}, f32[3,32,256]{2,1,0:T(8,128)S(1)}) custom-call(s32[8,128]{1,0:T(8,128)S(1)} %get-tuple-element.24.ends, s32[128,128]{1,0:T(8,128)S(1)} %get-tuple-element.25.keys_ref, f32[128,8,128]{2,1,0:T(8,128)S(1)} %get-tuple-element.26.table_ref, ...), custom_call_target="tpu_custom_call" | custom-call | tf_op jit(solution)/shard_map/deposits/pallas_call | solution.py:846
  52.6 0.8 %collective-permute-start.4 = (f32[3,32,256]{2,1,0:T(8,128)S(1)}, f32[3,32,256]{2,1,0:T(8,128)S(1)}, u32[]{:S(2)}, u32[]{:S(2)}) collective-permute-start(f32[3,32,256]{2,1,0:T(8,128)S(1)} %get-tuple-element.38), channel_id=1, source_target_pairs={{0,64},{64,0},{128,192},{192,128},{1,65},{65,1},{129,193},{193,129... | collective-permute-start | bytes 294920 | tf_op jit(solution)/shard_map/ppermute | solution.py:981
  53.4 2.8 %collective-permute-start.5 = (f32[3,32,256]{2,1,0:T(8,128)S(1)}, f32[3,32,256]{2,1,0:T(8,128)S(1)}, u32[]{:S(2)}, u32[]{:S(2)}) collective-permute-start(f32[3,32,256]{2,1,0:T(8,128)S(1)} %get-tuple-element.39), channel_id=1, source_target_pairs={{0,0},{64,128},{128,64},{192,192},{1,1},{65,129},{129,65},{193,193... | collective-permute-start | bytes 294920 | tf_op jit(solution)/shard_map/ppermute | solution.py:981
  56.2 1.0 %collective-permute-done.4.one_in = f32[3,32,256]{2,1,0:T(8,128)S(1)} collective-permute-done((f32[3,32,256]{2,1,0:T(8,128)S(1)}, f32[3,32,256]{2,1,0:T(8,128)S(1)}, u32[]{:S(2)}, u32[]{:S(2)}) %collective-permute-start.4) | collective-permute-done | bytes 98336 | tf_op jit(solution)/shard_map/ppermute | solution.py:981
  57.2 2.7 %collective-permute-done.5.other_in = f32[3,32,256]{2,1,0:T(8,128)S(1)} collective-permute-done((f32[3,32,256]{2,1,0:T(8,128)S(1)}, f32[3,32,256]{2,1,0:T(8,128)S(1)}, u32[]{:S(2)}, u32[]{:S(2)}) %collective-permute-start.5) | collective-permute-done | bytes 98336 | tf_op jit(solution)/shard_map/ppermute | solution.py:981
  59.9 0.2 axial_filter.1
  60.1 0.1 collective-permute-start.6
  60.2 2.5 %collective-permute-start.7 = (f32[3,16,256]{2,1,0:T(8,128)S(1)}, f32[3,16,256]{2,1,0:T(8,128)S(1)}, u32[]{:S(2)}, u32[]{:S(2)}) collective-permute-start(f32[3,16,256]{2,1,0:T(8,128)S(1)} %get-tuple-element.42), channel_id=1, source_target_pairs={{0,0},{8,16},{16,8},{24,32},{32,24},{40,48},{48,40},{56,56},{1,1},... | collective-permute-start | bytes 147464 | tf_op jit(solution)/shard_map/ppermute | solution.py:981
  62.7 0.0 collective-permute-done.6.one_in
  62.7 2.9 %collective-permute-done.7.other_in = f32[3,16,256]{2,1,0:T(8,128)S(1)} collective-permute-done((f32[3,16,256]{2,1,0:T(8,128)S(1)}, f32[3,16,256]{2,1,0:T(8,128)S(1)}, u32[]{:S(2)}, u32[]{:S(2)}) %collective-permute-start.7) | collective-permute-done | bytes 49184 | tf_op jit(solution)/shard_map/ppermute | solution.py:981
  65.6 0.5 radial_filter.1
  66.1 2.7 %collective-permute-start.8 = (f32[8,128]{1,0:T(8,128)S(1)}, f32[8,128]{1,0:T(8,128)S(1)}, u32[]{:S(2)}, u32[]{:S(2)}) collective-permute-start(f32[8,128]{1,0:T(8,128)S(1)} %get-tuple-element.44), channel_id=1, source_target_pairs={{0,1},{1,0},{2,3},{3,2},{4,5},{5,4},{6,7},{7,6},{8,9},{9,8},{10,11... | collective-permute-start | bytes 12296 | tf_op jit(solution)/shard_map/ppermute | solution.py:981
  68.8 3.9 %collective-permute-start.9 = (f32[8,128]{1,0:T(8,128)S(1)}, f32[8,128]{1,0:T(8,128)S(1)}, u32[]{:S(2)}, u32[]{:S(2)}) collective-permute-start(f32[8,128]{1,0:T(8,128)S(1)} %get-tuple-element.45), channel_id=1, source_target_pairs={{0,7},{1,2},{2,1},{3,4},{4,3},{5,6},{6,5},{7,0},{8,15},{9,10},{10,... | collective-permute-start | bytes 12296 | tf_op jit(solution)/shard_map/ppermute | solution.py:981
  72.8 0.5 inner_azimuthal_filter.1.inner_ref
  73.3 0.4 collective-permute-done.8.one_in
  73.7 4.8 %collective-permute-done.9.other_in = f32[8,128]{1,0:T(8,128)S(1)} collective-permute-done((f32[8,128]{1,0:T(8,128)S(1)}, f32[8,128]{1,0:T(8,128)S(1)}, u32[]{:S(2)}, u32[]{:S(2)}) %collective-permute-start.9) | collective-permute-done | bytes 4128 | tf_op jit(solution)/shard_map/ppermute | solution.py:981
  78.5 1.1 %azimuthal_filter.1 = f32[3,128,256]{2,1,0:T(8,128)} custom-call(f32[3,128,256]{2,1,0:T(8,128)S(1)} %inner_azimuthal_filter.1.inner_ref, f32[8,128]{1,0:T(8,128)S(1)} %collective-permute-done.8.one_in, f32[8,128]{1,0:T(8,128)S(1)} %collective-permute-done.9.other_in), custom_call_target="tpu_custom_call" | custom-call | tf_op jit(solution)/shard_map/azimuthal_filter/pallas_call | solution.py:965
Async XLA Ops:
  0.6 16.6 %copy-start = (s32[2,1,1,32768]{3,2,1,0:T(1,128)S(1)}, s32[2,1,1,32768]{3,2,1,0:T(1,128)}, u32[]{:S(2)}) copy-start(s32[2,1,1,32768]{3,2,1,0:T(1,128)} %param.11) | copy-start | bytes 786436
  7.9 14.4 %collective-permute-start = (f32[16,8,128]{2,1,0:T(8,128)S(1)}, f32[16,8,128]{2,1,0:T(8,128)S(1)}, u32[]{:S(2)}, u32[]{:S(2)}) collective-permute-start(f32[16,8,128]{2,1,0:T(8,128)S(1)} %get-tuple-element.31), channel_id=1, source_target_pairs={{0,1},{1,0},{2,3},{3,2},{4,5},{5,4},{6,7},{7,6},{8,9},{9,8},{10,11... | collective-permute-start | bytes 196616 | tf_op jit(solution)/shard_map/ppermute | solution.py:981
  14.3 11.5 %collective-permute-start.1 = (f32[16,8,128]{2,1,0:T(8,128)S(1)}, f32[16,8,128]{2,1,0:T(8,128)S(1)}, u32[]{:S(2)}, u32[]{:S(2)}) collective-permute-start(f32[16,8,128]{2,1,0:T(8,128)S(1)} %get-tuple-element.32), channel_id=1, source_target_pairs={{0,7},{1,2},{2,1},{3,4},{4,3},{5,6},{6,5},{7,0},{8,15},{9,10},{10,... | collective-permute-start | bytes 196616 | tf_op jit(solution)/shard_map/ppermute | solution.py:981
  32.4 14.4 %collective-permute-start.2 = (f32[3,16,128]{2,1,0:T(8,128)S(1)}, f32[3,16,128]{2,1,0:T(8,128)S(1)}, u32[]{:S(2)}, u32[]{:S(2)}) collective-permute-start(f32[3,16,128]{2,1,0:T(8,128)S(1)} %get-tuple-element.34), channel_id=1, source_target_pairs={{0,1},{1,0},{2,3},{3,2},{4,5},{5,4},{6,7},{7,6},{8,9},{9,8},{10,11... | collective-permute-start | bytes 73736 | tf_op jit(solution)/shard_map/ppermute | solution.py:981
  34.3 12.6 %collective-permute-start.3 = (f32[3,16,128]{2,1,0:T(8,128)S(1)}, f32[3,16,128]{2,1,0:T(8,128)S(1)}, u32[]{:S(2)}, u32[]{:S(2)}) collective-permute-start(f32[3,16,128]{2,1,0:T(8,128)S(1)} %get-tuple-element.35), channel_id=1, source_target_pairs={{0,7},{1,2},{2,1},{3,4},{4,3},{5,6},{6,5},{7,0},{8,15},{9,10},{10,... | collective-permute-start | bytes 73736 | tf_op jit(solution)/shard_map/ppermute | solution.py:981
  52.6 4.6 %collective-permute-start.4 = (f32[3,32,256]{2,1,0:T(8,128)S(1)}, f32[3,32,256]{2,1,0:T(8,128)S(1)}, u32[]{:S(2)}, u32[]{:S(2)}) collective-permute-start(f32[3,32,256]{2,1,0:T(8,128)S(1)} %get-tuple-element.38), channel_id=1, source_target_pairs={{0,64},{64,0},{128,192},{192,128},{1,65},{65,1},{129,193},{193,129... | collective-permute-start | bytes 294920 | tf_op jit(solution)/shard_map/ppermute | solution.py:981
  53.4 6.5 %collective-permute-start.5 = (f32[3,32,256]{2,1,0:T(8,128)S(1)}, f32[3,32,256]{2,1,0:T(8,128)S(1)}, u32[]{:S(2)}, u32[]{:S(2)}) collective-permute-start(f32[3,32,256]{2,1,0:T(8,128)S(1)} %get-tuple-element.39), channel_id=1, source_target_pairs={{0,0},{64,128},{128,64},{192,192},{1,1},{65,129},{129,65},{193,193... | collective-permute-start | bytes 294920 | tf_op jit(solution)/shard_map/ppermute | solution.py:981
  60.1 2.6 %collective-permute-start.6 = (f32[3,16,256]{2,1,0:T(8,128)S(1)}, f32[3,16,256]{2,1,0:T(8,128)S(1)}, u32[]{:S(2)}, u32[]{:S(2)}) collective-permute-start(f32[3,16,256]{2,1,0:T(8,128)S(1)} %get-tuple-element.41), channel_id=1, source_target_pairs={{0,8},{8,0},{16,24},{24,16},{32,40},{40,32},{48,56},{56,48},{1,9},... | collective-permute-start | bytes 147464 | tf_op jit(solution)/shard_map/ppermute | solution.py:981
  60.2 5.4 %collective-permute-start.7 = (f32[3,16,256]{2,1,0:T(8,128)S(1)}, f32[3,16,256]{2,1,0:T(8,128)S(1)}, u32[]{:S(2)}, u32[]{:S(2)}) collective-permute-start(f32[3,16,256]{2,1,0:T(8,128)S(1)} %get-tuple-element.42), channel_id=1, source_target_pairs={{0,0},{8,16},{16,8},{24,32},{32,24},{40,48},{48,40},{56,56},{1,1},... | collective-permute-start | bytes 147464 | tf_op jit(solution)/shard_map/ppermute | solution.py:981
  66.1 7.6 %collective-permute-start.8 = (f32[8,128]{1,0:T(8,128)S(1)}, f32[8,128]{1,0:T(8,128)S(1)}, u32[]{:S(2)}, u32[]{:S(2)}) collective-permute-start(f32[8,128]{1,0:T(8,128)S(1)} %get-tuple-element.44), channel_id=1, source_target_pairs={{0,1},{1,0},{2,3},{3,2},{4,5},{5,4},{6,7},{7,6},{8,9},{9,8},{10,11... | collective-permute-start | bytes 12296 | tf_op jit(solution)/shard_map/ppermute | solution.py:981
  68.8 9.6 %collective-permute-start.9 = (f32[8,128]{1,0:T(8,128)S(1)}, f32[8,128]{1,0:T(8,128)S(1)}, u32[]{:S(2)}, u32[]{:S(2)}) collective-permute-start(f32[8,128]{1,0:T(8,128)S(1)} %get-tuple-element.45), channel_id=1, source_target_pairs={{0,7},{1,2},{2,1},{3,4},{4,3},{5,6},{6,5},{7,0},{8,15},{9,10},{10,... | collective-permute-start | bytes 12296 | tf_op jit(solution)/shard_map/ppermute | solution.py:981
